TPU v7x, 256 devices: a whole 4x4x8 slice. The times are simulated.
256 devices in a mesh: group: 8 (over z), sub: 32 (over x, y, core).
Axes of the slice: x: 4, y: 4, z: 8, core: 2. Of those that a mesh axis runs over, the one named last changes fastest.
Arguments:
- right_sides: float32 [6, 512, 32, 128], P(None, ('group', 'sub')), may hold values from -6 to 6
- lower_inv: bfloat16 [6, 512, 128, 128], P(None, ('group', 'sub'))
- upper_inv: bfloat16 [6, 512, 128, 128], P(None, ('group', 'sub'))
- lower_off: bfloat16 [15, 512, 4, 128, 128], P(None, ('group', 'sub')), may hold values from -0.125 to 0.125
- upper_off: bfloat16 [15, 512, 4, 128, 128], P(None, ('group', 'sub')), may hold values from -0.125 to 0.125
- lower_pattern: int32 [15, 512, 4], P(None, ('group', 'sub')), may hold values from 0 to 255, as said below
- upper_pattern: int32 [15, 512, 4], P(None, ('group', 'sub')), may hold values from 0 to 255, as said below
Outputs:
- solution: float32 [6, 512, 32, 128], P(None, ('group', 'sub'))
Inputs may be any that keep to these rules, and one draw needn't show every extreme that they name: `lower_pattern`: entry [p, i, n], for the pair p = k (k - 1) / 2 + l of a level l and a deeper level k, is below 512 // 2^k. `upper_pattern`: entry [p, i, n], for the pair p = k (k - 1) / 2 + l of a level l and a deeper level k, is below 512 // 2^k.
All inputs are finite; a program needn't handle non-finite values.
Results may differ from a plain program's by a relative error of at most 0.017.
Values may be sent and summed in bfloat16 or wider, within the bound.
No kernel may reach another device: no remote copies, remote signals or barrier semaphores. Data moves between devices by JAX's collectives and lax.ppermute only.
A program may use at most 64 MiB of HBM per device.

v0:
```python
import jax
import jax.numpy as jnp
import numpy as np
from jax import lax
from jax.sharding import PartitionSpec as P


def swapped(block, axis, bit):
    count = lax.axis_size(axis)
    route = []
    for low in range(count):
        high = low | 1 << bit
        if high != low and high < count:
            route += [(low, high), (high, low)]
    return lax.ppermute(block, axis, route)


def ordered_join(buffer, partner, high_half):
    return jnp.where(
        high_half == 0, jnp.concatenate([buffer, partner], 0), jnp.concatenate([partner, buffer], 0)
    )


def gather_subcube(block_piece, span_bits, sub_bits):
    buffer = block_piece
    for bit_index in range(min(span_bits, sub_bits)):
        partner = swapped(buffer, "sub", bit_index)
        buffer = ordered_join(buffer, partner, (lax.axis_index("sub") >> bit_index) % 2)
    group_bits = span_bits - sub_bits
    if group_bits > 0:
        for bit_index in range(group_bits):
            partner = swapped(buffer, "group", bit_index)
            buffer = ordered_join(buffer, partner, (lax.axis_index("group") >> bit_index) % 2)
    return buffer


def apply_inverse(residual, inverse):
    return jnp.einsum(
        "jrb,jbc->jrc", residual.astype(jnp.bfloat16), inverse, preferred_element_type=jnp.float32
    )


def on_device(
    right_sides, lower_inv, upper_inv, lower_off, upper_off, lower_pattern, upper_pattern
):
    levels = right_sides.shape[0]
    blocks = right_sides.shape[1]
    sub_bits = lax.axis_size("sub").bit_length() - 1
    all_bits = (lax.axis_size("group") * lax.axis_size("sub")).bit_length() - 1
    device = lax.axis_index("group") * lax.axis_size("sub") + lax.axis_index("sub")
    pending = jnp.zeros(right_sides.shape, jnp.float32)
    forward = [None] * levels
    for deeper in range(levels - 1, -1, -1):
        solved = apply_inverse(right_sides[deeper] - pending[deeper], lower_inv[deeper])
        forward[deeper] = solved
        if deeper > 0:
            nearby = gather_subcube(solved.astype(jnp.bfloat16), all_bits - deeper, sub_bits)
            first_pair = deeper * (deeper - 1) // 2
            picked = jnp.take(nearby, lower_pattern[first_pair : first_pair + deeper], axis=0)
            update = jnp.einsum(
                "sjnrb,sjnbc->sjrc",
                picked,
                lower_off[first_pair : first_pair + deeper],
                preferred_element_type=jnp.float32,
            )
            pending = pending.at[:deeper].add(update)
    backlog = jnp.zeros(right_sides.shape, jnp.float32)
    results = [None] * levels
    for shallow in range(levels):
        solution = apply_inverse(forward[shallow] - backlog[shallow], upper_inv[shallow])
        results[shallow] = solution
        if shallow < levels - 1:
            span_bits = all_bits - shallow - 1
            nearby = gather_subcube(solution.astype(jnp.bfloat16), span_bits, sub_bits)
            local_rank = device % (1 << span_bits)
            pair_list = np.array(
                [deeper * (deeper - 1) // 2 + shallow for deeper in range(shallow + 1, levels)],
                dtype=np.int32,
            )
            offsets = jnp.stack(
                [
                    (local_rank >> all_bits - deeper) * (blocks << all_bits - deeper)
                    for deeper in range(shallow + 1, levels)
                ]
            )
            source_index = upper_pattern[pair_list] + offsets[:, None, None]
            picked = jnp.take(nearby, source_index, axis=0)
            update = jnp.einsum(
                "sjnrb,sjnbc->sjrc",
                picked,
                upper_off[pair_list],
                preferred_element_type=jnp.float32,
            )
            backlog = backlog.at[shallow + 1 :].add(update)
    return jnp.stack(results)


def solution(mesh):
    return jax.shard_map(
        on_device,
        mesh=mesh,
        in_specs=(
            P(None, ("group", "sub"), None, None),
            P(None, ("group", "sub"), None, None),
            P(None, ("group", "sub"), None, None),
            P(None, ("group", "sub"), None, None, None),
            P(None, ("group", "sub"), None, None, None),
            P(None, ("group", "sub"), None),
            P(None, ("group", "sub"), None),
        ),
        out_specs=P(None, ("group", "sub"), None, None),
        check_vma=False,
    )
```

profile of v0, /device:TPU:1, one launch (start us, length us, event | category | flops | bytes accessed | tf_op | source)
XLA Modules:
  0.0 362.8 jit_solution(5002867311483202899)
XLA Ops:
  1.7 3.2 collective-permute-start
  9.9 3.4 collective-permute-done.2
  23.9 3.4 collective-permute-done.5
  27.6 3.7 %collective-permute-done.6 = bf16[16,32,128]{2,1,0:T(8,128)(2,1)S(1)} collective-permute-done((bf16[16,32,128]{2,1,0:T(8,128)(2,1)S(1)}, bf16[16,32,128]{2,1,0:T(8,128)(2,1)S(1)}, u32[]{:S(2)}, u32[]{:S(2)}) %collective-permute-start.6) | collective-permute-done | bytes 131104 | tf_op jit(solution)/shard_map/ppermute | solution.py:15
  34.2 3.9 %collective-permute-start.7 = (bf16[2,32,128]{2,1,0:T(8,128)(2,1)S(1)}, bf16[2,32,128]{2,1,0:T(8,128)(2,1)S(1)}, u32[]{:S(2)}, u32[]{:S(2)}) collective-permute-start(bf16[2,32,128]{2,1,0:T(8,128)(2,1)S(1)} %get-tuple-element.154), channel_id=1, source_target_pairs={{0,1},{1,0},{2,3},{3,2},{4,5},{5,4},{6,7},{7,6},{8,9},{9,8},{10,11... | collective-permute-start | bytes 49160 | tf_op jit(solution)/shard_map/ppermute | solution.py:15
  43.0 3.4 collective-permute-done.9
  46.8 3.5 collective-permute-done.10
  51.7 5.5 %collective-permute-done.11 = bf16[32,32,128]{2,1,0:T(8,128)(2,1)S(1)} collective-permute-done((bf16[32,32,128]{2,1,0:T(8,128)(2,1)S(1)}, bf16[32,32,128]{2,1,0:T(8,128)(2,1)S(1)}, u32[]{:S(2)}, u32[]{:S(2)}) %collective-permute-start.11) | collective-permute-done | bytes 262176 | tf_op jit(solution)/shard_map/ppermute | solution.py:15
  60.1 5.9 %collective-permute-start.12 = (bf16[2,32,128]{2,1,0:T(8,128)(2,1)S(1)}, bf16[2,32,128]{2,1,0:T(8,128)(2,1)S(1)}, u32[]{:S(2)}, u32[]{:S(2)}) collective-permute-start(bf16[2,32,128]{2,1,0:T(8,128)(2,1)S(1)} %get-tuple-element.156), channel_id=1, source_target_pairs={{0,1},{1,0},{2,3},{3,2},{4,5},{5,4},{6,7},{7,6},{8,9},{9,8},{10,11... | collective-permute-start | bytes 49160 | tf_op jit(solution)/shard_map/ppermute | solution.py:15
  70.0 4.3 %collective-permute-done.14 = bf16[8,32,128]{2,1,0:T(8,128)(2,1)S(1)} collective-permute-done((bf16[8,32,128]{2,1,0:T(8,128)(2,1)S(1)}, bf16[8,32,128]{2,1,0:T(8,128)(2,1)S(1)}, u32[]{:S(2)}, u32[]{:S(2)}) %collective-permute-start.14) | collective-permute-done | bytes 65568 | tf_op jit(solution)/shard_map/ppermute | solution.py:15
  74.4 3.8 %collective-permute-done.15 = bf16[16,32,128]{2,1,0:T(8,128)(2,1)S(1)} collective-permute-done((bf16[16,32,128]{2,1,0:T(8,128)(2,1)S(1)}, bf16[16,32,128]{2,1,0:T(8,128)(2,1)S(1)}, u32[]{:S(2)}, u32[]{:S(2)}) %collective-permute-start.15) | collective-permute-done | bytes 131104 | tf_op jit(solution)/shard_map/ppermute | solution.py:15
  79.4 5.6 %collective-permute-done.16 = bf16[32,32,128]{2,1,0:T(8,128)(2,1)S(1)} collective-permute-done((bf16[32,32,128]{2,1,0:T(8,128)(2,1)S(1)}, bf16[32,32,128]{2,1,0:T(8,128)(2,1)S(1)}, u32[]{:S(2)}, u32[]{:S(2)}) %collective-permute-start.16) | collective-permute-done | bytes 262176 | tf_op jit(solution)/shard_map/ppermute | solution.py:15
  86.4 7.1 %collective-permute-done.17 = bf16[64,32,128]{2,1,0:T(8,128)(2,1)S(1)} collective-permute-done((bf16[64,32,128]{2,1,0:T(8,128)(2,1)S(1)}, bf16[64,32,128]{2,1,0:T(8,128)(2,1)S(1)}, u32[]{:S(2)}, u32[]{:S(2)}) %collective-permute-start.17) | collective-permute-done | bytes 524320 | tf_op jit(solution)/shard_map/ppermute | solution.py:15
  96.2 6.3 %collective-permute-start.18 = (bf16[2,32,128]{2,1,0:T(8,128)(2,1)S(1)}, bf16[2,32,128]{2,1,0:T(8,128)(2,1)S(1)}, u32[]{:S(2)}, u32[]{:S(2)}) collective-permute-start(bf16[2,32,128]{2,1,0:T(8,128)(2,1)S(1)} %get-tuple-element.158), channel_id=1, source_target_pairs={{0,1},{1,0},{2,3},{3,2},{4,5},{5,4},{6,7},{7,6},{8,9},{9,8},{10,11... | collective-permute-start | bytes 49160 | tf_op jit(solution)/shard_map/ppermute | solution.py:15
  111.0 3.8 %collective-permute-done.21 = bf16[16,32,128]{2,1,0:T(8,128)(2,1)S(1)} collective-permute-done((bf16[16,32,128]{2,1,0:T(8,128)(2,1)S(1)}, bf16[16,32,128]{2,1,0:T(8,128)(2,1)S(1)}, u32[]{:S(2)}, u32[]{:S(2)}) %collective-permute-start.21) | collective-permute-done | bytes 131104 | tf_op jit(solution)/shard_map/ppermute | solution.py:15
  116.9 5.8 %collective-permute-done.22 = bf16[32,32,128]{2,1,0:T(8,128)(2,1)S(1)} collective-permute-done((bf16[32,32,128]{2,1,0:T(8,128)(2,1)S(1)}, bf16[32,32,128]{2,1,0:T(8,128)(2,1)S(1)}, u32[]{:S(2)}, u32[]{:S(2)}) %collective-permute-start.22) | collective-permute-done | bytes 262176 | tf_op jit(solution)/shard_map/ppermute | solution.py:15
  124.1 8.2 %collective-permute-done.23 = bf16[64,32,128]{2,1,0:T(8,128)(2,1)S(1)} collective-permute-done((bf16[64,32,128]{2,1,0:T(8,128)(2,1)S(1)}, bf16[64,32,128]{2,1,0:T(8,128)(2,1)S(1)}, u32[]{:S(2)}, u32[]{:S(2)}) %collective-permute-start.23) | collective-permute-done | bytes 524320 | tf_op jit(solution)/shard_map/ppermute | solution.py:15
  132.4 3.2 collective-permute-start.24
  136.1 43.4 %collective-permute-done.24 = bf16[128,32,128]{2,1,0:T(8,128)(2,1)} collective-permute-done((bf16[128,32,128]{2,1,0:T(8,128)(2,1)S(1)}, bf16[128,32,128]{2,1,0:T(8,128)(2,1)}, u32[]{:S(2)}, u32[]{:S(2)}) %collective-permute-start.24) | collective-permute-done | bytes 1048608 | tf_op jit(solution)/shard_map/ppermute | solution.py:15
  196.3 3.8 %collective-permute-done.28 = bf16[16,32,128]{2,1,0:T(8,128)(2,1)S(1)} collective-permute-done((bf16[16,32,128]{2,1,0:T(8,128)(2,1)S(1)}, bf16[16,32,128]{2,1,0:T(8,128)(2,1)S(1)}, u32[]{:S(2)}, u32[]{:S(2)}) %collective-permute-start.28) | collective-permute-done | bytes 131104 | tf_op jit(solution)/shard_map/ppermute | solution.py:15
  200.2 6.7 %collective-permute-done.29 = bf16[32,32,128]{2,1,0:T(8,128)(2,1)S(1)} collective-permute-done((bf16[32,32,128]{2,1,0:T(8,128)(2,1)S(1)}, bf16[32,32,128]{2,1,0:T(8,128)(2,1)S(1)}, u32[]{:S(2)}, u32[]{:S(2)}) %collective-permute-start.29) | collective-permute-done | bytes 262176 | tf_op jit(solution)/shard_map/ppermute | solution.py:15
  207.4 7.7 %collective-permute-done.30 = bf16[64,32,128]{2,1,0:T(8,128)(2,1)S(1)} collective-permute-done((bf16[64,32,128]{2,1,0:T(8,128)(2,1)S(1)}, bf16[64,32,128]{2,1,0:T(8,128)(2,1)S(1)}, u32[]{:S(2)}, u32[]{:S(2)}) %collective-permute-start.30) | collective-permute-done | bytes 524320 | tf_op jit(solution)/shard_map/ppermute | solution.py:15
  221.6 37.5 %collective-permute-done.31 = bf16[128,32,128]{2,1,0:T(8,128)(2,1)S(1)} collective-permute-done((bf16[128,32,128]{2,1,0:T(8,128)(2,1)S(1)}, bf16[128,32,128]{2,1,0:T(8,128)(2,1)S(1)}, u32[]{:S(2)}, u32[]{:S(2)}) %collective-permute-start.31) | collective-permute-done | bytes 1048608 | tf_op jit(solution)/shard_map/ppermute | solution.py:15
  264.9 5.3 %collective-permute-start.32 = (bf16[2,32,128]{2,1,0:T(8,128)(2,1)S(1)}, bf16[2,32,128]{2,1,0:T(8,128)(2,1)S(1)}, u32[]{:S(2)}, u32[]{:S(2)}) collective-permute-start(bf16[2,32,128]{2,1,0:T(8,128)(2,1)S(1)} %get-tuple-element.163), channel_id=1, source_target_pairs={{0,1},{1,0},{2,3},{3,2},{4,5},{5,4},{6,7},{7,6},{8,9},{9,8},{10,11... | collective-permute-start | bytes 49160 | tf_op jit(solution)/shard_map/ppermute | solution.py:15
  278.9 3.8 %collective-permute-done.35 = bf16[16,32,128]{2,1,0:T(8,128)(2,1)S(1)} collective-permute-done((bf16[16,32,128]{2,1,0:T(8,128)(2,1)S(1)}, bf16[16,32,128]{2,1,0:T(8,128)(2,1)S(1)}, u32[]{:S(2)}, u32[]{:S(2)}) %collective-permute-start.35) | collective-permute-done | bytes 131104 | tf_op jit(solution)/shard_map/ppermute | solution.py:15
  282.7 3.0 collective-permute-start.36
  291.8 8.8 %collective-permute-done.37 = bf16[64,32,128]{2,1,0:T(8,128)(2,1)S(1)} collective-permute-done((bf16[64,32,128]{2,1,0:T(8,128)(2,1)S(1)}, bf16[64,32,128]{2,1,0:T(8,128)(2,1)S(1)}, u32[]{:S(2)}, u32[]{:S(2)}) %collective-permute-start.37) | collective-permute-done | bytes 524320 | tf_op jit(solution)/shard_map/ppermute | solution.py:15
  303.3 4.9 %collective-permute-start.38 = (bf16[2,32,128]{2,1,0:T(8,128)(2,1)S(1)}, bf16[2,32,128]{2,1,0:T(8,128)(2,1)S(1)}, u32[]{:S(2)}, u32[]{:S(2)}) collective-permute-start(bf16[2,32,128]{2,1,0:T(8,128)(2,1)S(1)} %get-tuple-element.165), channel_id=1, source_target_pairs={{0,1},{1,0},{2,3},{3,2},{4,5},{5,4},{6,7},{7,6},{8,9},{9,8},{10,11... | collective-permute-start | bytes 49160 | tf_op jit(solution)/shard_map/ppermute | solution.py:15
  330.4 3.7 %collective-permute-start.43 = (bf16[2,32,128]{2,1,0:T(8,128)(2,1)S(1)}, bf16[2,32,128]{2,1,0:T(8,128)(2,1)S(1)}, u32[]{:S(2)}, u32[]{:S(2)}) collective-permute-start(bf16[2,32,128]{2,1,0:T(8,128)(2,1)S(1)} %get-tuple-element.167), channel_id=1, source_target_pairs={{0,1},{1,0},{2,3},{3,2},{4,5},{5,4},{6,7},{7,6},{8,9},{9,8},{10,11... | collective-permute-start | bytes 49160 | tf_op jit(solution)/shard_map/ppermute | solution.py:15
  337.8 3.0 collective-permute-start.45
  348.8 3.1 collective-permute-start.47
  355.5 3.0 collective-permute-start.49
  (245 shorter events, 140.1 us)
Async XLA Ops:
  1.7 4.1 %collective-permute-start = (bf16[2,32,128]{2,1,0:T(8,128)(2,1)S(1)}, bf16[2,32,128]{2,1,0:T(8,128)(2,1)S(1)}, u32[]{:S(2)}, u32[]{:S(2)}) collective-permute-start(bf16[2,32,128]{2,1,0:T(8,128)(2,1)S(1)} %get-tuple-element.150), channel_id=1, source_target_pairs={{0,1},{1,0},{2,3},{3,2},{4,5},{5,4},{6,7},{7,6},{8,9},{9,8},{10,11... | collective-permute-start | bytes 49160 | tf_op jit(solution)/shard_map/ppermute | solution.py:15
  8.6 4.7 %collective-permute-start.2 = (bf16[8,32,128]{2,1,0:T(8,128)(2,1)S(1)}, bf16[8,32,128]{2,1,0:T(8,128)(2,1)S(1)}, u32[]{:S(2)}, u32[]{:S(2)}) collective-permute-start(bf16[8,32,128]{2,1,0:T(8,128)(2,1)S(1)} %maximum_select_fusion.30), channel_id=1, source_target_pairs={{0,4},{4,0},{1,5},{5,1},{2,6},{6,2},{3,7},{7,3},{8,12},{12,8},{9,1... | collective-permute-start | bytes 196616 | tf_op jit(solution)/shard_map/ppermute | solution.py:15
  22.7 4.7 %collective-permute-start.5 = (bf16[8,32,128]{2,1,0:T(8,128)(2,1)S(1)}, bf16[8,32,128]{2,1,0:T(8,128)(2,1)S(1)}, u32[]{:S(2)}, u32[]{:S(2)}) collective-permute-start(bf16[8,32,128]{2,1,0:T(8,128)(2,1)S(1)} %maximum_select_fusion.31), channel_id=1, source_target_pairs={{0,4},{4,0},{1,5},{5,1},{2,6},{6,2},{3,7},{7,3},{8,12},{12,8},{9,1... | collective-permute-start | bytes 196616 | tf_op jit(solution)/shard_map/ppermute | solution.py:15
  34.2 4.7 %collective-permute-start.7 = (bf16[2,32,128]{2,1,0:T(8,128)(2,1)S(1)}, bf16[2,32,128]{2,1,0:T(8,128)(2,1)S(1)}, u32[]{:S(2)}, u32[]{:S(2)}) collective-permute-start(bf16[2,32,128]{2,1,0:T(8,128)(2,1)S(1)} %get-tuple-element.154), channel_id=1, source_target_pairs={{0,1},{1,0},{2,3},{3,2},{4,5},{5,4},{6,7},{7,6},{8,9},{9,8},{10,11... | collective-permute-start | bytes 49160 | tf_op jit(solution)/shard_map/ppermute | solution.py:15
  41.7 4.7 %collective-permute-start.9 = (bf16[8,32,128]{2,1,0:T(8,128)(2,1)S(1)}, bf16[8,32,128]{2,1,0:T(8,128)(2,1)S(1)}, u32[]{:S(2)}, u32[]{:S(2)}) collective-permute-start(bf16[8,32,128]{2,1,0:T(8,128)(2,1)S(1)} %maximum_select_fusion.32), channel_id=1, source_target_pairs={{0,4},{4,0},{1,5},{5,1},{2,6},{6,2},{3,7},{7,3},{8,12},{12,8},{9,1... | collective-permute-start | bytes 196616 | tf_op jit(solution)/shard_map/ppermute | solution.py:15
  50.4 6.8 %collective-permute-start.11 = (bf16[32,32,128]{2,1,0:T(8,128)(2,1)S(1)}, bf16[32,32,128]{2,1,0:T(8,128)(2,1)S(1)}, u32[]{:S(2)}, u32[]{:S(2)}) collective-permute-start(bf16[32,32,128]{2,1,0:T(8,128)(2,1)S(1)} %maximum_select_fusion.13), channel_id=1, source_target_pairs={{0,16},{16,0},{1,17},{17,1},{2,18},{18,2},{3,19},{19,3},{4,20},{20... | collective-permute-start | bytes 786440 | tf_op jit(solution)/shard_map/ppermute | solution.py:15
  60.1 6.7 %collective-permute-start.12 = (bf16[2,32,128]{2,1,0:T(8,128)(2,1)S(1)}, bf16[2,32,128]{2,1,0:T(8,128)(2,1)S(1)}, u32[]{:S(2)}, u32[]{:S(2)}) collective-permute-start(bf16[2,32,128]{2,1,0:T(8,128)(2,1)S(1)} %get-tuple-element.156), channel_id=1, source_target_pairs={{0,1},{1,0},{2,3},{3,2},{4,5},{5,4},{6,7},{7,6},{8,9},{9,8},{10,11... | collective-permute-start | bytes 49160 | tf_op jit(solution)/shard_map/ppermute | solution.py:15
  69.6 4.7 %collective-permute-start.14 = (bf16[8,32,128]{2,1,0:T(8,128)(2,1)S(1)}, bf16[8,32,128]{2,1,0:T(8,128)(2,1)S(1)}, u32[]{:S(2)}, u32[]{:S(2)}) collective-permute-start(bf16[8,32,128]{2,1,0:T(8,128)(2,1)S(1)} %maximum_select_fusion.33), channel_id=1, source_target_pairs={{0,4},{4,0},{1,5},{5,1},{2,6},{6,2},{3,7},{7,3},{8,12},{12,8},{9,1... | collective-permute-start | bytes 196616 | tf_op jit(solution)/shard_map/ppermute | solution.py:15
  78.2 6.8 %collective-permute-start.16 = (bf16[32,32,128]{2,1,0:T(8,128)(2,1)S(1)}, bf16[32,32,128]{2,1,0:T(8,128)(2,1)S(1)}, u32[]{:S(2)}, u32[]{:S(2)}) collective-permute-start(bf16[32,32,128]{2,1,0:T(8,128)(2,1)S(1)} %maximum_select_fusion.14), channel_id=1, source_target_pairs={{0,16},{16,0},{1,17},{17,1},{2,18},{18,2},{3,19},{19,3},{4,20},{20... | collective-permute-start | bytes 786440 | tf_op jit(solution)/shard_map/ppermute | solution.py:15
  85.1 8.3 %collective-permute-start.17 = (bf16[64,32,128]{2,1,0:T(8,128)(2,1)S(1)}, bf16[64,32,128]{2,1,0:T(8,128)(2,1)S(1)}, u32[]{:S(2)}, u32[]{:S(2)}) collective-permute-start(bf16[64,32,128]{2,1,0:T(8,128)(2,1)S(1)} %maximum_select_fusion.7), channel_id=1, source_target_pairs={{0,32},{32,0},{64,96},{96,64},{128,160},{160,128},{192,224},{224,1... | collective-permute-start | bytes 1572872 | tf_op jit(solution)/shard_map/ppermute | solution.py:15
  96.2 7.2 %collective-permute-start.18 = (bf16[2,32,128]{2,1,0:T(8,128)(2,1)S(1)}, bf16[2,32,128]{2,1,0:T(8,128)(2,1)S(1)}, u32[]{:S(2)}, u32[]{:S(2)}) collective-permute-start(bf16[2,32,128]{2,1,0:T(8,128)(2,1)S(1)} %get-tuple-element.158), channel_id=1, source_target_pairs={{0,1},{1,0},{2,3},{3,2},{4,5},{5,4},{6,7},{7,6},{8,9},{9,8},{10,11... | collective-permute-start | bytes 49160 | tf_op jit(solution)/shard_map/ppermute | solution.py:15
  106.2 4.7 %collective-permute-start.20 = (bf16[8,32,128]{2,1,0:T(8,128)(2,1)S(1)}, bf16[8,32,128]{2,1,0:T(8,128)(2,1)S(1)}, u32[]{:S(2)}, u32[]{:S(2)}) collective-permute-start(bf16[8,32,128]{2,1,0:T(8,128)(2,1)S(1)} %maximum_select_fusion.34), channel_id=1, source_target_pairs={{0,4},{4,0},{1,5},{5,1},{2,6},{6,2},{3,7},{7,3},{8,12},{12,8},{9,1... | collective-permute-start | bytes 196616 | tf_op jit(solution)/shard_map/ppermute | solution.py:15
  114.9 7.8 %collective-permute-start.22 = (bf16[32,32,128]{2,1,0:T(8,128)(2,1)S(1)}, bf16[32,32,128]{2,1,0:T(8,128)(2,1)S(1)}, u32[]{:S(2)}, u32[]{:S(2)}) collective-permute-start(bf16[32,32,128]{2,1,0:T(8,128)(2,1)S(1)} %maximum_select_fusion.15), channel_id=1, source_target_pairs={{0,16},{16,0},{1,17},{17,1},{2,18},{18,2},{3,19},{19,3},{4,20},{20... | collective-permute-start | bytes 786440 | tf_op jit(solution)/shard_map/ppermute | solution.py:15
  122.8 9.5 %collective-permute-start.23 = (bf16[64,32,128]{2,1,0:T(8,128)(2,1)S(1)}, bf16[64,32,128]{2,1,0:T(8,128)(2,1)S(1)}, u32[]{:S(2)}, u32[]{:S(2)}) collective-permute-start(bf16[64,32,128]{2,1,0:T(8,128)(2,1)S(1)} %maximum_select_fusion.8), channel_id=1, source_target_pairs={{0,32},{32,0},{64,96},{96,64},{128,160},{160,128},{192,224},{224,1... | collective-permute-start | bytes 1572872 | tf_op jit(solution)/shard_map/ppermute | solution.py:15
  132.4 47.0 %collective-permute-start.24 = (bf16[128,32,128]{2,1,0:T(8,128)(2,1)S(1)}, bf16[128,32,128]{2,1,0:T(8,128)(2,1)}, u32[]{:S(2)}, u32[]{:S(2)}) collective-permute-start(bf16[128,32,128]{2,1,0:T(8,128)(2,1)S(1)} %maximum_select_fusion.3), channel_id=1, source_target_pairs={{0,64},{64,0},{32,96},{96,32},{128,192},{192,128},{160,224},{224,1... | collective-permute-start | bytes 3145736 | tf_op jit(solution)/shard_map/ppermute | solution.py:15
  191.4 4.7 %collective-permute-start.27 = (bf16[8,32,128]{2,1,0:T(8,128)(2,1)S(1)}, bf16[8,32,128]{2,1,0:T(8,128)(2,1)S(1)}, u32[]{:S(2)}, u32[]{:S(2)}) collective-permute-start(bf16[8,32,128]{2,1,0:T(8,128)(2,1)S(1)} %maximum_select_fusion.35), channel_id=1, source_target_pairs={{0,4},{4,0},{1,5},{5,1},{2,6},{6,2},{3,7},{7,3},{8,12},{12,8},{9,1... | collective-permute-start | bytes 196616 | tf_op jit(solution)/shard_map/ppermute | solution.py:15
  200.1 6.8 %collective-permute-start.29 = (bf16[32,32,128]{2,1,0:T(8,128)(2,1)S(1)}, bf16[32,32,128]{2,1,0:T(8,128)(2,1)S(1)}, u32[]{:S(2)}, u32[]{:S(2)}) collective-permute-start(bf16[32,32,128]{2,1,0:T(8,128)(2,1)S(1)} %maximum_select_fusion.16), channel_id=1, source_target_pairs={{0,16},{16,0},{1,17},{17,1},{2,18},{18,2},{3,19},{19,3},{4,20},{20... | collective-permute-start | bytes 786440 | tf_op jit(solution)/shard_map/ppermute | solution.py:15
  207.0 8.1 %collective-permute-start.30 = (bf16[64,32,128]{2,1,0:T(8,128)(2,1)S(1)}, bf16[64,32,128]{2,1,0:T(8,128)(2,1)S(1)}, u32[]{:S(2)}, u32[]{:S(2)}) collective-permute-start(bf16[64,32,128]{2,1,0:T(8,128)(2,1)S(1)} %maximum_select_fusion.9), channel_id=1, source_target_pairs={{0,32},{32,0},{64,96},{96,64},{128,160},{160,128},{192,224},{224,1... | collective-permute-start | bytes 1572872 | tf_op jit(solution)/shard_map/ppermute | solution.py:15
  215.3 43.8 %collective-permute-start.31 = (bf16[128,32,128]{2,1,0:T(8,128)(2,1)S(1)}, bf16[128,32,128]{2,1,0:T(8,128)(2,1)S(1)}, u32[]{:S(2)}, u32[]{:S(2)}) collective-permute-start(bf16[128,32,128]{2,1,0:T(8,128)(2,1)S(1)} %maximum_select_fusion.4), channel_id=1, source_target_pairs={{0,64},{64,0},{32,96},{96,32},{128,192},{192,128},{160,224},{224,1... | collective-permute-start | bytes 3145736 | tf_op jit(solution)/shard_map/ppermute | solution.py:15
  264.9 6.1 %collective-permute-start.32 = (bf16[2,32,128]{2,1,0:T(8,128)(2,1)S(1)}, bf16[2,32,128]{2,1,0:T(8,128)(2,1)S(1)}, u32[]{:S(2)}, u32[]{:S(2)}) collective-permute-start(bf16[2,32,128]{2,1,0:T(8,128)(2,1)S(1)} %get-tuple-element.163), channel_id=1, source_target_pairs={{0,1},{1,0},{2,3},{3,2},{4,5},{5,4},{6,7},{7,6},{8,9},{9,8},{10,11... | collective-permute-start | bytes 49160 | tf_op jit(solution)/shard_map/ppermute | solution.py:15
  273.8 4.7 %collective-permute-start.34 = (bf16[8,32,128]{2,1,0:T(8,128)(2,1)S(1)}, bf16[8,32,128]{2,1,0:T(8,128)(2,1)S(1)}, u32[]{:S(2)}, u32[]{:S(2)}) collective-permute-start(bf16[8,32,128]{2,1,0:T(8,128)(2,1)S(1)} %maximum_select_fusion.36), channel_id=1, source_target_pairs={{0,4},{4,0},{1,5},{5,1},{2,6},{6,2},{3,7},{7,3},{8,12},{12,8},{9,1... | collective-permute-start | bytes 196616 | tf_op jit(solution)/shard_map/ppermute | solution.py:15
  278.5 4.1 %collective-permute-start.35 = (bf16[16,32,128]{2,1,0:T(8,128)(2,1)S(1)}, bf16[16,32,128]{2,1,0:T(8,128)(2,1)S(1)}, u32[]{:S(2)}, u32[]{:S(2)}) collective-permute-start(bf16[16,32,128]{2,1,0:T(8,128)(2,1)S(1)} %maximum_select_fusion.26), channel_id=1, source_target_pairs={{0,8},{8,0},{1,9},{9,1},{2,10},{10,2},{3,11},{11,3},{4,12},{12,4},... | collective-permute-start | bytes 393224 | tf_op jit(solution)/shard_map/ppermute | solution.py:15
  282.7 8.2 %collective-permute-start.36 = (bf16[32,32,128]{2,1,0:T(8,128)(2,1)S(1)}, bf16[32,32,128]{2,1,0:T(8,128)(2,1)S(1)}, u32[]{:S(2)}, u32[]{:S(2)}) collective-permute-start(bf16[32,32,128]{2,1,0:T(8,128)(2,1)S(1)} %maximum_select_fusion.17), channel_id=1, source_target_pairs={{0,16},{16,0},{1,17},{17,1},{2,18},{18,2},{3,19},{19,3},{4,20},{20... | collective-permute-start | bytes 786440 | tf_op jit(solution)/shard_map/ppermute | solution.py:15
  291.0 9.6 %collective-permute-start.37 = (bf16[64,32,128]{2,1,0:T(8,128)(2,1)S(1)}, bf16[64,32,128]{2,1,0:T(8,128)(2,1)S(1)}, u32[]{:S(2)}, u32[]{:S(2)}) collective-permute-start(bf16[64,32,128]{2,1,0:T(8,128)(2,1)S(1)} %maximum_select_fusion.10), channel_id=1, source_target_pairs={{0,32},{32,0},{64,96},{96,64},{128,160},{160,128},{192,224},{224,1... | collective-permute-start | bytes 1572872 | tf_op jit(solution)/shard_map/ppermute | solution.py:15
  303.3 5.7 %collective-permute-start.38 = (bf16[2,32,128]{2,1,0:T(8,128)(2,1)S(1)}, bf16[2,32,128]{2,1,0:T(8,128)(2,1)S(1)}, u32[]{:S(2)}, u32[]{:S(2)}) collective-permute-start(bf16[2,32,128]{2,1,0:T(8,128)(2,1)S(1)} %get-tuple-element.165), channel_id=1, source_target_pairs={{0,1},{1,0},{2,3},{3,2},{4,5},{5,4},{6,7},{7,6},{8,9},{9,8},{10,11... | collective-permute-start | bytes 49160 | tf_op jit(solution)/shard_map/ppermute | solution.py:15
  311.8 4.7 %collective-permute-start.40 = (bf16[8,32,128]{2,1,0:T(8,128)(2,1)S(1)}, bf16[8,32,128]{2,1,0:T(8,128)(2,1)S(1)}, u32[]{:S(2)}, u32[]{:S(2)}) collective-permute-start(bf16[8,32,128]{2,1,0:T(8,128)(2,1)S(1)} %maximum_select_fusion.37), channel_id=1, source_target_pairs={{0,4},{4,0},{1,5},{5,1},{2,6},{6,2},{3,7},{7,3},{8,12},{12,8},{9,1... | collective-permute-start | bytes 196616 | tf_op jit(solution)/shard_map/ppermute | solution.py:15
  320.4 8.2 %collective-permute-start.42 = (bf16[32,32,128]{2,1,0:T(8,128)(2,1)S(1)}, bf16[32,32,128]{2,1,0:T(8,128)(2,1)S(1)}, u32[]{:S(2)}, u32[]{:S(2)}) collective-permute-start(bf16[32,32,128]{2,1,0:T(8,128)(2,1)S(1)} %maximum_select_fusion.18), channel_id=1, source_target_pairs={{0,16},{16,0},{1,17},{17,1},{2,18},{18,2},{3,19},{19,3},{4,20},{20... | collective-permute-start | bytes 786440 | tf_op jit(solution)/shard_map/ppermute | solution.py:15
  330.4 4.6 %collective-permute-start.43 = (bf16[2,32,128]{2,1,0:T(8,128)(2,1)S(1)}, bf16[2,32,128]{2,1,0:T(8,128)(2,1)S(1)}, u32[]{:S(2)}, u32[]{:S(2)}) collective-permute-start(bf16[2,32,128]{2,1,0:T(8,128)(2,1)S(1)} %get-tuple-element.167), channel_id=1, source_target_pairs={{0,1},{1,0},{2,3},{3,2},{4,5},{5,4},{6,7},{7,6},{8,9},{9,8},{10,11... | collective-permute-start | bytes 49160 | tf_op jit(solution)/shard_map/ppermute | solution.py:15
  337.8 4.7 %collective-permute-start.45 = (bf16[8,32,128]{2,1,0:T(8,128)(2,1)S(1)}, bf16[8,32,128]{2,1,0:T(8,128)(2,1)S(1)}, u32[]{:S(2)}, u32[]{:S(2)}) collective-permute-start(bf16[8,32,128]{2,1,0:T(8,128)(2,1)S(1)} %maximum_select_fusion.38), channel_id=1, source_target_pairs={{0,4},{4,0},{1,5},{5,1},{2,6},{6,2},{3,7},{7,3},{8,12},{12,8},{9,1... | collective-permute-start | bytes 196616 | tf_op jit(solution)/shard_map/ppermute | solution.py:15
  342.5 4.7 %collective-permute-start.46 = (bf16[16,32,128]{2,1,0:T(8,128)(2,1)S(1)}, bf16[16,32,128]{2,1,0:T(8,128)(2,1)S(1)}, u32[]{:S(2)}, u32[]{:S(2)}) collective-permute-start(bf16[16,32,128]{2,1,0:T(8,128)(2,1)S(1)} %maximum_select_fusion.28), channel_id=1, source_target_pairs={{0,8},{8,0},{1,9},{9,1},{2,10},{10,2},{3,11},{11,3},{4,12},{12,4},... | collective-permute-start | bytes 393224 | tf_op jit(solution)/shard_map/ppermute | solution.py:15
  348.8 3.9 %collective-permute-start.47 = (bf16[2,32,128]{2,1,0:T(8,128)(2,1)S(1)}, bf16[2,32,128]{2,1,0:T(8,128)(2,1)S(1)}, u32[]{:S(2)}, u32[]{:S(2)}) collective-permute-start(bf16[2,32,128]{2,1,0:T(8,128)(2,1)S(1)} %get-tuple-element.169), channel_id=1, source_target_pairs={{0,1},{1,0},{2,3},{3,2},{4,5},{5,4},{6,7},{7,6},{8,9},{9,8},{10,11... | collective-permute-start | bytes 49160 | tf_op jit(solution)/shard_map/ppermute | solution.py:15
  355.5 4.7 %collective-permute-start.49 = (bf16[8,32,128]{2,1,0:T(8,128)(2,1)S(1)}, bf16[8,32,128]{2,1,0:T(8,128)(2,1)S(1)}, u32[]{:S(2)}, u32[]{:S(2)}) collective-permute-start(bf16[8,32,128]{2,1,0:T(8,128)(2,1)S(1)} %maximum_select_fusion.39), channel_id=1, source_target_pairs={{0,4},{4,0},{1,5},{5,1},{2,6},{6,2},{3,7},{7,3},{8,12},{12,8},{9,1... | collective-permute-start | bytes 196616 | tf_op jit(solution)/shard_map/ppermute | solution.py:15
  (33 other events, 353.8 us)
where the time goes:
time: 366 us; the launch traced here: 363 us
  waiting for transfers between devices  217 us (59%)
  starting transfers between devices  92.6 us (25%)
  local copies, waits for them, and re-layouts  23.9 us (7%)
  matrix products  21.3 us (6%)
  other arithmetic  6.8 us (2%)
    ppermute x50, waiting for transfers between devices, swapped(): return lax.ppermute(block, axis, route)  217 us
    ppermute x50, starting transfers between devices, swapped(): return lax.ppermute(block, axis, route)  92.6 us
    dot_general x11, matrix products, apply_inverse(): jnp.einsum('jrb,jbc->jrc', residual.astype(jnp.bfloat16), inverse, prefer...  12.9 us
    gather x4, local copies, waits for them, and re-layouts, on_device(): upper_off[pair_list]  11.4 us
  transfers between devices with their start and end apart: 50, of which 48 were waited for; matrix products, arithmetic and copies ran while one was open for 5% of the time, Pallas kernels for 0%

commit v1 on v0

v1 whole, which is shorter than its diff:
```python
import functools

import jax
import jax.numpy as jnp
from jax import lax
from jax.experimental import pallas as pl
from jax.experimental.pallas import tpu as pltpu
from jax.sharding import PartitionSpec as P

SUB_BITS = 5
PLANE = 64
VMEM = pl.BlockSpec(memory_space=pltpu.VMEM)
SMEM = pl.BlockSpec(memory_space=pltpu.SMEM)
PARAMS = pltpu.CompilerParams(vmem_limit_bytes=20 * 2**20)


def pair(deeper, shallow):
    return deeper * (deeper - 1) // 2 + shallow


def span(masks):
    groups, seen = [], set()
    for first in range(1 << SUB_BITS):
        if first not in seen:
            group = [first]
            for mask in masks:
                group = group + [member ^ mask for member in group]
            seen.update(group)
            groups.append(sorted(group))
    return groups


def swapped(block, axis, mask):
    return lax.ppermute(block, axis, [(i, i ^ mask) for i in range(lax.axis_size(axis))])


def spread(block, masks):
    ways = 1 << len(masks)
    copies = jnp.broadcast_to(block[None], (ways,) + block.shape).reshape((-1,) + block.shape[1:])
    return lax.all_to_all(copies, "sub", 0, 0, tiled=True, axis_index_groups=span(masks))


def collected(block, masks):
    own = spread(block, masks)
    return own, swapped(own, "sub", 1)


def place(local, core):
    index = (local >> 2 << 1) | (local & 1)
    other = (local >> 1 & 1) ^ core
    return index | other << 8


def read(kind, refs, code, slot):
    index = code & 255
    if kind == "one":
        return refs[0][index]
    if kind == "planes":
        return refs[0][(code >> 9) * 8 + slot]
    near = jnp.where((code >> 8 & 1) == 0, refs[0][index], refs[1][index])
    if kind == "halves":
        return near
    return jnp.where(code >> 9 == 0, near, refs[2][slot])


def update_kernel(plan, first, level, inverses, outs, *refs):
    refs = list(refs)
    base = refs.pop(0)
    codes, off = (refs.pop(0), refs.pop(0)) if plan else (None, None)
    near = []
    for kind, _ in plan:
        count = {"one": 1, "planes": 1, "halves": 2, "far": 3}[kind]
        near.append([refs.pop(0) for _ in range(count)])
    inverse = [refs.pop(0) for _ in range(inverses)]
    for j in range(2):
        total = base[first, j] if first is not None else base[j]
        for (kind, p), buffers in zip(plan, near):
            picked = [read(kind, buffers, codes[p, j * 4 + n], j * 4 + n) for n in range(4)]
            total = total - jnp.dot(
                jnp.concatenate(picked, 1),
                off[p, j].reshape(512, 128),
                preferred_element_type=jnp.float32,
            )
        at = 0
        if not inverses:
            refs[at][j] = total
            at += 1
        for matrix in inverse:
            total = jnp.dot(
                total.astype(jnp.bfloat16), matrix[level, j], preferred_element_type=jnp.float32
            )
            refs[at][j] = total
            at += 1
        if outs > at:
            refs[at][j] = total.astype(jnp.bfloat16)


def update(base, first, plan, near, codes, off, level=0, inverse=(), low=False):
    block = (2,) + base.shape[-2:]
    shapes = [jax.ShapeDtypeStruct(block, jnp.float32)] * max(1, len(inverse))
    shapes += [jax.ShapeDtypeStruct(block, jnp.bfloat16)] * low
    arguments = [base] + ([codes, off] if plan else [])
    for buffers in near:
        arguments += list(buffers)
    arguments += list(inverse)
    specs = [SMEM if argument is codes and plan else VMEM for argument in arguments]
    products = 2 * (4 * len(plan) + len(inverse))
    return pl.pallas_call(
        functools.partial(update_kernel, tuple(plan), first, level, len(inverse), len(shapes)),
        out_shape=shapes,
        in_specs=specs,
        out_specs=[VMEM] * len(shapes),
        compiler_params=PARAMS,
        cost_estimate=pl.CostEstimate(
            flops=products * 2 * 32 * 128 * 128, bytes_accessed=products * 32768, transcendentals=0
        ),
    )(*arguments)


def pick_kernel(kind, codes, *refs):
    out = refs[-1]
    for slot in range(out.shape[0]):
        out[slot] = read(kind, refs[:-1], codes[slot // 8, slot % 8], slot)


def pick(codes, buffers):
    count = codes.shape[0] * 8
    block = buffers[0].shape[1:]
    return pl.pallas_call(
        functools.partial(pick_kernel, "halves"),
        out_shape=jax.ShapeDtypeStruct((count,) + block, jnp.bfloat16),
        in_specs=[SMEM] + [VMEM] * len(buffers),
        out_specs=VMEM,
        compiler_params=PARAMS,
        cost_estimate=pl.CostEstimate(flops=0, bytes_accessed=count * 16384, transcendentals=0),
    )(codes, *buffers)


def on_device(
    right_sides, lower_inv, upper_inv, lower_off, upper_off, lower_pattern, upper_pattern
):
    sub, group = lax.axis_index("sub"), lax.axis_index("group")
    core = sub & 1
    half = [[0, 1, 2, 3], [4, 5, 6, 7]]

    lower_pattern, upper_pattern = (x.reshape(-1, 8) for x in (lower_pattern, upper_pattern))
    asked = jnp.stack([lower_pattern[:3], upper_pattern[:3]])
    beside = swapped(asked, "group", 1)
    both = jnp.stack([asked[:, 0], beside[:, 0]])
    every = jnp.concatenate([both, swapped(both, "group", 2)])
    every = every[jnp.arange(4) ^ (group & 3)]
    beside = place(beside % PLANE, core)
    every = place(every % PLANE, core)

    low_code, up_code = [], []
    for deeper in range(1, 6):
        for shallow in range(deeper):
            value, wanted = lower_pattern[pair(deeper, shallow)], upper_pattern[pair(deeper, shallow)]
            if deeper == 5:
                low_code.append(value)
            else:
                plane = value // PLANE
                plane = plane ^ (group & 1) if deeper == 2 else plane
                low_code.append(place(value % PLANE, core) | plane << 9)
            if shallow == 4:
                up_code.append(wanted)
            else:
                plane = wanted // PLANE
                plane = plane ^ (group & 1) if deeper == 2 else plane
                local = wanted % PLANE
                if deeper == 4 and shallow < 3:
                    local = local + (sub >> 4) * 32
                if deeper == 5:
                    local = local + ((sub >> 3) & (3 if shallow < 3 else 1)) * 16
                up_code.append(place(local, core) | plane << 9)
    low_code, up_code = jnp.stack(low_code), jnp.stack(up_code)

    low = functools.partial(update, codes=low_code, off=lower_off)
    up = functools.partial(update, codes=up_code, off=upper_off)

    row, square, plane = (2, 4), (2, 4, 8), (2, 4, 8, 16)
    f5, sent = low(right_sides, 5, [], [], level=5, inverse=[lower_inv], low=True)
    near5 = [spread(sent, (1, 2, 4))]
    f4, sent = low(right_sides, 4, [("one", 14)], [near5], level=4, inverse=[lower_inv], low=True)
    near4 = collected(sent, square)
    (r3,) = low(right_sides, 3, [("one", 13)], [near5])
    f3, sent = low(r3, None, [("halves", 9)], [near4], level=3, inverse=[lower_inv], low=True)
    near3 = collected(sent, plane)
    (r2,) = low(right_sides, 2, [("one", 12), ("halves", 8)], [near5, near4])
    f2, sent = low(r2, None, [("halves", 5)], [near3], level=2, inverse=[lower_inv], low=True)
    near2 = collected(sent, plane)
    (r1,) = low(right_sides, 1, [("one", 11), ("halves", 7), ("halves", 4)], [near5, near4, near3])
    far2 = swapped(pick(beside[0, 2:3], near2), "group", 1)
    more2 = swapped(pick(beside[0, 1:2], near2), "group", 1)
    f1, sent = low(
        r1, None, [("far", 2)], [near2 + (far2,)], level=1, inverse=[lower_inv], low=True
    )
    near1 = collected(sent, plane)
    (r0,) = low(
        right_sides,
        0,
        [("one", 10), ("halves", 6), ("halves", 3), ("far", 1)],
        [near5, near4, near3, near2 + (more2,)],
    )
    asked1 = lax.all_to_all(
        pick(every[:, 0], near1), "group", 0, 0, tiled=True, axis_index_groups=half
    )
    _, s0, sent = low(
        r0, None, [("planes", 0)], [[asked1]], level=0, inverse=[lower_inv, upper_inv], low=True
    )

    near0 = collected(sent, plane)
    asked0 = lax.all_to_all(
        pick(every[:, 1], near0), "group", 0, 0, tiled=True, axis_index_groups=half
    )
    more0 = swapped(pick(beside[1, 1:2], near0), "group", 1)
    s1, sent = up(f1, None, [("planes", 0)], [[asked0]], level=1, inverse=[upper_inv], low=True)
    near1 = collected(sent, plane)
    (r2,) = up(f2, None, [("far", 1)], [near0 + (more0,)])
    far1 = swapped(pick(beside[1, 2:3], near1), "group", 1)
    s2, sent = up(
        r2, None, [("far", 2)], [near1 + (far1,)], level=2, inverse=[upper_inv], low=True
    )
    near2 = collected(sent, plane)
    (r3,) = up(f3, None, [("halves", 3), ("halves", 4)], [near0, near1])
    s3, sent = up(r3, None, [("halves", 5)], [near2], level=3, inverse=[upper_inv], low=True)
    near3 = collected(sent, square)
    (r4,) = up(f4, None, [("halves", 6), ("halves", 7), ("halves", 8)], [near0, near1, near2])
    s4, sent = up(r4, None, [("halves", 9)], [near3], level=4, inverse=[upper_inv], low=True)
    near4 = [spread(sent, (1, 2, 4))]
    (r5,) = up(
        f5,
        None,
        [("halves", 10), ("halves", 11), ("halves", 12), ("halves", 13)],
        [near0, near1, near2, near3],
    )
    (s5,) = up(r5, None, [("one", 14)], [near4], level=5, inverse=[upper_inv])
    return jnp.stack([s0, s1, s2, s3, s4, s5])


def solution(mesh):
    return jax.shard_map(
        on_device,
        mesh=mesh,
        in_specs=(
            P(None, ("group", "sub"), None, None),
            P(None, ("group", "sub"), None, None),
            P(None, ("group", "sub"), None, None),
            P(None, ("group", "sub"), None, None, None),
            P(None, ("group", "sub"), None, None, None),
            P(None, ("group", "sub"), None),
            P(None, ("group", "sub"), None),
        ),
        out_specs=P(None, ("group", "sub"), None, None),
        check_vma=False,
    )
```

time: 366 us -> 203 us (0.55)
  waiting for transfers between devices: 217 us -> 41.2 us
  blocking collectives: 0 us -> 40.9 us
  starting transfers between devices: 92.6 us -> 60.2 us
  Pallas kernels: 0 us -> 23.8 us
  matrix products: 21.3 us -> 0 us
  local copies, waits for them, and re-layouts: 23.9 us -> 35.1 us
  other arithmetic: 6.8 us -> 0.3 us
    ppermute x50 -> x14, waiting for transfers between devices: 217 us -> 11.9 us  [swapped(): lax.ppermute(block, axis, [(i, i ^ mask) for i in range(lax.axis_size(axi...]
    ppermute x50 -> x14, starting transfers between devices: 92.6 us -> 28.3 us  [swapped(): lax.ppermute(block, axis, [(i, i ^ mask) for i in range(lax.axis_size(axi...]
    all_to_all x0 -> x4, blocking collectives: none -> 40.9 us  [spread(): lax.all_to_all(copies, 'sub', 0, 0, tiled=True, axis_index_groups=span(ma...]
    all_to_all x0 -> x8, starting transfers between devices: none -> 31.8 us  [the longest x6 24.2 us: spread(): lax.all_to_all(copies, 'sub', 0, 0, tiled=True, axis_index_groups=span(ma...]
    all_to_all x0 -> x8, waiting for transfers between devices: none -> 29.3 us  [the longest x6 22 us: spread(): lax.all_to_all(copies, 'sub', 0, 0, tiled=True, axis_index_groups=span(ma...]
    pallas_call x0 -> x25, Pallas kernels: none -> 23.8 us  [the longest x19 18.7 us: update(): pl.pallas_call(functools.partial(update_kernel, tuple(plan), first, level...]
    unnamed x34 -> x49, local copies, waits for them, and re-layouts: 0.47 us -> 24.1 us
    dot_general x20 -> x0, matrix products: 21.3 us -> none  [the longest x11 12.9 us: apply_inverse(): jnp.einsum('jrb,jbc->jrc', residual.astype(jnp.bfloat16), inverse, prefer...]
  transfers between devices with their start and end apart: 50 -> 22, of which waited for: 48 -> 18; matrix products, arithmetic and copies ran while one was open for 5% -> 3% of each run, Pallas kernels for 0% -> 4%
where the time goes in v1:
time: 203 us; the launch traced here: 202 us
  starting transfers between devices  60.2 us (30%)
  waiting for transfers between devices  41.2 us (20%)
  blocking collectives  40.9 us (20%)
  local copies, waits for them, and re-layouts  35.1 us (17%)
  Pallas kernels  23.8 us (12%)
    all_to_all x4, blocking collectives, spread(): lax.all_to_all(copies, 'sub', 0, 0, tiled=True, axis_index_groups=span(ma...  40.9 us
    ppermute x14, starting transfers between devices, swapped(): lax.ppermute(block, axis, [(i, i ^ mask) for i in range(lax.axis_size(axi...  28.3 us
    all_to_all x6, starting transfers between devices, spread(): lax.all_to_all(copies, 'sub', 0, 0, tiled=True, axis_index_groups=span(ma...  24.2 us
    unnamed x49, local copies, waits for them, and re-layouts  24.1 us
    all_to_all x6, waiting for transfers between devices, spread(): lax.all_to_all(copies, 'sub', 0, 0, tiled=True, axis_index_groups=span(ma...  22 us
    pallas_call x19, Pallas kernels, update(): pl.pallas_call(functools.partial(update_kernel, tuple(plan), first, level...  18.7 us
    ppermute x14, waiting for transfers between devices, swapped(): lax.ppermute(block, axis, [(i, i ^ mask) for i in range(lax.axis_size(axi...  11.9 us
    all_to_all x1, waiting for transfers between devices, on_device(): lax.all_to_all(pick(every[:, 1], near0), 'group', 0, 0, tiled=True, axis_...  7.27 us
  transfers between devices with their start and end apart: 22, of which 18 were waited for; matrix products, arithmetic and copies ran while one was open for 3% of the time, Pallas kernels for 4%

profile of v1, /device:TPU:1, one launch (start us, length us, event | category | flops | bytes accessed | tf_op | source)
XLA Modules:
  0.0 201.9 jit_solution(4826218332445571878)
XLA Ops:
  2.7 6.5 %all-to-all-start = ((bf16[16,32,128]{2,1,0:T(8,128)(2,1)}), bf16[16,32,128]{2,1,0:T(8,128)(2,1)S(1)}, u32[]{:S(2)}, u32[]{:S(2)}) async-start(bf16[16,32,128]{2,1,0:T(8,128)(2,1)} %bitcast), calls=%async_computation | async-start | bytes 262144 | tf_op jit(solution)/shard_map/all_to_all | solution.py:40
  14.5 2.1 %copy-done = bf16[15,2,4,128,128]{4,3,2,1,0:T(8,128)(2,1)S(1)} copy-done((bf16[15,2,4,128,128]{4,3,2,1,0:T(8,128)(2,1)S(1)}, bf16[15,2,4,128,128]{4,3,2,1,0:T(8,128)(2,1)}, u32[]{:S(2)}) %copy-start) | copy-done | bytes 3932184
  19.7 8.0 %all_to_all.60.refs_3_.refs_4_ = bf16[16,32,128]{2,1,0:T(8,128)(2,1)S(1)} all-to-all(bf16[16,32,128]{2,1,0:T(8,128)(2,1)S(1)} %bitcast.47), channel_id=1, replica_groups={{0,2,4,6,8,10,12,14},{1,3,5,7,9,11,13,15},{16,18,20,22,24,26,28,30},{17..., dimensions={0} | all-to-all | bytes 262144 | tf_op jit(solution)/shard_map/all_to_all | solution.py:40
  27.7 2.2 %collective-permute-start = (bf16[16,32,128]{2,1,0:T(8,128)(2,1)S(1)}, bf16[16,32,128]{2,1,0:T(8,128)(2,1)S(1)}, u32[]{:S(2)}, u32[]{:S(2)}) collective-permute-start(bf16[16,32,128]{2,1,0:T(8,128)(2,1)S(1)} %all_to_all.60.refs_3_.refs_4_), channel_id=1, source_target_pairs={{0,1},{1,0},{2,3},{3,2},{4,5},{5,4},{6,7},{7,6},{8,9},{9,8},{10,11... | collective-permute-start | bytes 393224 | tf_op jit(solution)/shard_map/ppermute | solution.py:34
  32.0 11.7 %all_to_all.61.refs_3_.refs_6_ = bf16[32,32,128]{2,1,0:T(8,128)(2,1)S(1)} all-to-all(bf16[32,32,128]{2,1,0:T(8,128)(2,1)S(1)} %bitcast.44), channel_id=1, replica_groups={{0,2,4,6,8,10,12,14,16,18,20,22,24,26,28,30},{1,3,5,7,9,11,13,15,17,19,..., dimensions={0} | all-to-all | bytes 524288 | tf_op jit(solution)/shard_map/all_to_all | solution.py:40
  48.6 3.5 %all-to-all-start.3 = ((bf16[32,32,128]{2,1,0:T(8,128)(2,1)}), bf16[32,32,128]{2,1,0:T(8,128)(2,1)S(1)}, u32[]{:S(2)}, u32[]{:S(2)}) async-start(bf16[32,32,128]{2,1,0:T(8,128)(2,1)} %bitcast.3), calls=%async_computation.3 | async-start | bytes 524288 | tf_op jit(solution)/shard_map/all_to_all | solution.py:40
  54.0 5.8 %all-to-all-done.3.refs_0_.refs_8_.refs_3_ = bf16[32,32,128]{2,1,0:T(8,128)(2,1)S(1)} async-done(((bf16[32,32,128]{2,1,0:T(8,128)(2,1)}), bf16[32,32,128]{2,1,0:T(8,128)(2,1)S(1)}, u32[]{:S(2)}, u32[]{:S(2)}) %all-to-all-start.3) | async-done | bytes 262176 | tf_op jit(solution)/shard_map/all_to_all | solution.py:40
  65.1 2.1 %copy-done.2 = bf16[15,2,4,128,128]{4,3,2,1,0:T(8,128)(2,1)S(1)} copy-done((bf16[15,2,4,128,128]{4,3,2,1,0:T(8,128)(2,1)S(1)}, bf16[15,2,4,128,128]{4,3,2,1,0:T(8,128)(2,1)}, u32[]{:S(2)}) %copy-start.2) | copy-done | bytes 3932184
  71.1 3.5 %all-to-all-start.4 = ((bf16[32,32,128]{2,1,0:T(8,128)(2,1)}), bf16[32,32,128]{2,1,0:T(8,128)(2,1)S(1)}, u32[]{:S(2)}, u32[]{:S(2)}) async-start(bf16[32,32,128]{2,1,0:T(8,128)(2,1)} %bitcast.12), calls=%async_computation.4 | async-start | bytes 524288 | tf_op jit(solution)/shard_map/all_to_all | solution.py:40
  74.7 3.1 %collective-permute-start.5 = (s32[2,2,8]{2,1,0:T(2,128)S(1)}, s32[2,2,8]{2,1,0:T(2,128)S(1)}, u32[]{:S(2)}, u32[]{:S(2)}) collective-permute-start(s32[2,2,8]{2,1,0:T(2,128)S(1)} %pad_add_fusion.2), channel_id=1, source_target_pairs={{0,64},{32,96},{64,0},{96,32},{128,192},{160,224},{192,128},{224,1... | collective-permute-start | bytes 392 | tf_op jit(solution)/shard_map/ppermute | solution.py:34
  79.3 2.8 %all-to-all-done.4.refs_0_ = bf16[32,32,128]{2,1,0:T(8,128)(2,1)S(1)} async-done(((bf16[32,32,128]{2,1,0:T(8,128)(2,1)}), bf16[32,32,128]{2,1,0:T(8,128)(2,1)S(1)}, u32[]{:S(2)}, u32[]{:S(2)}) %all-to-all-start.4) | async-done | bytes 262176 | tf_op jit(solution)/shard_map/all_to_all | solution.py:40
  86.6 4.3 %all-to-all-start.5 = ((bf16[32,32,128]{2,1,0:T(8,128)(2,1)}), bf16[32,32,128]{2,1,0:T(8,128)(2,1)S(1)}, u32[]{:S(2)}, u32[]{:S(2)}) async-start(bf16[32,32,128]{2,1,0:T(8,128)(2,1)} %shard_map.84), calls=%async_computation.5 | async-start | bytes 524288 | tf_op jit(solution)/shard_map/all_to_all | solution.py:205
  94.1 4.6 %collective-permute-done.4.refs_10_ = bf16[8,32,128]{2,1,0:T(8,128)(2,1)S(1)} collective-permute-done((bf16[8,32,128]{2,1,0:T(8,128)(2,1)S(1)}, bf16[8,32,128]{2,1,0:T(8,128)(2,1)S(1)}, u32[]{:S(2)}, u32[]{:S(2)}) %collective-permute-start.4) | collective-permute-done | bytes 65568 | tf_op jit(solution)/shard_map/ppermute | solution.py:34
  98.6 2.1 %copy-done.4 = bf16[15,2,4,128,128]{4,3,2,1,0:T(8,128)(2,1)S(1)} copy-done((bf16[15,2,4,128,128]{4,3,2,1,0:T(8,128)(2,1)S(1)}, bf16[15,2,4,128,128]{4,3,2,1,0:T(8,128)(2,1)}, u32[]{:S(2)}) %copy-start.4) | copy-done | bytes 3932184
  101.8 2.1 %copy-done.5 = bf16[15,2,4,128,128]{4,3,2,1,0:T(8,128)(2,1)S(1)} copy-done((bf16[15,2,4,128,128]{4,3,2,1,0:T(8,128)(2,1)S(1)}, bf16[15,2,4,128,128]{4,3,2,1,0:T(8,128)(2,1)}, u32[]{:S(2)}) %copy-start.5) | copy-done | bytes 3932184
  106.4 3.6 %all-to-all-start.6 = ((bf16[32,32,128]{2,1,0:T(8,128)(2,1)}), bf16[32,32,128]{2,1,0:T(8,128)(2,1)S(1)}, u32[]{:S(2)}, u32[]{:S(2)}) async-start(bf16[32,32,128]{2,1,0:T(8,128)(2,1)} %bitcast.15), calls=%async_computation.6 | async-start | bytes 524288 | tf_op jit(solution)/shard_map/all_to_all | solution.py:40
  110.4 6.9 %all-to-all-done.6.refs_0_.refs_3_ = bf16[32,32,128]{2,1,0:T(8,128)(2,1)S(1)} async-done(((bf16[32,32,128]{2,1,0:T(8,128)(2,1)}), bf16[32,32,128]{2,1,0:T(8,128)(2,1)S(1)}, u32[]{:S(2)}, u32[]{:S(2)}) %all-to-all-start.6) | async-done | bytes 262176 | tf_op jit(solution)/shard_map/all_to_all | solution.py:40
  117.3 3.0 %collective-permute-start.8 = (bf16[32,32,128]{2,1,0:T(8,128)(2,1)S(1)}, bf16[32,32,128]{2,1,0:T(8,128)(2,1)S(1)}, u32[]{:S(2)}, u32[]{:S(2)}) collective-permute-start(bf16[32,32,128]{2,1,0:T(8,128)(2,1)S(1)} %all-to-all-done.6.refs_0_.refs_3_), channel_id=1, source_target_pairs={{0,1},{1,0},{2,3},{3,2},{4,5},{5,4},{6,7},{7,6},{8,9},{9,8},{10,11... | collective-permute-start | bytes 786440 | tf_op jit(solution)/shard_map/ppermute | solution.py:34
  122.9 3.4 %all-to-all-start.7 = ((bf16[32,32,128]{2,1,0:T(8,128)(2,1)}), bf16[32,32,128]{2,1,0:T(8,128)(2,1)S(1)}, u32[]{:S(2)}, u32[]{:S(2)}) async-start(bf16[32,32,128]{2,1,0:T(8,128)(2,1)} %shard_map.86), calls=%async_computation.7 | async-start | bytes 524288 | tf_op jit(solution)/shard_map/all_to_all | solution.py:213
  126.4 7.3 %all-to-all-done.7.refs_3_ = bf16[32,32,128]{2,1,0:T(8,128)(2,1)S(1)} async-done(((bf16[32,32,128]{2,1,0:T(8,128)(2,1)}), bf16[32,32,128]{2,1,0:T(8,128)(2,1)S(1)}, u32[]{:S(2)}, u32[]{:S(2)}) %all-to-all-start.7) | async-done | bytes 262176 | tf_op jit(solution)/shard_map/all_to_all | solution.py:213
  133.7 2.1 %copy-done.6 = bf16[15,2,4,128,128]{4,3,2,1,0:T(8,128)(2,1)S(1)} copy-done((bf16[15,2,4,128,128]{4,3,2,1,0:T(8,128)(2,1)S(1)}, bf16[15,2,4,128,128]{4,3,2,1,0:T(8,128)(2,1)}, u32[]{:S(2)}) %copy-start.6) | copy-done | bytes 3932184
  136.9 10.7 %all_to_all.62.refs_0_.refs_3_.refs_5_ = bf16[32,32,128]{2,1,0:T(8,128)(2,1)S(1)} all-to-all(bf16[32,32,128]{2,1,0:T(8,128)(2,1)S(1)} %bitcast.45), channel_id=1, replica_groups={{0,2,4,6,8,10,12,14,16,18,20,22,24,26,28,30},{1,3,5,7,9,11,13,15,17,19,..., dimensions={0} | all-to-all | bytes 524288 | tf_op jit(solution)/shard_map/all_to_all | solution.py:40
  147.6 3.8 %collective-permute-start.10 = (bf16[32,32,128]{2,1,0:T(8,128)(2,1)S(1)}, bf16[32,32,128]{2,1,0:T(8,128)(2,1)S(1)}, u32[]{:S(2)}, u32[]{:S(2)}) collective-permute-start(bf16[32,32,128]{2,1,0:T(8,128)(2,1)S(1)} %all_to_all.62.refs_0_.refs_3_.refs_5_), channel_id=1, source_target_pairs={{0,1},{1,0},{2,3},{3,2},{4,5},{5,4},{6,7},{7,6},{8,9},{9,8},{10,11... | collective-permute-start | bytes 786440 | tf_op jit(solution)/shard_map/ppermute | solution.py:34
  157.8 10.5 %all_to_all.63.refs_3_.refs_7_ = bf16[32,32,128]{2,1,0:T(8,128)(2,1)S(1)} all-to-all(bf16[32,32,128]{2,1,0:T(8,128)(2,1)S(1)} %bitcast.46), channel_id=1, replica_groups={{0,2,4,6,8,10,12,14,16,18,20,22,24,26,28,30},{1,3,5,7,9,11,13,15,17,19,..., dimensions={0} | all-to-all | bytes 524288 | tf_op jit(solution)/shard_map/all_to_all | solution.py:40
  168.3 2.8 %collective-permute-start.12 = (bf16[32,32,128]{2,1,0:T(8,128)(2,1)S(1)}, bf16[32,32,128]{2,1,0:T(8,128)(2,1)S(1)}, u32[]{:S(2)}, u32[]{:S(2)}) collective-permute-start(bf16[32,32,128]{2,1,0:T(8,128)(2,1)S(1)} %all_to_all.63.refs_3_.refs_7_), channel_id=1, source_target_pairs={{0,1},{1,0},{2,3},{3,2},{4,5},{5,4},{6,7},{7,6},{8,9},{9,8},{10,11... | collective-permute-start | bytes 786440 | tf_op jit(solution)/shard_map/ppermute | solution.py:34
  174.0 3.4 %all-to-all-start.10 = ((bf16[16,32,128]{2,1,0:T(8,128)(2,1)}), bf16[16,32,128]{2,1,0:T(8,128)(2,1)S(1)}, u32[]{:S(2)}, u32[]{:S(2)}) async-start(bf16[16,32,128]{2,1,0:T(8,128)(2,1)} %bitcast.23), calls=%async_computation.10 | async-start | bytes 262144 | tf_op jit(solution)/shard_map/all_to_all | solution.py:40
  180.5 2.3 %all-to-all-done.10.refs_3_.refs_9_ = bf16[16,32,128]{2,1,0:T(8,128)(2,1)S(1)} async-done(((bf16[16,32,128]{2,1,0:T(8,128)(2,1)}), bf16[16,32,128]{2,1,0:T(8,128)(2,1)S(1)}, u32[]{:S(2)}, u32[]{:S(2)}) %all-to-all-start.10) | async-done | bytes 131104 | tf_op jit(solution)/shard_map/all_to_all | solution.py:40
  185.3 2.1 %copy-done.9 = bf16[15,2,4,128,128]{4,3,2,1,0:T(8,128)(2,1)S(1)} copy-done((bf16[15,2,4,128,128]{4,3,2,1,0:T(8,128)(2,1)S(1)}, bf16[15,2,4,128,128]{4,3,2,1,0:T(8,128)(2,1)}, u32[]{:S(2)}) %copy-start.9) | copy-done | bytes 3932184
  189.2 3.6 %all-to-all-start.11 = ((bf16[16,32,128]{2,1,0:T(8,128)(2,1)}), bf16[16,32,128]{2,1,0:T(8,128)(2,1)S(1)}, u32[]{:S(2)}, u32[]{:S(2)}) async-start(bf16[16,32,128]{2,1,0:T(8,128)(2,1)} %bitcast.25), calls=%async_computation.11 | async-start | bytes 262144 | tf_op jit(solution)/shard_map/all_to_all | solution.py:40
  192.8 2.1 %copy-done.10 = bf16[15,2,4,128,128]{4,3,2,1,0:T(8,128)(2,1)S(1)} copy-done((bf16[15,2,4,128,128]{4,3,2,1,0:T(8,128)(2,1)S(1)}, bf16[15,2,4,128,128]{4,3,2,1,0:T(8,128)(2,1)}, u32[]{:S(2)}) %copy-start.10) | copy-done | bytes 3932184
  195.9 2.2 %all-to-all-done.11.refs_3_ = bf16[16,32,128]{2,1,0:T(8,128)(2,1)S(1)} async-done(((bf16[16,32,128]{2,1,0:T(8,128)(2,1)}), bf16[16,32,128]{2,1,0:T(8,128)(2,1)S(1)}, u32[]{:S(2)}, u32[]{:S(2)}) %all-to-all-start.11) | async-done | bytes 131104 | tf_op jit(solution)/shard_map/all_to_all | solution.py:40
  198.1 2.1 %copy-done.11 = bf16[15,2,4,128,128]{4,3,2,1,0:T(8,128)(2,1)S(1)} copy-done((bf16[15,2,4,128,128]{4,3,2,1,0:T(8,128)(2,1)S(1)}, bf16[15,2,4,128,128]{4,3,2,1,0:T(8,128)(2,1)}, u32[]{:S(2)}) %copy-start.11) | copy-done | bytes 3932184
  (161 shorter events, 65.0 us)
Async XLA Ops:
  2.7 11.8 %all-to-all-start = ((bf16[16,32,128]{2,1,0:T(8,128)(2,1)}), bf16[16,32,128]{2,1,0:T(8,128)(2,1)S(1)}, u32[]{:S(2)}, u32[]{:S(2)}) async-start(bf16[16,32,128]{2,1,0:T(8,128)(2,1)} %bitcast), calls=%async_computation | async-start | bytes 262144 | tf_op jit(solution)/shard_map/all_to_all | solution.py:40
  18.6 11.3 %copy-start.1 = (bf16[15,2,4,128,128]{4,3,2,1,0:T(8,128)(2,1)S(1)}, bf16[15,2,4,128,128]{4,3,2,1,0:T(8,128)(2,1)}, u32[]{:S(2)}) copy-start(bf16[15,2,4,128,128]{4,3,2,1,0:T(8,128)(2,1)} %refs_2_.26) | copy-start | bytes 11796484
  18.6 12.3 %copy-start.14 = (bf16[6,2,128,128]{3,2,1,0:T(8,128)(2,1)S(1)}, bf16[6,2,128,128]{3,2,1,0:T(8,128)(2,1)}, u32[]{:S(2)}) copy-start(bf16[6,2,128,128]{3,2,1,0:T(8,128)(2,1)} %refs_4_.5) | copy-start | bytes 1179652
  27.7 3.2 %collective-permute-start = (bf16[16,32,128]{2,1,0:T(8,128)(2,1)S(1)}, bf16[16,32,128]{2,1,0:T(8,128)(2,1)S(1)}, u32[]{:S(2)}, u32[]{:S(2)}) collective-permute-start(bf16[16,32,128]{2,1,0:T(8,128)(2,1)S(1)} %all_to_all.60.refs_3_.refs_4_), channel_id=1, source_target_pairs={{0,1},{1,0},{2,3},{3,2},{4,5},{5,4},{6,7},{7,6},{8,9},{9,8},{10,11... | collective-permute-start | bytes 393224 | tf_op jit(solution)/shard_map/ppermute | solution.py:34
  43.7 3.1 %collective-permute-start.1 = (bf16[32,32,128]{2,1,0:T(8,128)(2,1)S(1)}, bf16[32,32,128]{2,1,0:T(8,128)(2,1)S(1)}, u32[]{:S(2)}, u32[]{:S(2)}) collective-permute-start(bf16[32,32,128]{2,1,0:T(8,128)(2,1)S(1)} %all_to_all.61.refs_3_.refs_6_), channel_id=1, source_target_pairs={{0,1},{1,0},{2,3},{3,2},{4,5},{5,4},{6,7},{7,6},{8,9},{9,8},{10,11... | collective-permute-start | bytes 786440 | tf_op jit(solution)/shard_map/ppermute | solution.py:34
  46.5 5.7 %copy-start.20 = (s32[15,2,4]{0,2,1:T(4,128)S(1)}, s32[15,2,4]{0,2,1:T(4,128)}, u32[]{:S(2)}) copy-start(s32[15,2,4]{0,2,1:T(4,128)} %param.13) | copy-start | bytes 1444
  46.5 5.7 %copy-start.19 = (s32[15,2,4]{0,2,1:T(4,128)S(1)}, s32[15,2,4]{0,2,1:T(4,128)}, u32[]{:S(2)}) copy-start(s32[15,2,4]{0,2,1:T(4,128)} %param.12) | copy-start | bytes 1444
  46.5 18.5 %copy-start.18 = (f32[6,2,32,128]{3,2,1,0:T(8,128)S(1)}, f32[6,2,32,128]{3,2,1,0:T(8,128)}, u32[]{:S(2)}) copy-start(f32[6,2,32,128]{3,2,1,0:T(8,128)} %refs_0_.11) | copy-start | bytes 589828
  48.6 11.1 %all-to-all-start.3 = ((bf16[32,32,128]{2,1,0:T(8,128)(2,1)}), bf16[32,32,128]{2,1,0:T(8,128)(2,1)S(1)}, u32[]{:S(2)}, u32[]{:S(2)}) async-start(bf16[32,32,128]{2,1,0:T(8,128)(2,1)} %bitcast.3), calls=%async_computation.3 | async-start | bytes 524288 | tf_op jit(solution)/shard_map/all_to_all | solution.py:40
  52.3 9.2 %collective-permute-start.3 = (s32[2,3,8]{2,1,0:T(4,128)S(1)}, s32[2,3,8]{2,1,0:T(4,128)S(1)}, u32[]{:S(2)}, u32[]{:S(2)}) collective-permute-start(s32[2,3,8]{2,1,0:T(4,128)S(1)} %pad_add_fusion), channel_id=1, source_target_pairs={{0,32},{32,0},{64,96},{96,64},{128,160},{160,128},{192,224},{224,1... | collective-permute-start | bytes 584 | tf_op jit(solution)/shard_map/ppermute | solution.py:34
  59.8 3.0 %collective-permute-start.2 = (bf16[32,32,128]{2,1,0:T(8,128)(2,1)S(1)}, bf16[32,32,128]{2,1,0:T(8,128)(2,1)S(1)}, u32[]{:S(2)}, u32[]{:S(2)}) collective-permute-start(bf16[32,32,128]{2,1,0:T(8,128)(2,1)S(1)} %all-to-all-done.3.refs_0_.refs_8_.refs_3_), channel_id=1, source_target_pairs={{0,1},{1,0},{2,3},{3,2},{4,5},{5,4},{6,7},{7,6},{8,9},{9,8},{10,11... | collective-permute-start | bytes 786440 | tf_op jit(solution)/shard_map/ppermute | solution.py:34
  63.3 4.8 %collective-permute-start.6 = (bf16[8,32,128]{2,1,0:T(8,128)(2,1)S(1)}, bf16[8,32,128]{2,1,0:T(8,128)(2,1)S(1)}, u32[]{:S(2)}, u32[]{:S(2)}) collective-permute-start(bf16[8,32,128]{2,1,0:T(8,128)(2,1)S(1)} %shard_map.82), channel_id=1, source_target_pairs={{0,32},{32,0},{64,96},{96,64},{128,160},{160,128},{192,224},{224,1... | collective-permute-start | bytes 196616 | tf_op jit(solution)/shard_map/ppermute | solution.py:34
  71.1 11.0 %all-to-all-start.4 = ((bf16[32,32,128]{2,1,0:T(8,128)(2,1)}), bf16[32,32,128]{2,1,0:T(8,128)(2,1)S(1)}, u32[]{:S(2)}, u32[]{:S(2)}) async-start(bf16[32,32,128]{2,1,0:T(8,128)(2,1)} %bitcast.12), calls=%async_computation.4 | async-start | bytes 524288 | tf_op jit(solution)/shard_map/all_to_all | solution.py:40
  74.6 27.1 %copy-start.15 = (bf16[6,2,128,128]{3,2,1,0:T(8,128)(2,1)S(1)}, bf16[6,2,128,128]{3,2,1,0:T(8,128)(2,1)}, u32[]{:S(2)}) copy-start(bf16[6,2,128,128]{3,2,1,0:T(8,128)(2,1)} %refs_4_.7) | copy-start | bytes 1179652
  74.7 4.1 %collective-permute-start.5 = (s32[2,2,8]{2,1,0:T(2,128)S(1)}, s32[2,2,8]{2,1,0:T(2,128)S(1)}, u32[]{:S(2)}, u32[]{:S(2)}) collective-permute-start(s32[2,2,8]{2,1,0:T(2,128)S(1)} %pad_add_fusion.2), channel_id=1, source_target_pairs={{0,64},{32,96},{64,0},{96,32},{128,192},{160,224},{192,128},{224,1... | collective-permute-start | bytes 392 | tf_op jit(solution)/shard_map/ppermute | solution.py:34
  82.1 3.1 %collective-permute-start.7 = (bf16[32,32,128]{2,1,0:T(8,128)(2,1)S(1)}, bf16[32,32,128]{2,1,0:T(8,128)(2,1)S(1)}, u32[]{:S(2)}, u32[]{:S(2)}) collective-permute-start(bf16[32,32,128]{2,1,0:T(8,128)(2,1)S(1)} %all-to-all-done.4.refs_0_), channel_id=1, source_target_pairs={{0,1},{1,0},{2,3},{3,2},{4,5},{5,4},{6,7},{7,6},{8,9},{9,8},{10,11... | collective-permute-start | bytes 786440 | tf_op jit(solution)/shard_map/ppermute | solution.py:34
  86.6 15.1 %all-to-all-start.5 = ((bf16[32,32,128]{2,1,0:T(8,128)(2,1)}), bf16[32,32,128]{2,1,0:T(8,128)(2,1)S(1)}, u32[]{:S(2)}, u32[]{:S(2)}) async-start(bf16[32,32,128]{2,1,0:T(8,128)(2,1)} %shard_map.84), calls=%async_computation.5 | async-start | bytes 524288 | tf_op jit(solution)/shard_map/all_to_all | solution.py:205
  92.3 6.3 %collective-permute-start.4 = (bf16[8,32,128]{2,1,0:T(8,128)(2,1)S(1)}, bf16[8,32,128]{2,1,0:T(8,128)(2,1)S(1)}, u32[]{:S(2)}, u32[]{:S(2)}) collective-permute-start(bf16[8,32,128]{2,1,0:T(8,128)(2,1)S(1)} %shard_map.79), channel_id=1, source_target_pairs={{0,32},{32,0},{64,96},{96,64},{128,160},{160,128},{192,224},{224,1... | collective-permute-start | bytes 196616 | tf_op jit(solution)/shard_map/ppermute | solution.py:34
  101.7 2.1 %copy-start.5 = (bf16[15,2,4,128,128]{4,3,2,1,0:T(8,128)(2,1)S(1)}, bf16[15,2,4,128,128]{4,3,2,1,0:T(8,128)(2,1)}, u32[]{:S(2)}) copy-start(bf16[15,2,4,128,128]{4,3,2,1,0:T(8,128)(2,1)} %refs_2_.26) | copy-start | bytes 11796484
  106.4 10.9 %all-to-all-start.6 = ((bf16[32,32,128]{2,1,0:T(8,128)(2,1)}), bf16[32,32,128]{2,1,0:T(8,128)(2,1)S(1)}, u32[]{:S(2)}, u32[]{:S(2)}) async-start(bf16[32,32,128]{2,1,0:T(8,128)(2,1)} %bitcast.15), calls=%async_computation.6 | async-start | bytes 524288 | tf_op jit(solution)/shard_map/all_to_all | solution.py:40
  117.3 4.2 %collective-permute-start.8 = (bf16[32,32,128]{2,1,0:T(8,128)(2,1)S(1)}, bf16[32,32,128]{2,1,0:T(8,128)(2,1)S(1)}, u32[]{:S(2)}, u32[]{:S(2)}) collective-permute-start(bf16[32,32,128]{2,1,0:T(8,128)(2,1)S(1)} %all-to-all-done.6.refs_0_.refs_3_), channel_id=1, source_target_pairs={{0,1},{1,0},{2,3},{3,2},{4,5},{5,4},{6,7},{7,6},{8,9},{9,8},{10,11... | collective-permute-start | bytes 786440 | tf_op jit(solution)/shard_map/ppermute | solution.py:34
  122.9 10.8 %all-to-all-start.7 = ((bf16[32,32,128]{2,1,0:T(8,128)(2,1)}), bf16[32,32,128]{2,1,0:T(8,128)(2,1)S(1)}, u32[]{:S(2)}, u32[]{:S(2)}) async-start(bf16[32,32,128]{2,1,0:T(8,128)(2,1)} %shard_map.86), calls=%async_computation.7 | async-start | bytes 524288 | tf_op jit(solution)/shard_map/all_to_all | solution.py:213
  135.8 20.0 %copy-start.7 = (bf16[15,2,4,128,128]{4,3,2,1,0:T(8,128)(2,1)S(1)}, bf16[15,2,4,128,128]{4,3,2,1,0:T(8,128)(2,1)}, u32[]{:S(2)}) copy-start(bf16[15,2,4,128,128]{4,3,2,1,0:T(8,128)(2,1)} %refs_2_.35) | copy-start | bytes 11796484
  147.6 5.0 %collective-permute-start.10 = (bf16[32,32,128]{2,1,0:T(8,128)(2,1)S(1)}, bf16[32,32,128]{2,1,0:T(8,128)(2,1)S(1)}, u32[]{:S(2)}, u32[]{:S(2)}) collective-permute-start(bf16[32,32,128]{2,1,0:T(8,128)(2,1)S(1)} %all_to_all.62.refs_0_.refs_3_.refs_5_), channel_id=1, source_target_pairs={{0,1},{1,0},{2,3},{3,2},{4,5},{5,4},{6,7},{7,6},{8,9},{9,8},{10,11... | collective-permute-start | bytes 786440 | tf_op jit(solution)/shard_map/ppermute | solution.py:34
  152.0 3.8 %collective-permute-start.9 = (bf16[8,32,128]{2,1,0:T(8,128)(2,1)S(1)}, bf16[8,32,128]{2,1,0:T(8,128)(2,1)S(1)}, u32[]{:S(2)}, u32[]{:S(2)}) collective-permute-start(bf16[8,32,128]{2,1,0:T(8,128)(2,1)S(1)} %shard_map.88), channel_id=1, source_target_pairs={{0,32},{32,0},{64,96},{96,64},{128,160},{160,128},{192,224},{224,1... | collective-permute-start | bytes 196616 | tf_op jit(solution)/shard_map/ppermute | solution.py:34
  153.1 3.5 %collective-permute-start.11 = (bf16[8,32,128]{2,1,0:T(8,128)(2,1)S(1)}, bf16[8,32,128]{2,1,0:T(8,128)(2,1)S(1)}, u32[]{:S(2)}, u32[]{:S(2)}) collective-permute-start(bf16[8,32,128]{2,1,0:T(8,128)(2,1)S(1)} %shard_map.90), channel_id=1, source_target_pairs={{0,32},{32,0},{64,96},{96,64},{128,160},{160,128},{192,224},{224,1... | collective-permute-start | bytes 196616 | tf_op jit(solution)/shard_map/ppermute | solution.py:34
  168.3 4.0 %collective-permute-start.12 = (bf16[32,32,128]{2,1,0:T(8,128)(2,1)S(1)}, bf16[32,32,128]{2,1,0:T(8,128)(2,1)S(1)}, u32[]{:S(2)}, u32[]{:S(2)}) collective-permute-start(bf16[32,32,128]{2,1,0:T(8,128)(2,1)S(1)} %all_to_all.63.refs_3_.refs_7_), channel_id=1, source_target_pairs={{0,1},{1,0},{2,3},{3,2},{4,5},{5,4},{6,7},{7,6},{8,9},{9,8},{10,11... | collective-permute-start | bytes 786440 | tf_op jit(solution)/shard_map/ppermute | solution.py:34
  174.0 8.8 %all-to-all-start.10 = ((bf16[16,32,128]{2,1,0:T(8,128)(2,1)}), bf16[16,32,128]{2,1,0:T(8,128)(2,1)S(1)}, u32[]{:S(2)}, u32[]{:S(2)}) async-start(bf16[16,32,128]{2,1,0:T(8,128)(2,1)} %bitcast.23), calls=%async_computation.10 | async-start | bytes 262144 | tf_op jit(solution)/shard_map/all_to_all | solution.py:40
  177.4 2.1 %copy-start.8 = (bf16[15,2,4,128,128]{4,3,2,1,0:T(8,128)(2,1)S(1)}, bf16[15,2,4,128,128]{4,3,2,1,0:T(8,128)(2,1)}, u32[]{:S(2)}) copy-start(bf16[15,2,4,128,128]{4,3,2,1,0:T(8,128)(2,1)} %refs_2_.35) | copy-start | bytes 11796484
  182.8 2.5 %collective-permute-start.13 = (bf16[16,32,128]{2,1,0:T(8,128)(2,1)S(1)}, bf16[16,32,128]{2,1,0:T(8,128)(2,1)S(1)}, u32[]{:S(2)}, u32[]{:S(2)}) collective-permute-start(bf16[16,32,128]{2,1,0:T(8,128)(2,1)S(1)} %all-to-all-done.10.refs_3_.refs_9_), channel_id=1, source_target_pairs={{0,1},{1,0},{2,3},{3,2},{4,5},{5,4},{6,7},{7,6},{8,9},{9,8},{10,11... | collective-permute-start | bytes 393224 | tf_op jit(solution)/shard_map/ppermute | solution.py:34
  189.2 8.9 %all-to-all-start.11 = ((bf16[16,32,128]{2,1,0:T(8,128)(2,1)}), bf16[16,32,128]{2,1,0:T(8,128)(2,1)S(1)}, u32[]{:S(2)}, u32[]{:S(2)}) async-start(bf16[16,32,128]{2,1,0:T(8,128)(2,1)} %bitcast.25), calls=%async_computation.11 | async-start | bytes 262144 | tf_op jit(solution)/shard_map/all_to_all | solution.py:40
  195.9 5.4 %copy-start.21 = (f32[6,2,32,128]{3,2,1,0:T(8,128)}, f32[6,2,32,128]{3,2,1,0:T(8,128)S(1)}, u32[]{:S(2)}) copy-start(f32[6,2,32,128]{3,2,1,0:T(8,128)S(1)} %bitcast_dynamic-update-slice_fusion.1) | copy-start | bytes 589828
  (12 other events, 20.8 us)

commit v2 on v0

v2 whole, which is shorter than its diff:
```python
import functools

import jax
import jax.numpy as jnp
from jax import lax
from jax.experimental import pallas as pl
from jax.experimental.pallas import tpu as pltpu
from jax.sharding import PartitionSpec as P

SUB_BITS = 5
PLANE_BITS = 6
PLANE = 1 << PLANE_BITS
VMEM = pl.BlockSpec(memory_space=pltpu.VMEM)
SMEM = pl.BlockSpec(memory_space=pltpu.SMEM)
HBM = pl.BlockSpec(memory_space=pl.ANY)
PARAMS = pltpu.CompilerParams(vmem_limit_bytes=8 * 2**20)


def span(masks):
    groups, seen = [], set()
    for first in range(1 << SUB_BITS):
        if first not in seen:
            group = [first]
            for mask in masks:
                group = group + [member ^ mask for member in group]
            seen.update(group)
            groups.append(sorted(group))
    return groups


def swapped(block, axis, mask):
    return lax.ppermute(block, axis, [(i, i ^ mask) for i in range(lax.axis_size(axis))])


def spread(copies, masks):
    return lax.all_to_all(copies, "sub", 0, 0, tiled=True, axis_index_groups=span(masks))


def collected(copies, masks):
    own = spread(copies, masks)
    return own, swapped(own, "sub", 1)


def planes(copies):
    half = [[0, 1, 2, 3], [4, 5, 6, 7]]
    return lax.all_to_all(copies, "group", 0, 0, tiled=True, axis_index_groups=half)


def after(value, *others):
    return lax.optimization_barrier((value,) + others)[0]


def in_vmem(value):
    return pltpu.with_memory_space_constraint(value, pltpu.VMEM)


def in_smem(value):
    return pltpu.with_memory_space_constraint(value, pltpu.SMEM)


def in_hbm(value):
    return pltpu.with_memory_space_constraint(value, pltpu.HBM)


CORE, ODD, MINE, START16, START8, START8IN16, NONE = range(7)


def positions(sub, group):
    return jnp.stack(
        [sub & 1, group & 1, group & 3, (sub >> 4) * 32, (sub >> 3) * 16, (sub >> 3 & 1) * 16]
    )


def block(own, other, local, core):
    index = (local >> 2 << 1) | (local & 1)
    return jnp.where((local >> 1 & 1) == core, own[index], other[index])


def read(kind, start, refs, me, wanted, slot):
    if kind == "one":
        return refs[0][wanted]
    if kind == "planes":
        return refs[0][(wanted >> PLANE_BITS) * 8 + slot]
    if kind == "halves":
        local = wanted if start == NONE else wanted + me[start]
        return block(refs[0], refs[1], local, me[CORE])
    near = block(refs[0], refs[1], wanted & PLANE - 1, me[CORE])
    return jnp.where(wanted >> PLANE_BITS == me[ODD], near, refs[2][slot])


def send(ref, j, value):
    value = value.astype(jnp.bfloat16)
    for way in range(ref.shape[0] // 2):
        ref[2 * way + j] = value


FIRST = (14, 13, 9, 12, 8, 5)
BUFFERS = {"one": 1, "planes": 1, "halves": 2, "far": 3}


def coupled(total, j, plan, near, side, me, table, off):
    for (kind, p, start, shift), buffers in zip(plan, near):
        at = FIRST.index(p) if off.shape[0] == len(FIRST) else p
        matrices = off[at, j].reshape(512, 128)
        picked = [
            read(kind, start, buffers, me, table[2 * side + j, n, p], shift + j * 4 + n)
            for n in range(4)
        ]
        total = total - jnp.dot(
            jnp.concatenate(picked, 1), matrices, preferred_element_type=jnp.float32
        )
    return total


def times(total, matrix):
    return jnp.dot(total.astype(jnp.bfloat16), matrix, preferred_element_type=jnp.float32)


def update_kernel(plan, side, first, level, inverses, ways, me, table, off, base, *refs):
    refs = list(refs)
    near = [[refs.pop(0) for _ in range(BUFFERS[entry[0]])] for entry in plan]
    inverse = [refs.pop(0) for _ in range(inverses)]
    for j in range(2):
        total = base[first, j] if first is not None else base[j]
        total = coupled(total, j, plan, near, side, me, table, off)
        if not inverses:
            refs[0][j] = total
        for matrix in inverse:
            total = times(total, matrix[level, j])
        if inverses:
            refs[0][j] = total
        if ways:
            send(refs[-1], j, total)


def update(me, table, off, base, first, plan, near, side, level=0, inverse=(), ways=0):
    shape = (2,) + base.shape[-2:]
    shapes = [jax.ShapeDtypeStruct(shape, jnp.float32)]
    if ways:
        shapes.append(jax.ShapeDtypeStruct((2 * ways,) + shape[1:], jnp.bfloat16))
    arguments = [in_smem(me), in_smem(table), in_vmem(off), in_vmem(base)]
    for buffers in near:
        arguments += list(buffers)
    arguments += [in_vmem(matrix) for matrix in inverse]
    products = 2 * (4 * len(plan) + len(inverse))
    return pl.pallas_call(
        functools.partial(update_kernel, tuple(plan), side, first, level, len(inverse), ways),
        out_shape=shapes,
        in_specs=[SMEM, SMEM] + [VMEM] * (len(arguments) - 2),
        out_specs=[VMEM] * len(shapes),
        compiler_params=PARAMS,
        cost_estimate=pl.CostEstimate(
            flops=products * 2 * 32 * 128 * 128, bytes_accessed=products * 32768, transcendentals=0
        ),
    )(*arguments)


def first_kernel(level, pairs, *refs):
    right, matrix, off, lower, upper = refs[:5]
    out, low, right_kept, matrix_kept, off_kept, table, sems = refs[5:]
    copies = [
        (right, right_kept),
        (matrix, matrix_kept),
        (lower, table.at[pl.ds(0, 2)]),
        (upper, table.at[pl.ds(2, 2)]),
    ]
    copies += [(off.at[p], off_kept.at[at]) for at, p in enumerate(pairs)]
    copies = [pltpu.make_async_copy(*ends, sems.at[at]) for at, ends in enumerate(copies)]
    for copy in copies:
        copy.start()
    copies[0].wait()
    copies[1].wait()
    for j in range(2):
        total = times(right_kept[level, j], matrix_kept[level, j])
        out[j] = total
        send(low, j, total)
    for copy in copies[2:]:
        copy.wait()


def first_update(right_sides, inverse, off, pairs, lower, upper, ways):
    levels = right_sides.shape[0]
    shape = right_sides.shape[1:]
    return pl.pallas_call(
        functools.partial(first_kernel, levels - 1, tuple(pairs)),
        out_shape=[
            jax.ShapeDtypeStruct(shape, jnp.float32),
            jax.ShapeDtypeStruct((2 * ways,) + shape[1:], jnp.bfloat16),
            pltpu.VMEM(right_sides.shape, right_sides.dtype),
            pltpu.VMEM(inverse.shape, inverse.dtype),
            pltpu.VMEM((len(pairs),) + off.shape[1:], off.dtype),
            pltpu.SMEM((4,) + lower.shape[1:], lower.dtype),
        ],
        in_specs=[HBM] * 5,
        out_specs=[VMEM] * 5 + [SMEM],
        scratch_shapes=[pltpu.SemaphoreType.DMA((4 + len(pairs),))],
        compiler_params=PARAMS,
    )(in_hbm(right_sides), in_hbm(inverse), in_hbm(off), in_hbm(lower), in_hbm(upper))


def last_kernel(plan, level, me, table, off, base, *refs):
    refs = list(refs)
    near = [[refs.pop(0) for _ in range(BUFFERS[entry[0]])] for entry in plan]
    inverse = refs.pop(0)
    out, result, sems = refs[-3:]
    copies = [
        pltpu.make_async_copy(ref, out.at[at], sems.at[at]) for at, ref in enumerate(refs[:-3])
    ]
    for copy in copies:
        copy.start()
    for j in range(2):
        total = coupled(base[j], j, plan, near, 1, me, table, off)
        result[j] = times(total, inverse[level, j])
    copies.append(pltpu.make_async_copy(result, out.at[level], sems.at[level]))
    copies[-1].start()
    for copy in copies:
        copy.wait()


def last_update(me, table, off, base, plan, near, inverse, solved):
    levels = len(solved) + 1
    arguments = [in_smem(me), in_smem(table), in_vmem(off), in_vmem(base)]
    for buffers in near:
        arguments += list(buffers)
    arguments += [in_vmem(inverse)] + [in_vmem(value) for value in solved]
    return pl.pallas_call(
        functools.partial(last_kernel, tuple(plan), levels - 1),
        out_shape=jax.ShapeDtypeStruct((levels,) + base.shape, jnp.float32),
        in_specs=[SMEM, SMEM] + [VMEM] * (len(arguments) - 2),
        out_specs=HBM,
        scratch_shapes=[
            pltpu.VMEM(base.shape, jnp.float32),
            pltpu.SemaphoreType.DMA((levels,)),
        ],
        compiler_params=PARAMS,
    )(*arguments)


def stage_kernel(count, *refs):
    sems = refs[-1]
    copies = []
    for at, (ref, kept) in enumerate(zip(refs[:count], refs[count:-1])):
        part = ref.at[pl.ds(0, kept.shape[0])]
        copies.append(pltpu.make_async_copy(part, kept, sems.at[at]))
    for copy in copies:
        copy.start()
    for copy in copies:
        copy.wait()


def staged(space, *arrays, counts=None):
    counts = counts or (None,) * len(arrays)
    shapes = [
        (count or array.shape[0],) + array.shape[1:] for array, count in zip(arrays, counts)
    ]
    return pl.pallas_call(
        functools.partial(stage_kernel, len(arrays)),
        out_shape=[space(shape, array.dtype) for array, shape in zip(arrays, shapes)],
        in_specs=[HBM] * len(arrays),
        out_specs=[VMEM if space is pltpu.VMEM else SMEM] * len(arrays),
        scratch_shapes=[pltpu.SemaphoreType.DMA((len(arrays),))],
        compiler_params=PARAMS,
        cost_estimate=pl.CostEstimate(
            flops=0,
            bytes_accessed=sum(array.size * array.dtype.itemsize for array in arrays),
            transcendentals=0,
        ),
    )(*arrays)


def pick_kernel(plan, side, me, table, *refs):
    out = refs[-1]
    for at, (peer, p, which) in enumerate(plan):
        peer = me[MINE] ^ peer if len(plan) == 4 else peer
        for j in range(2):
            for n in range(4):
                local = table[peer, 2 * side + j, n, p] & PLANE - 1
                out[at * 8 + j * 4 + n] = block(refs[2 * which], refs[2 * which + 1], local, me[CORE])


def pick(me, table, plan, side, *buffers):
    near = [half for pair_of in buffers for half in pair_of]
    shape = near[0].shape[1:]
    return pl.pallas_call(
        functools.partial(pick_kernel, tuple(plan), side),
        out_shape=jax.ShapeDtypeStruct((8 * len(plan),) + shape, jnp.bfloat16),
        in_specs=[SMEM, SMEM] + [VMEM] * len(near),
        out_specs=VMEM,
        compiler_params=PARAMS,
        cost_estimate=pl.CostEstimate(
            flops=0, bytes_accessed=len(plan) * 131072, transcendentals=0
        ),
    )(in_smem(me), in_smem(table), *near)


def halves(p, start=NONE):
    return ("halves", p, start, 0)


def on_device(
    right_sides, lower_inv, upper_inv, lower_off, upper_off, lower_pattern, upper_pattern
):
    sub, group = lax.axis_index("sub"), lax.axis_index("group")
    square, plane = (2, 4, 8), (2, 4, 8, 16)

    tables = [x.transpose(1, 2, 0) for x in (lower_pattern, upper_pattern)]
    mine = jnp.concatenate(tables)
    beside = swapped(mine, "group", 1)

    f5, sent, right, lower_inv, off_first, table = first_update(
        right_sides, lower_inv, lower_off, FIRST, *tables, 8
    )
    (me,) = staged(pltpu.SMEM, after(positions(sub, group), sent))
    near5, beside, me = lax.optimization_barrier((spread(sent, (1, 2, 4)), beside, me))
    near5 = (near5,)
    both = jnp.stack([mine, beside])
    across = swapped(both, "group", 2)
    low_first = functools.partial(update, me, table, off_first, side=0)

    f4, sent = low_first(
        right, 4, [("one", 14, NONE, 0)], [near5], level=4, inverse=[lower_inv], ways=8
    )
    near4 = collected(sent, square)
    (r3,) = low_first(after(right, near4[0]), 3, [("one", 13, NONE, 0)], [near5])
    f3, sent = low_first(r3, None, [halves(9)], [near4], level=3, inverse=[lower_inv], ways=16)
    near3, across = lax.optimization_barrier((spread(sent, plane), across))
    near3 = (near3, swapped(near3, "sub", 1))
    (peers,) = staged(pltpu.SMEM, jnp.concatenate([both, across]))
    (r2,) = low_first(
        after(right, near3[0]), 2, [("one", 12, NONE, 0), halves(8)], [near5, near4]
    )
    near3 = (near3[0], after(near3[1], peers))
    f2, sent = low_first(r2, None, [halves(5)], [near3], level=2, inverse=[lower_inv], ways=16)
    near2 = collected(sent, plane)
    far2 = swapped(pick(me, peers, [(1, 2, 0), (1, 1, 0)], 0, near2), "group", 1)
    lower_off, upper_inv, upper_first = staged(
        pltpu.VMEM,
        in_hbm(after(lower_off, near2[1])),
        in_hbm(after(upper_inv, near2[1])),
        in_hbm(after(upper_off, near2[1])),
        counts=(None, None, 1),
    )
    low = functools.partial(update, me, table, lower_off, side=0)
    (r1,) = low(
        after(right, near2[1]),
        1,
        [("one", 11, NONE, 0), halves(7), halves(4)],
        [near5, near4, near3],
    )
    far2, r1, upper_first = lax.optimization_barrier((far2, r1, upper_first))
    near2 = near2 + (far2,)
    f1, sent = low(
        r1, None, [("far", 2, NONE, 0)], [near2], level=1, inverse=[lower_inv], ways=16
    )
    near1 = collected(sent, plane)
    (r0,) = low(
        after(right, near1[0]),
        0,
        [("one", 10, NONE, 0), halves(6), halves(3), ("far", 1, NONE, 8)],
        [near5, near4, near3, near2],
    )
    near1 = (near1[0], after(near1[1], r0))
    asked = planes(pick(me, peers, [(at, 0, 0) for at in range(4)], 0, near1))
    s0, sent = low(
        r0,
        None,
        [("planes", 0, NONE, 0)],
        [(asked,)],
        level=0,
        inverse=[lower_inv, upper_inv],
        ways=16,
    )

    near0 = collected(sent, plane)
    asked = planes(pick(me, peers, [(at, 0, 0) for at in range(4)], 1, near0))
    s1, sent = update(
        me, table, upper_first, f1, None, [("planes", 0, NONE, 0)], [(asked,)], 1, 1, [upper_inv], 16
    )
    near1 = collected(sent, plane)
    far = swapped(pick(me, peers, [(1, 1, 0), (1, 2, 1)], 1, near0, near1), "group", 1)
    (upper_off,) = staged(pltpu.VMEM, in_hbm(after(upper_off, near1[1])))
    up = functools.partial(update, me, table, upper_off, side=1)
    (r3,) = up(after(f3, near1[1]), None, [halves(3), halves(4)], [near0, near1])
    (r4,) = up(after(f4, near1[1]), None, [halves(6, START16), halves(7, START16)], [near0, near1])
    (r5,) = up(after(f5, near1[1]), None, [halves(10, START8), halves(11, START8)], [near0, near1])
    far, r3, r4, r5 = lax.optimization_barrier((far, r3, r4, r5))
    s2, sent = up(
        f2,
        None,
        [("far", 1, NONE, 0), ("far", 2, NONE, 8)],
        [near0 + (far,), near1 + (far,)],
        level=2,
        inverse=[upper_inv],
        ways=16,
    )
    near2 = collected(sent, plane)
    (r4,) = up(after(r4, near2[0]), None, [halves(8, START16)], [(near2[0], near2[1])])
    s3, sent = up(r3, None, [halves(5)], [near2], level=3, inverse=[upper_inv], ways=8)
    near3 = collected(sent, square)
    (r5,) = up(after(r5, near3[0]), None, [halves(12, START8)], [near2])
    near3 = (near3[0], after(near3[1], r5))
    s4, sent = up(r4, None, [halves(9)], [near3], level=4, inverse=[upper_inv], ways=8)
    near4 = (spread(sent, (1, 2, 4)),)
    return last_update(
        me,
        table,
        upper_off,
        r5,
        [halves(13, START8IN16), ("one", 14, NONE, 0)],
        [near3, near4],
        upper_inv,
        [s0, s1, s2, s3, s4],
    )


def solution(mesh):
    return jax.shard_map(
        on_device,
        mesh=mesh,
        in_specs=(
            P(None, ("group", "sub"), None, None),
            P(None, ("group", "sub"), None, None),
            P(None, ("group", "sub"), None, None),
            P(None, ("group", "sub"), None, None, None),
            P(None, ("group", "sub"), None, None, None),
            P(None, ("group", "sub"), None),
            P(None, ("group", "sub"), None),
        ),
        out_specs=P(None, ("group", "sub"), None, None),
        check_vma=False,
    )
```

time: 366 us -> 171 us (0.47)
  waiting for transfers between devices: 217 us -> 17.7 us
  blocking collectives: 0 us -> 98.6 us
  starting transfers between devices: 92.6 us -> 37.7 us
  local copies, waits for them, and re-layouts: 23.9 us -> 0.09 us
  matrix products: 21.3 us -> 0 us
  Pallas kernels: 0 us -> 16.4 us
  other arithmetic: 6.8 us -> 0.02 us
    ppermute x50 -> x12, waiting for transfers between devices: 217 us -> 11.7 us  [swapped(): lax.ppermute(block, axis, [(i, i ^ mask) for i in range(lax.axis_size(axi...]
    all_to_all x0 -> x10, blocking collectives: none -> 98.6 us  [the longest x8 76.9 us: spread(): lax.all_to_all(copies, 'sub', 0, 0, tiled=True, axis_index_groups=span(ma...]
    ppermute x50 -> x12, starting transfers between devices: 92.6 us -> 26.8 us  [swapped(): lax.ppermute(block, axis, [(i, i ^ mask) for i in range(lax.axis_size(axi...]
    dot_general x20 -> x0, matrix products: 21.3 us -> none  [the longest x11 12.9 us: apply_inverse(): jnp.einsum('jrb,jbc->jrc', residual.astype(jnp.bfloat16), inverse, prefer...]
    gather x19 -> x0, local copies, waits for them, and re-layouts: 21.2 us -> none  [the longest x4 11.4 us: on_device(): upper_off[pair_list]]
    pallas_call x0 -> x28, Pallas kernels: none -> 16.4 us  [the longest x18 6.52 us: update(): pl.pallas_call(functools.partial(update_kernel, tuple(plan), side, first,...]
    all_to_all x0 -> x2, starting transfers between devices: none -> 10.9 us  [spread(): lax.all_to_all(copies, 'sub', 0, 0, tiled=True, axis_index_groups=span(ma...]
    all_to_all x0 -> x2, waiting for transfers between devices: none -> 6.02 us  [spread(): lax.all_to_all(copies, 'sub', 0, 0, tiled=True, axis_index_groups=span(ma...]
  transfers between devices with their start and end apart: 50 -> 14, of which waited for: 48 -> 13; matrix products, arithmetic and copies ran while one was open for 5% -> 0% of each run, Pallas kernels for 0% -> 5%
where the time goes in v2:
time: 171 us
  blocking collectives  98.6 us (58%)
  starting transfers between devices  37.7 us (22%)
  waiting for transfers between devices  17.7 us (10%)
  Pallas kernels  16.4 us (10%)
    all_to_all x8, blocking collectives, spread(): lax.all_to_all(copies, 'sub', 0, 0, tiled=True, axis_index_groups=span(ma...  76.9 us
    ppermute x12, starting transfers between devices, swapped(): lax.ppermute(block, axis, [(i, i ^ mask) for i in range(lax.axis_size(axi...  26.8 us
    all_to_all x2, blocking collectives, planes(): lax.all_to_all(copies, 'group', 0, 0, tiled=True, axis_index_groups=half)  21.7 us
    ppermute x12, waiting for transfers between devices, swapped(): lax.ppermute(block, axis, [(i, i ^ mask) for i in range(lax.axis_size(axi...  11.7 us
    all_to_all x2, starting transfers between devices, spread(): lax.all_to_all(copies, 'sub', 0, 0, tiled=True, axis_index_groups=span(ma...  10.9 us
    pallas_call x18, Pallas kernels, update(): pl.pallas_call(functools.partial(update_kernel, tuple(plan), side, first,...  6.52 us
    pallas_call x4, Pallas kernels, staged(): pl.pallas_call(functools.partial(stage_kernel, len(arrays)), out_shape=[s...  6.03 us
    all_to_all x2, waiting for transfers between devices, spread(): lax.all_to_all(copies, 'sub', 0, 0, tiled=True, axis_index_groups=span(ma...  6.02 us
  transfers between devices with their start and end apart: 14, of which 13 were waited for; matrix products, arithmetic and copies ran while one was open for 0% of the time, Pallas kernels for 5%

profile of v2, /device:TPU:1, one launch (start us, length us, event | category | flops | bytes accessed | tf_op | source)
XLA Modules:
  0.0 170.8 jit_solution(3045184546656028059)
XLA Ops:
  0.0 2.3 %shard_map.73 = (f32[2,32,128]{2,1,0:T(8,128)S(1)}, bf16[16,32,128]{2,1,0:T(8,128)(2,1)}, f32[6,2,32,128]{3,2,1,0:T(8,128)S(1)}, bf16[6,2,128,128]{3,2,1,0:T(8,1...) custom-call(f32[6,2,32,128]{3,2,1,0:T(8,128)} %refs_0_.1, ...), custom_call_target="tpu_custom_call" | custom-call | tf_op jit(solution)/shard_map/pallas_call | solution.py:184
  2.3 6.5 %all-to-all-start = ((bf16[16,32,128]{2,1,0:T(8,128)(2,1)}), bf16[16,32,128]{2,1,0:T(8,128)(2,1)S(1)}, u32[]{:S(2)}, u32[]{:S(2)}) async-start(bf16[16,32,128]{2,1,0:T(8,128)(2,1)} %get-tuple-element.61), calls=%async_computation | async-start | bytes 262144 | tf_op jit(solution)/shard_map/all_to_all | solution.py:36
  8.9 1.2 collective-permute-start
  11.5 2.7 %all-to-all-done.refs_0_ = bf16[16,32,128]{2,1,0:T(8,128)(2,1)S(1)} async-done(((bf16[16,32,128]{2,1,0:T(8,128)(2,1)}), bf16[16,32,128]{2,1,0:T(8,128)(2,1)S(1)}, u32[]{:S(2)}, u32[]{:S(2)}) %all-to-all-start) | async-done | bytes 131104 | tf_op jit(solution)/shard_map/all_to_all | solution.py:36
  14.6 7.8 %all_to_all.60.refs_0_.refs_1_ = bf16[16,32,128]{2,1,0:T(8,128)(2,1)S(1)} all-to-all(bf16[16,32,128]{2,1,0:T(8,128)(2,1)S(1)} %get-tuple-element.70), channel_id=1, replica_groups={{0,2,4,6,8,10,12,14},{1,3,5,7,9,11,13,15},{16,18,20,22,24,26,28,30},{17..., dimensions={0} | all-to-all | bytes 262144 | tf_op jit(solution)/shard_map/all_to_all | solution.py:36
  22.4 2.2 %collective-permute-start.1 = (bf16[16,32,128]{2,1,0:T(8,128)(2,1)S(1)}, bf16[16,32,128]{2,1,0:T(8,128)(2,1)S(1)}, u32[]{:S(2)}, u32[]{:S(2)}) collective-permute-start(bf16[16,32,128]{2,1,0:T(8,128)(2,1)S(1)} %all_to_all.60.refs_0_.refs_1_), channel_id=1, source_target_pairs={{0,1},{1,0},{2,3},{3,2},{4,5},{5,4},{6,7},{7,6},{8,9},{9,8},{10,11... | collective-permute-start | bytes 393224 | tf_op jit(solution)/shard_map/ppermute | solution.py:32
  26.7 4.4 %all-to-all-start.2 = ((bf16[32,32,128]{2,1,0:T(8,128)(2,1)}), bf16[32,32,128]{2,1,0:T(8,128)(2,1)S(1)}, u32[]{:S(2)}, u32[]{:S(2)}) async-start(bf16[32,32,128]{2,1,0:T(8,128)(2,1)} %get-tuple-element.72), calls=%async_computation.2 | async-start | bytes 524288 | tf_op jit(solution)/shard_map/all_to_all | solution.py:36
  31.1 3.1 %collective-permute-start.2 = (s32[2,4,4,15]{3,2,1,0:T(4,128)S(1)}, s32[2,4,4,15]{3,2,1,0:T(4,128)S(1)}, u32[]{:S(2)}, u32[]{:S(2)}) collective-permute-start(s32[2,4,4,15]{3,2,1,0:T(4,128)S(1)} %pad_add_fusion.1), channel_id=1, source_target_pairs={{0,64},{32,96},{64,0},{96,32},{128,192},{160,224},{192,128},{224,1... | collective-permute-start | bytes 5768 | tf_op jit(solution)/shard_map/ppermute | solution.py:32
  35.3 3.3 %all-to-all-done.2.refs_0_.refs_3_ = bf16[32,32,128]{2,1,0:T(8,128)(2,1)S(1)} async-done(((bf16[32,32,128]{2,1,0:T(8,128)(2,1)}), bf16[32,32,128]{2,1,0:T(8,128)(2,1)S(1)}, u32[]{:S(2)}, u32[]{:S(2)}) %all-to-all-start.2) | async-done | bytes 262176 | tf_op jit(solution)/shard_map/all_to_all | solution.py:36
  38.7 1.9 %collective-permute-start.3 = (bf16[32,32,128]{2,1,0:T(8,128)(2,1)S(1)}, bf16[32,32,128]{2,1,0:T(8,128)(2,1)S(1)}, u32[]{:S(2)}, u32[]{:S(2)}) collective-permute-start(bf16[32,32,128]{2,1,0:T(8,128)(2,1)S(1)} %all-to-all-done.2.refs_0_.refs_3_), channel_id=1, source_target_pairs={{0,1},{1,0},{2,3},{3,2},{4,5},{5,4},{6,7},{7,6},{8,9},{9,8},{10,11... | collective-permute-start | bytes 786440 | tf_op jit(solution)/shard_map/ppermute | solution.py:32
  42.3 10.9 %all_to_all.61.refs_0_.refs_5_ = bf16[32,32,128]{2,1,0:T(8,128)(2,1)S(1)} all-to-all(bf16[32,32,128]{2,1,0:T(8,128)(2,1)S(1)} %get-tuple-element.77), channel_id=1, replica_groups={{0,2,4,6,8,10,12,14,16,18,20,22,24,26,28,30},{1,3,5,7,9,11,13,15,17,19,..., dimensions={0} | all-to-all | bytes 524288 | tf_op jit(solution)/shard_map/all_to_all | solution.py:36
  53.2 1.7 %collective-permute-start.4 = (bf16[32,32,128]{2,1,0:T(8,128)(2,1)S(1)}, bf16[32,32,128]{2,1,0:T(8,128)(2,1)S(1)}, u32[]{:S(2)}, u32[]{:S(2)}) collective-permute-start(bf16[32,32,128]{2,1,0:T(8,128)(2,1)S(1)} %all_to_all.61.refs_0_.refs_5_), channel_id=1, source_target_pairs={{0,1},{1,0},{2,3},{3,2},{4,5},{5,4},{6,7},{7,6},{8,9},{9,8},{10,11... | collective-permute-start | bytes 786440 | tf_op jit(solution)/shard_map/ppermute | solution.py:32
  54.9 1.2 collective-permute-done.4.refs_1_.refs_6_
  56.2 1.7 %collective-permute-start.5 = (bf16[16,32,128]{2,1,0:T(8,128)(2,1)S(1)}, bf16[16,32,128]{2,1,0:T(8,128)(2,1)S(1)}, u32[]{:S(2)}, u32[]{:S(2)}) collective-permute-start(bf16[16,32,128]{2,1,0:T(8,128)(2,1)S(1)} %shard_map.81), channel_id=1, source_target_pairs={{0,32},{32,0},{64,96},{96,64},{128,160},{160,128},{192,224},{224,1... | collective-permute-start | bytes 393224 | tf_op jit(solution)/shard_map/ppermute | solution.py:32
  57.9 2.3 %shard_map.82 = (bf16[15,2,4,128,128]{4,3,2,1,0:T(8,128)(2,1)S(1)}, bf16[6,2,128,128]{3,2,1,0:T(8,128)(2,1)S(1)}, bf16[1,2,4,128,128]{4,3,2,1,0:T(8,128)(2,1)S(1)}) custom-call(bf16[15,2,4,128,128]{4,3,2,1,0:T(8,128)(2,1)} %refs_0_.2, bf16[6,2,128,128]{3,2,1,0:T(8,128)(2,1)} %refs_1_.2, bf16[15,2,4,128,128]{4,3,2,1,0:T(8,128)(2,1)} %refs_0_.3), custom_call_target="tpu_custom_call" | custom-call | bytes 8257536 | tf_op jit(solution)/shard_map/pallas_call | solution.py:256
  61.8 10.6 %all_to_all.62.refs_0_ = bf16[32,32,128]{2,1,0:T(8,128)(2,1)S(1)} all-to-all(bf16[32,32,128]{2,1,0:T(8,128)(2,1)S(1)} %get-tuple-element.88), channel_id=1, replica_groups={{0,2,4,6,8,10,12,14,16,18,20,22,24,26,28,30},{1,3,5,7,9,11,13,15,17,19,..., dimensions={0} | all-to-all | bytes 524288 | tf_op jit(solution)/shard_map/all_to_all | solution.py:36
  72.4 2.3 %collective-permute-start.6 = (bf16[32,32,128]{2,1,0:T(8,128)(2,1)S(1)}, bf16[32,32,128]{2,1,0:T(8,128)(2,1)S(1)}, u32[]{:S(2)}, u32[]{:S(2)}) collective-permute-start(bf16[32,32,128]{2,1,0:T(8,128)(2,1)S(1)} %all_to_all.62.refs_0_), channel_id=1, source_target_pairs={{0,1},{1,0},{2,3},{3,2},{4,5},{5,4},{6,7},{7,6},{8,9},{9,8},{10,11... | collective-permute-start | bytes 786440 | tf_op jit(solution)/shard_map/ppermute | solution.py:32
  76.0 12.3 %all_to_all.63.refs_0_ = bf16[32,32,128]{2,1,0:T(8,128)(2,1)S(1)} all-to-all(bf16[32,32,128]{2,1,0:T(8,128)(2,1)S(1)} %shard_map.86), channel_id=1, replica_groups={{0,32,64,96},{128,160,192,224},{1,33,65,97},{129,161,193,225},{2,34,66,..., dimensions={0} | all-to-all | bytes 524288 | tf_op jit(solution)/shard_map/all_to_all | solution.py:46
  88.9 10.5 %all_to_all.64.refs_0_ = bf16[32,32,128]{2,1,0:T(8,128)(2,1)S(1)} all-to-all(bf16[32,32,128]{2,1,0:T(8,128)(2,1)S(1)} %get-tuple-element.92), channel_id=1, replica_groups={{0,2,4,6,8,10,12,14,16,18,20,22,24,26,28,30},{1,3,5,7,9,11,13,15,17,19,..., dimensions={0} | all-to-all | bytes 524288 | tf_op jit(solution)/shard_map/all_to_all | solution.py:36
  99.4 4.2 %collective-permute-start.7 = (bf16[32,32,128]{2,1,0:T(8,128)(2,1)S(1)}, bf16[32,32,128]{2,1,0:T(8,128)(2,1)S(1)}, u32[]{:S(2)}, u32[]{:S(2)}) collective-permute-start(bf16[32,32,128]{2,1,0:T(8,128)(2,1)S(1)} %all_to_all.64.refs_0_), channel_id=1, source_target_pairs={{0,1},{1,0},{2,3},{3,2},{4,5},{5,4},{6,7},{7,6},{8,9},{9,8},{10,11... | collective-permute-start | bytes 786440 | tf_op jit(solution)/shard_map/ppermute | solution.py:32
  103.6 1.2 collective-permute-done.7.refs_1_
  104.9 9.4 %all_to_all.65.refs_0_ = bf16[32,32,128]{2,1,0:T(8,128)(2,1)S(1)} all-to-all(bf16[32,32,128]{2,1,0:T(8,128)(2,1)S(1)} %shard_map.88), channel_id=1, replica_groups={{0,32,64,96},{128,160,192,224},{1,33,65,97},{129,161,193,225},{2,34,66,..., dimensions={0} | all-to-all | bytes 524288 | tf_op jit(solution)/shard_map/all_to_all | solution.py:46
  114.8 10.6 %all_to_all.66.refs_2_.refs_3_ = bf16[32,32,128]{2,1,0:T(8,128)(2,1)S(1)} all-to-all(bf16[32,32,128]{2,1,0:T(8,128)(2,1)S(1)} %get-tuple-element.93), channel_id=1, replica_groups={{0,2,4,6,8,10,12,14,16,18,20,22,24,26,28,30},{1,3,5,7,9,11,13,15,17,19,..., dimensions={0} | all-to-all | bytes 524288 | tf_op jit(solution)/shard_map/all_to_all | solution.py:36
  125.3 4.2 %collective-permute-start.8 = (bf16[32,32,128]{2,1,0:T(8,128)(2,1)S(1)}, bf16[32,32,128]{2,1,0:T(8,128)(2,1)S(1)}, u32[]{:S(2)}, u32[]{:S(2)}) collective-permute-start(bf16[32,32,128]{2,1,0:T(8,128)(2,1)S(1)} %all_to_all.66.refs_2_.refs_3_), channel_id=1, source_target_pairs={{0,1},{1,0},{2,3},{3,2},{4,5},{5,4},{6,7},{7,6},{8,9},{9,8},{10,11... | collective-permute-start | bytes 786440 | tf_op jit(solution)/shard_map/ppermute | solution.py:32
  129.5 1.2 collective-permute-done.8.refs_3_.refs_4_
  130.8 2.1 %shard_map.90.off = bf16[15,2,4,128,128]{4,3,2,1,0:T(8,128)(2,1)S(1)} custom-call(bf16[15,2,4,128,128]{4,3,2,1,0:T(8,128)(2,1)} %refs_0_.3), custom_call_target="tpu_custom_call" | custom-call | bytes 3932160 | tf_op jit(solution)/shard_map/pallas_call | solution.py:256
  133.6 1.9 %collective-permute-done.9.refs_2_.refs_5_ = bf16[16,32,128]{2,1,0:T(8,128)(2,1)S(1)} collective-permute-done((bf16[16,32,128]{2,1,0:T(8,128)(2,1)S(1)}, bf16[16,32,128]{2,1,0:T(8,128)(2,1)S(1)}, u32[]{:S(2)}, u32[]{:S(2)}) %collective-permute-start.9) | collective-permute-done | bytes 131104 | tf_op jit(solution)/shard_map/ppermute | solution.py:32
  136.0 10.5 %all_to_all.67.refs_0_ = bf16[32,32,128]{2,1,0:T(8,128)(2,1)S(1)} all-to-all(bf16[32,32,128]{2,1,0:T(8,128)(2,1)S(1)} %get-tuple-element.105), channel_id=1, replica_groups={{0,2,4,6,8,10,12,14,16,18,20,22,24,26,28,30},{1,3,5,7,9,11,13,15,17,19,..., dimensions={0} | all-to-all | bytes 524288 | tf_op jit(solution)/shard_map/all_to_all | solution.py:36
  146.5 2.7 %collective-permute-start.10 = (bf16[32,32,128]{2,1,0:T(8,128)(2,1)S(1)}, bf16[32,32,128]{2,1,0:T(8,128)(2,1)S(1)}, u32[]{:S(2)}, u32[]{:S(2)}) collective-permute-start(bf16[32,32,128]{2,1,0:T(8,128)(2,1)S(1)} %all_to_all.67.refs_0_), channel_id=1, source_target_pairs={{0,1},{1,0},{2,3},{3,2},{4,5},{5,4},{6,7},{7,6},{8,9},{9,8},{10,11... | collective-permute-start | bytes 786440 | tf_op jit(solution)/shard_map/ppermute | solution.py:32
  150.8 8.0 %all_to_all.68.refs_0_ = bf16[16,32,128]{2,1,0:T(8,128)(2,1)S(1)} all-to-all(bf16[16,32,128]{2,1,0:T(8,128)(2,1)S(1)} %get-tuple-element.106), channel_id=1, replica_groups={{0,2,4,6,8,10,12,14},{1,3,5,7,9,11,13,15},{16,18,20,22,24,26,28,30},{17..., dimensions={0} | all-to-all | bytes 262144 | tf_op jit(solution)/shard_map/all_to_all | solution.py:36
  158.8 1.5 collective-permute-start.11
  161.6 8.0 %all_to_all.69.refs_2_ = bf16[16,32,128]{2,1,0:T(8,128)(2,1)S(1)} all-to-all(bf16[16,32,128]{2,1,0:T(8,128)(2,1)S(1)} %get-tuple-element.111), channel_id=1, replica_groups={{0,1,2,3,4,5,6,7},{8,9,10,11,12,13,14,15},{16,17,18,19,20,21,22,23},{24..., dimensions={0} | all-to-all | bytes 262144 | tf_op jit(solution)/shard_map/all_to_all | solution.py:36
  (42 shorter events, 16.2 us)
Async XLA Ops:
  0.0 8.9 %copy-start.1 = (s32[15,2,4]{0,2,1:T(4,128)S(1)}, s32[15,2,4]{0,2,1:T(4,128)}, u32[]{:S(2)}) copy-start(s32[15,2,4]{0,2,1:T(4,128)} %param.13) | copy-start | bytes 1444
  0.0 8.9 %copy-start = (s32[15,2,4]{0,2,1:T(4,128)S(1)}, s32[15,2,4]{0,2,1:T(4,128)}, u32[]{:S(2)}) copy-start(s32[15,2,4]{0,2,1:T(4,128)} %param.12) | copy-start | bytes 1444
  2.3 11.8 %all-to-all-start = ((bf16[16,32,128]{2,1,0:T(8,128)(2,1)}), bf16[16,32,128]{2,1,0:T(8,128)(2,1)S(1)}, u32[]{:S(2)}, u32[]{:S(2)}) async-start(bf16[16,32,128]{2,1,0:T(8,128)(2,1)} %get-tuple-element.61), calls=%async_computation | async-start | bytes 262144 | tf_op jit(solution)/shard_map/all_to_all | solution.py:36
  8.9 2.6 %collective-permute-start = (s32[4,4,15]{2,1,0:T(4,128)S(1)}, s32[4,4,15]{2,1,0:T(4,128)S(1)}, u32[]{:S(2)}, u32[]{:S(2)}) collective-permute-start(s32[4,4,15]{2,1,0:T(4,128)S(1)} %get-tuple-element.118), channel_id=1, source_target_pairs={{0,32},{32,0},{64,96},{96,64},{128,160},{160,128},{192,224},{224,1... | collective-permute-start | bytes 2888 | tf_op jit(solution)/shard_map/ppermute | solution.py:32
  22.4 3.2 %collective-permute-start.1 = (bf16[16,32,128]{2,1,0:T(8,128)(2,1)S(1)}, bf16[16,32,128]{2,1,0:T(8,128)(2,1)S(1)}, u32[]{:S(2)}, u32[]{:S(2)}) collective-permute-start(bf16[16,32,128]{2,1,0:T(8,128)(2,1)S(1)} %all_to_all.60.refs_0_.refs_1_), channel_id=1, source_target_pairs={{0,1},{1,0},{2,3},{3,2},{4,5},{5,4},{6,7},{7,6},{8,9},{9,8},{10,11... | collective-permute-start | bytes 393224 | tf_op jit(solution)/shard_map/ppermute | solution.py:32
  26.7 11.9 %all-to-all-start.2 = ((bf16[32,32,128]{2,1,0:T(8,128)(2,1)}), bf16[32,32,128]{2,1,0:T(8,128)(2,1)S(1)}, u32[]{:S(2)}, u32[]{:S(2)}) async-start(bf16[32,32,128]{2,1,0:T(8,128)(2,1)} %get-tuple-element.72), calls=%async_computation.2 | async-start | bytes 524288 | tf_op jit(solution)/shard_map/all_to_all | solution.py:36
  31.1 4.2 %collective-permute-start.2 = (s32[2,4,4,15]{3,2,1,0:T(4,128)S(1)}, s32[2,4,4,15]{3,2,1,0:T(4,128)S(1)}, u32[]{:S(2)}, u32[]{:S(2)}) collective-permute-start(s32[2,4,4,15]{3,2,1,0:T(4,128)S(1)} %pad_add_fusion.1), channel_id=1, source_target_pairs={{0,64},{32,96},{64,0},{96,32},{128,192},{160,224},{192,128},{224,1... | collective-permute-start | bytes 5768 | tf_op jit(solution)/shard_map/ppermute | solution.py:32
  38.7 3.2 %collective-permute-start.3 = (bf16[32,32,128]{2,1,0:T(8,128)(2,1)S(1)}, bf16[32,32,128]{2,1,0:T(8,128)(2,1)S(1)}, u32[]{:S(2)}, u32[]{:S(2)}) collective-permute-start(bf16[32,32,128]{2,1,0:T(8,128)(2,1)S(1)} %all-to-all-done.2.refs_0_.refs_3_), channel_id=1, source_target_pairs={{0,1},{1,0},{2,3},{3,2},{4,5},{5,4},{6,7},{7,6},{8,9},{9,8},{10,11... | collective-permute-start | bytes 786440 | tf_op jit(solution)/shard_map/ppermute | solution.py:32
  53.2 2.9 %collective-permute-start.4 = (bf16[32,32,128]{2,1,0:T(8,128)(2,1)S(1)}, bf16[32,32,128]{2,1,0:T(8,128)(2,1)S(1)}, u32[]{:S(2)}, u32[]{:S(2)}) collective-permute-start(bf16[32,32,128]{2,1,0:T(8,128)(2,1)S(1)} %all_to_all.61.refs_0_.refs_5_), channel_id=1, source_target_pairs={{0,1},{1,0},{2,3},{3,2},{4,5},{5,4},{6,7},{7,6},{8,9},{9,8},{10,11... | collective-permute-start | bytes 786440 | tf_op jit(solution)/shard_map/ppermute | solution.py:32
  56.2 5.2 %collective-permute-start.5 = (bf16[16,32,128]{2,1,0:T(8,128)(2,1)S(1)}, bf16[16,32,128]{2,1,0:T(8,128)(2,1)S(1)}, u32[]{:S(2)}, u32[]{:S(2)}) collective-permute-start(bf16[16,32,128]{2,1,0:T(8,128)(2,1)S(1)} %shard_map.81), channel_id=1, source_target_pairs={{0,32},{32,0},{64,96},{96,64},{128,160},{160,128},{192,224},{224,1... | collective-permute-start | bytes 393224 | tf_op jit(solution)/shard_map/ppermute | solution.py:32
  72.4 3.5 %collective-permute-start.6 = (bf16[32,32,128]{2,1,0:T(8,128)(2,1)S(1)}, bf16[32,32,128]{2,1,0:T(8,128)(2,1)S(1)}, u32[]{:S(2)}, u32[]{:S(2)}) collective-permute-start(bf16[32,32,128]{2,1,0:T(8,128)(2,1)S(1)} %all_to_all.62.refs_0_), channel_id=1, source_target_pairs={{0,1},{1,0},{2,3},{3,2},{4,5},{5,4},{6,7},{7,6},{8,9},{9,8},{10,11... | collective-permute-start | bytes 786440 | tf_op jit(solution)/shard_map/ppermute | solution.py:32
  99.4 5.4 %collective-permute-start.7 = (bf16[32,32,128]{2,1,0:T(8,128)(2,1)S(1)}, bf16[32,32,128]{2,1,0:T(8,128)(2,1)S(1)}, u32[]{:S(2)}, u32[]{:S(2)}) collective-permute-start(bf16[32,32,128]{2,1,0:T(8,128)(2,1)S(1)} %all_to_all.64.refs_0_), channel_id=1, source_target_pairs={{0,1},{1,0},{2,3},{3,2},{4,5},{5,4},{6,7},{7,6},{8,9},{9,8},{10,11... | collective-permute-start | bytes 786440 | tf_op jit(solution)/shard_map/ppermute | solution.py:32
  125.3 5.4 %collective-permute-start.8 = (bf16[32,32,128]{2,1,0:T(8,128)(2,1)S(1)}, bf16[32,32,128]{2,1,0:T(8,128)(2,1)S(1)}, u32[]{:S(2)}, u32[]{:S(2)}) collective-permute-start(bf16[32,32,128]{2,1,0:T(8,128)(2,1)S(1)} %all_to_all.66.refs_2_.refs_3_), channel_id=1, source_target_pairs={{0,1},{1,0},{2,3},{3,2},{4,5},{5,4},{6,7},{7,6},{8,9},{9,8},{10,11... | collective-permute-start | bytes 786440 | tf_op jit(solution)/shard_map/ppermute | solution.py:32
  130.7 4.8 %collective-permute-start.9 = (bf16[16,32,128]{2,1,0:T(8,128)(2,1)S(1)}, bf16[16,32,128]{2,1,0:T(8,128)(2,1)S(1)}, u32[]{:S(2)}, u32[]{:S(2)}) collective-permute-start(bf16[16,32,128]{2,1,0:T(8,128)(2,1)S(1)} %shard_map.91), channel_id=1, source_target_pairs={{0,32},{32,0},{64,96},{96,64},{128,160},{160,128},{192,224},{224,1... | collective-permute-start | bytes 393224 | tf_op jit(solution)/shard_map/ppermute | solution.py:32
  146.5 3.8 %collective-permute-start.10 = (bf16[32,32,128]{2,1,0:T(8,128)(2,1)S(1)}, bf16[32,32,128]{2,1,0:T(8,128)(2,1)S(1)}, u32[]{:S(2)}, u32[]{:S(2)}) collective-permute-start(bf16[32,32,128]{2,1,0:T(8,128)(2,1)S(1)} %all_to_all.67.refs_0_), channel_id=1, source_target_pairs={{0,1},{1,0},{2,3},{3,2},{4,5},{5,4},{6,7},{7,6},{8,9},{9,8},{10,11... | collective-permute-start | bytes 786440 | tf_op jit(solution)/shard_map/ppermute | solution.py:32
  158.8 2.5 %collective-permute-start.11 = (bf16[16,32,128]{2,1,0:T(8,128)(2,1)S(1)}, bf16[16,32,128]{2,1,0:T(8,128)(2,1)S(1)}, u32[]{:S(2)}, u32[]{:S(2)}) collective-permute-start(bf16[16,32,128]{2,1,0:T(8,128)(2,1)S(1)} %all_to_all.68.refs_0_), channel_id=1, source_target_pairs={{0,1},{1,0},{2,3},{3,2},{4,5},{5,4},{6,7},{7,6},{8,9},{9,8},{10,11... | collective-permute-start | bytes 393224 | tf_op jit(solution)/shard_map/ppermute | solution.py:32

commit v3 on v2

v3 whole, which is shorter than its diff:
```python
import functools

import jax
import jax.numpy as jnp
from jax import lax
from jax.experimental import pallas as pl
from jax.experimental.pallas import tpu as pltpu
from jax.sharding import PartitionSpec as P

DUO_BITS = 7
DUO_BLOCKS = 1 << DUO_BITS
VMEM = pl.BlockSpec(memory_space=pltpu.VMEM)
SMEM = pl.BlockSpec(memory_space=pltpu.SMEM)
HBM = pl.BlockSpec(memory_space=pl.ANY)
PARAMS = pltpu.CompilerParams(vmem_limit_bytes=8 * 2**20)


def span(masks, count):
    groups, seen = [], set()
    for first in range(count):
        if first not in seen:
            group = [first]
            for mask in masks:
                group = group + [member ^ mask for member in group]
            seen.update(group)
            groups.append(sorted(group))
    return groups


def swapped(block, axis, mask):
    return lax.ppermute(block, axis, [(i, i ^ mask) for i in range(lax.axis_size(axis))])


def spread(copies, masks):
    axes = ("group", "sub")
    groups = span(masks, lax.axis_size("group") * lax.axis_size("sub"))
    return lax.all_to_all(copies, axes, 0, 0, tiled=True, axis_index_groups=groups)


def collected(copies, masks):
    own = spread(copies, masks)
    return own, swapped(own, "sub", 1)


def after(value, *others):
    return lax.optimization_barrier((value,) + others)[0]


def in_vmem(value):
    return pltpu.with_memory_space_constraint(value, pltpu.VMEM)


def in_smem(value):
    return pltpu.with_memory_space_constraint(value, pltpu.SMEM)


def in_hbm(value):
    return pltpu.with_memory_space_constraint(value, pltpu.HBM)


(CORE, DUO, PLANE64, SIXTEEN64, EIGHT64, SIXTEEN32, EIGHT32, EIGHT16, NONE) = range(9)
ACROSS, MATE, MATE_ACROSS = range(3)


def positions(sub, group):
    sixteen, eight = (sub >> 4) * 32, (sub >> 3) * 16
    plane = (group & 1) * 64
    return jnp.stack(
        [
            sub & 1,
            (group >> 1) & 1,
            plane,
            plane + sixteen,
            plane + eight,
            sixteen,
            eight,
            (sub >> 3 & 1) * 16,
        ]
    )


def block(own, other, local, core):
    index = (local >> 2 << 1) | (local & 1)
    return jnp.where((local >> 1 & 1) == core, own[index], other[index])


def read(kind, start, refs, me, wanted, slot):
    if kind == "one":
        return refs[0][wanted]
    if kind == "halves":
        local = wanted if start == NONE else wanted + me[start]
        return block(refs[0], refs[1], local, me[CORE])
    near = mixed(refs[0], refs[1], wanted & DUO_BLOCKS - 1, me[CORE], start + slot)
    if kind == "core":
        return near
    return jnp.where(wanted >> DUO_BITS == me[DUO], near, refs[2][slot])


def mixed(own, sent, local, core, slot):
    index = (local >> 2 << 1) | (local & 1)
    return jnp.where((local >> 1 & 1) == core, own[index], sent[slot])


def send(ref, j, value):
    value = value.astype(jnp.bfloat16)
    for way in range(ref.shape[0] // 2):
        ref[2 * way + j] = value


FIRST = (14, 13, 9, 12, 8, 5)
SECOND = (11, 7, 4, 2)
BUFFERS = {"one": 1, "halves": 2, "core": 2, "far": 3}


def coupled(total, j, plan, near, side, kept, me, table, off):
    for (kind, p, start), buffers in zip(plan, near):
        at = kept.index(p) if kept else p
        matrices = off[at, j].reshape(512, 128)
        picked = [
            read(kind, start, buffers, me, table[2 * side + j, n, p], j * 4 + n)
            for n in range(4)
        ]
        total = total - jnp.dot(
            jnp.concatenate(picked, 1), matrices, preferred_element_type=jnp.float32
        )
    return total


def times(total, matrix):
    return jnp.dot(total.astype(jnp.bfloat16), matrix, preferred_element_type=jnp.float32)


def update_kernel(plan, side, kept, first, level, inverses, ways, me, table, off, base, *refs):
    refs = list(refs)
    near = [[refs.pop(0) for _ in range(BUFFERS[entry[0]])] for entry in plan]
    inverse = [refs.pop(0) for _ in range(inverses)]
    for j in range(2):
        total = base[first, j] if first is not None else base[j]
        total = coupled(total, j, plan, near, side, kept, me, table, off)
        if not inverses:
            refs[0][j] = total
        for matrix in inverse:
            total = times(total, matrix[level, j])
        if inverses:
            refs[0][j] = total
        if ways:
            send(refs[-1], j, total)


def update(me, table, off, base, first, plan, near, side, level=0, inverse=(), ways=0, kept=None):
    shape = (2,) + base.shape[-2:]
    shapes = [jax.ShapeDtypeStruct(shape, jnp.float32)]
    if ways:
        shapes.append(jax.ShapeDtypeStruct((2 * ways,) + shape[1:], jnp.bfloat16))
    arguments = [in_smem(me), in_smem(table), in_vmem(off), in_vmem(base)]
    for buffers in near:
        arguments += list(buffers)
    arguments += [in_vmem(matrix) for matrix in inverse]
    products = 2 * (4 * len(plan) + len(inverse))
    return pl.pallas_call(
        functools.partial(
            update_kernel, tuple(plan), side, kept, first, level, len(inverse), ways
        ),
        out_shape=shapes,
        in_specs=[SMEM, SMEM] + [VMEM] * (len(arguments) - 2),
        out_specs=[VMEM] * len(shapes),
        compiler_params=PARAMS,
        cost_estimate=pl.CostEstimate(
            flops=products * 2 * 32 * 128 * 128, bytes_accessed=products * 32768, transcendentals=0
        ),
    )(*arguments)


def first_kernel(level, base, matrix, out, low, right, inverse, sems):
    copies = [
        pltpu.make_async_copy(base.at[level], right, sems.at[0]),
        pltpu.make_async_copy(matrix.at[level], inverse, sems.at[1]),
    ]
    for copy in copies:
        copy.start()
    for copy in copies:
        copy.wait()
    for j in range(2):
        total = times(right[j], inverse[j])
        out[j] = total
        send(low, j, total)


def first_update(right_sides, inverse, ways):
    levels = right_sides.shape[0]
    shape, matrix = right_sides.shape[1:], inverse.shape[1:]
    return pl.pallas_call(
        functools.partial(first_kernel, levels - 1),
        out_shape=[
            jax.ShapeDtypeStruct(shape, jnp.float32),
            jax.ShapeDtypeStruct((2 * ways,) + shape[1:], jnp.bfloat16),
        ],
        in_specs=[HBM, HBM],
        out_specs=[VMEM, VMEM],
        scratch_shapes=[
            pltpu.VMEM(shape, jnp.float32),
            pltpu.VMEM(matrix, jnp.bfloat16),
            pltpu.SemaphoreType.DMA((2,)),
        ],
        compiler_params=PARAMS,
    )(in_hbm(right_sides), in_hbm(inverse))


def last_kernel(plan, level, me, table, off, base, *refs):
    refs = list(refs)
    near = [[refs.pop(0) for _ in range(BUFFERS[entry[0]])] for entry in plan]
    inverse = refs.pop(0)
    out, result, sems = refs[-3:]
    copies = [
        pltpu.make_async_copy(ref, out.at[at], sems.at[at]) for at, ref in enumerate(refs[:-3])
    ]
    for copy in copies:
        copy.start()
    for j in range(2):
        total = coupled(base[j], j, plan, near, 1, None, me, table, off)
        result[j] = times(total, inverse[level, j])
    copies.append(pltpu.make_async_copy(result, out.at[level], sems.at[level]))
    copies[-1].start()
    for copy in copies:
        copy.wait()


def last_update(me, table, off, base, plan, near, inverse, solved):
    levels = len(solved) + 1
    arguments = [in_smem(me), in_smem(table), in_vmem(off), in_vmem(base)]
    for buffers in near:
        arguments += list(buffers)
    arguments += [in_vmem(inverse)] + [in_vmem(value) for value in solved]
    return pl.pallas_call(
        functools.partial(last_kernel, tuple(plan), levels - 1),
        out_shape=jax.ShapeDtypeStruct((levels,) + base.shape, jnp.float32),
        in_specs=[SMEM, SMEM] + [VMEM] * (len(arguments) - 2),
        out_specs=HBM,
        scratch_shapes=[
            pltpu.VMEM(base.shape, jnp.float32),
            pltpu.SemaphoreType.DMA((levels,)),
        ],
        compiler_params=PARAMS,
    )(*arguments)


def stage_kernel(plan, count, *refs):
    outs, sems = refs[count:-1], refs[-1]
    copies = []
    for which, place, rows, out, at in plan:
        target = outs[out] if at is None else outs[out].at[pl.ds(at, len(rows) if rows else place)]
        for offset, row in enumerate(rows or (None,)):
            source = refs[which] if row is None else refs[which].at[row]
            if row is not None:
                target = outs[out].at[at + offset]
            copies.append(pltpu.make_async_copy(source, target, sems.at[len(copies)]))
    for copy in copies:
        copy.start()
    for copy in copies:
        copy.wait()


def staged(*items):
    arrays, shapes, specs, plan, copies = [], [], [], [], 0
    for out, (space, parts, rows) in enumerate(items):
        at = 0
        for part in parts:
            size = part.shape[0]
            whole = rows is None and len(parts) == 1
            plan.append((len(arrays), size, rows, out, None if whole else at))
            arrays.append(in_hbm(part))
            copies += len(rows) if rows else 1
            at += len(rows) if rows else size
        shapes.append(space((at,) + parts[0].shape[1:], parts[0].dtype))
        specs.append(VMEM if space is pltpu.VMEM else SMEM)
    moved = sum(shape.size if hasattr(shape, "size") else 0 for shape in shapes)
    return pl.pallas_call(
        functools.partial(stage_kernel, tuple(plan), len(arrays)),
        out_shape=shapes,
        in_specs=[HBM] * len(arrays),
        out_specs=specs,
        scratch_shapes=[pltpu.SemaphoreType.DMA((copies,))],
        compiler_params=PARAMS,
        cost_estimate=pl.CostEstimate(
            flops=0, bytes_accessed=max(2 * moved, 4_000_000), transcendentals=0
        ),
    )(*arrays)


def pick_kernel(plan, side, me, table, own, *refs):
    sent, out = refs if len(refs) == 2 else (None, refs[0])
    for at, (peer, p) in enumerate(plan):
        for j in range(2):
            for n in range(4):
                local = table[peer, 2 * side + j, n, p] & DUO_BLOCKS - 1
                slot = 4 * j + n
                if sent is None:
                    out[8 * at + slot] = own[(local >> 2 << 1) | (local & 1)]
                else:
                    out[8 * at + slot] = mixed(own, sent, local, me[CORE], 8 + slot)


def pick(me, table, plan, side, own, *sent):
    return pl.pallas_call(
        functools.partial(pick_kernel, tuple(plan), side),
        out_shape=jax.ShapeDtypeStruct((8 * len(plan),) + own.shape[1:], jnp.bfloat16),
        in_specs=[SMEM, SMEM, VMEM] + [VMEM] * len(sent),
        out_specs=VMEM,
        compiler_params=PARAMS,
        cost_estimate=pl.CostEstimate(
            flops=0, bytes_accessed=131072 * len(plan), transcendentals=0
        ),
    )(in_smem(me), in_smem(table), own, *sent)


def halves(p, start=NONE):
    return ("halves", p, start)


def on_device(
    right_sides, lower_inv, upper_inv, lower_off, upper_off, lower_pattern, upper_pattern
):
    sub, group = lax.axis_index("sub"), lax.axis_index("group")
    square, plane, duo = (2, 4, 8), (2, 4, 8, 16), (2, 4, 8, 16, 32)

    tables = [x.transpose(1, 2, 0) for x in (lower_pattern, upper_pattern)]
    mine = jnp.concatenate(tables)
    across = swapped(mine, "group", 2)

    f5, sent = first_update(right_sides, lower_inv, 8)
    right, lower_inv, off_first, table, me = staged(
        (pltpu.VMEM, [after(right_sides, sent)], None),
        (pltpu.VMEM, [lower_inv], None),
        (pltpu.VMEM, [lower_off], FIRST),
        (pltpu.SMEM, tables, None),
        (pltpu.SMEM, [positions(sub, group)], None),
    )
    near5, across, me = lax.optimization_barrier((spread(sent, (1, 2, 4)), across, me))
    near5 = (near5,)
    low = functools.partial(update, me, table, off_first, side=0, kept=FIRST)

    f4, sent = low(right, 4, [("one", 14, NONE)], [near5], level=4, inverse=[lower_inv], ways=8)
    near4 = collected(sent, square)
    mates = swapped(after(jnp.stack([mine, across]), near4[0]), "sub", 1)
    (r3,) = low(after(right, near4[0]), 3, [("one", 13, NONE)], [near5])
    (off_second,) = staged((pltpu.VMEM, [after(lower_off, near4[0])], SECOND))
    near4 = (near4[0], after(near4[1], off_second, mates))
    f3, sent = low(r3, None, [halves(9)], [near4], level=3, inverse=[lower_inv], ways=16)
    near3 = collected(sent, plane)
    (peers,) = staged((pltpu.SMEM, [after(across[None], near3[0]), mates], None))
    (r2,) = low(after(right, near3[0]), 2, [("one", 12, NONE), halves(8)], [near5, near4])
    near3 = (near3[0], after(near3[1], peers))
    f2, sent = low(r2, None, [halves(5)], [near3], level=2, inverse=[lower_inv], ways=32)
    low = functools.partial(update, me, table, off_second, side=0, kept=SECOND)
    own2 = spread(sent, duo)
    near2 = (own2, swapped(pick(me, peers, [(MATE, 2), (MATE, 1)], 0, own2), "sub", 1))
    (r1,) = low(
        after(right, own2), 1, [("one", 11, NONE), halves(7), halves(4)], [near5, near4, near3]
    )
    f1, sent = low(r1, None, [("core", 2, 0)], [near2], level=1, inverse=[lower_inv], ways=32)
    own1 = spread(sent, duo)
    near1 = (own1, swapped(pick(me, peers, [(MATE, 0), (MATE_ACROSS, 0)], 0, own1), "sub", 1))
    sent = pick(me, peers, [(ACROSS, 0)], 0, *near1)
    far = swapped(sent, "group", 2)
    lower_off, upper_inv, upper_first = staged(
        (pltpu.VMEM, [after(lower_off, sent)], None),
        (pltpu.VMEM, [upper_inv], None),
        (pltpu.VMEM, [upper_off], (0,)),
    )
    low = functools.partial(update, me, table, lower_off, side=0)
    (r0,) = low(
        right,
        0,
        [("one", 10, NONE), halves(6), halves(3), ("core", 1, 8)],
        [near5, near4, near3, near2],
    )
    far, upper_first = lax.optimization_barrier((far, upper_first))
    s0, sent = low(
        r0,
        None,
        [("far", 0, 0)],
        [near1 + (far,)],
        level=0,
        inverse=[lower_inv, upper_inv],
        ways=32,
    )

    own0 = spread(sent, duo)
    near0 = (own0, swapped(pick(me, peers, [(MATE, 0), (MATE_ACROSS, 0)], 1, own0), "sub", 1))
    sent = pick(me, peers, [(ACROSS, 0)], 1, *near0)
    far = swapped(sent, "group", 2)
    (upper_off,) = staged((pltpu.VMEM, [after(upper_off, sent)], None))
    other0 = swapped(after(own0, sent), "sub", 1)
    far, upper_off, other0 = lax.optimization_barrier((far, upper_off, other0))
    up = functools.partial(update, me, table, upper_off, side=1)
    s1, sent = up(
        f1, None, [("far", 0, 0)], [near0 + (far,)], level=1, inverse=[upper_inv], ways=32
    )
    near0 = (own0, other0)
    own1 = spread(sent, duo)
    near1 = (own1, swapped(pick(me, peers, [(MATE, 2)], 1, own1), "sub", 1))
    (r2,) = up(after(f2, own1), None, [halves(1)], [near0])
    s2, sent = up(r2, None, [("core", 2, 0)], [near1], level=2, inverse=[upper_inv], ways=16)
    near1 = (own1, swapped(after(own1, sent), "sub", 1))
    near2 = collected(sent, plane)
    (r3,) = up(
        after(f3, near2[0]), None, [halves(3, PLANE64), halves(4, PLANE64)], [near0, near1]
    )
    s3, sent = up(r3, None, [halves(5)], [near2], level=3, inverse=[upper_inv], ways=8)
    near3 = collected(sent, square)
    (r4,) = up(
        after(f4, near3[0]),
        None,
        [halves(6, SIXTEEN64), halves(7, SIXTEEN64), halves(8, SIXTEEN32)],
        [near0, near1, near2],
    )
    (r5,) = up(
        after(f5, near3[0]),
        None,
        [halves(10, EIGHT64), halves(11, EIGHT64), halves(12, EIGHT32)],
        [near0, near1, near2],
    )
    near3 = (near3[0], after(near3[1], r5))
    s4, sent = up(r4, None, [halves(9)], [near3], level=4, inverse=[upper_inv], ways=8)
    near4 = (spread(sent, (1, 2, 4)),)
    return last_update(
        me,
        table,
        upper_off,
        r5,
        [halves(13, EIGHT16), ("one", 14, NONE)],
        [near3, near4],
        upper_inv,
        [s0, s1, s2, s3, s4],
    )


def solution(mesh):
    return jax.shard_map(
        on_device,
        mesh=mesh,
        in_specs=(
            P(None, ("group", "sub"), None, None),
            P(None, ("group", "sub"), None, None),
            P(None, ("group", "sub"), None, None),
            P(None, ("group", "sub"), None, None, None),
            P(None, ("group", "sub"), None, None, None),
            P(None, ("group", "sub"), None),
            P(None, ("group", "sub"), None),
        ),
        out_specs=P(None, ("group", "sub"), None, None),
        check_vma=False,
    )
```

time: 171 us -> 164 us (0.959)
  waiting for transfers between devices: 17.7 us -> 7.38 us
  blocking collectives: 98.6 us -> 106 us
  starting transfers between devices: 37.7 us -> 30.9 us
    all_to_all x10 -> x9, blocking collectives: 98.6 us -> 106 us  [spread(): lax.all_to_all(copies, axes, 0, 0, tiled=True, axis_index_groups=groups)]
    all_to_all x2 -> x1, waiting for transfers between devices: 6.02 us -> 0.01 us  [spread(): lax.all_to_all(copies, axes, 0, 0, tiled=True, axis_index_groups=groups)]
    all_to_all x2 -> x1, starting transfers between devices: 10.9 us -> 6.53 us  [spread(): lax.all_to_all(copies, axes, 0, 0, tiled=True, axis_index_groups=groups)]
    ppermute x12 -> x14, waiting for transfers between devices: 11.7 us -> 7.38 us  [swapped(): lax.ppermute(block, axis, [(i, i ^ mask) for i in range(lax.axis_size(axi...]
    ppermute x12 -> x14, starting transfers between devices: 26.8 us -> 24.3 us  [swapped(): lax.ppermute(block, axis, [(i, i ^ mask) for i in range(lax.axis_size(axi...]
  transfers between devices with their start and end apart: 14 -> 15, of which waited for: 13 -> 8; matrix products, arithmetic and copies ran while one was open for 0% -> 1% of each run, Pallas kernels for 5% -> 7%
where the time goes in v3:
time: 164 us; the launch traced here: 163 us
  blocking collectives  106 us (65%)
  starting transfers between devices  30.9 us (19%)
  Pallas kernels  17.8 us (11%)
  waiting for transfers between devices  7.38 us (4%)
    all_to_all x9, blocking collectives, spread(): lax.all_to_all(copies, axes, 0, 0, tiled=True, axis_index_groups=groups)  106 us
    ppermute x14, starting transfers between devices, swapped(): lax.ppermute(block, axis, [(i, i ^ mask) for i in range(lax.axis_size(axi...  24.3 us
    pallas_call x5, Pallas kernels, staged(): pl.pallas_call(functools.partial(stage_kernel, tuple(plan), len(arrays)),...  9.08 us
    ppermute x14, waiting for transfers between devices, swapped(): lax.ppermute(block, axis, [(i, i ^ mask) for i in range(lax.axis_size(axi...  7.38 us
    all_to_all x1, starting transfers between devices, spread(): lax.all_to_all(copies, axes, 0, 0, tiled=True, axis_index_groups=groups)  6.53 us
    pallas_call x17, Pallas kernels, update(): pl.pallas_call(functools.partial(update_kernel, tuple(plan), side, kept,...  5.77 us
  transfers between devices with their start and end apart: 15, of which 8 were waited for; matrix products, arithmetic and copies ran while one was open for 1% of the time, Pallas kernels for 7%

profile of v3, /device:TPU:1, one launch (start us, length us, event | category | flops | bytes accessed | tf_op | source)
XLA Modules:
  0.0 163.3 jit_solution(7976947618473969904)
XLA Ops:
  0.0 1.7 %shard_map.73 = (f32[2,32,128]{2,1,0:T(8,128)S(1)}, bf16[16,32,128]{2,1,0:T(8,128)(2,1)}) custom-call(f32[6,2,32,128]{3,2,1,0:T(8,128)} %refs_0_, bf16[6,2,128,128]{3,2,1,0:T(8,128)(2,1)} %refs_1_.2), custom_call_target="tpu_custom_call" | custom-call | tf_op jit(solution)/shard_map/pallas_call | solution.py:192
  1.7 6.5 %all-to-all-start = ((bf16[16,32,128]{2,1,0:T(8,128)(2,1)}), bf16[16,32,128]{2,1,0:T(8,128)(2,1)S(1)}, u32[]{:S(2)}, u32[]{:S(2)}) async-start(bf16[16,32,128]{2,1,0:T(8,128)(2,1)} %get-tuple-element.56), calls=%async_computation | async-start | bytes 262144 | tf_op jit(solution)/shard_map/all_to_all | solution.py:37
  8.9 2.4 %collective-permute-start = (s32[4,4,15]{2,1,0:T(4,128)S(1)}, s32[4,4,15]{2,1,0:T(4,128)S(1)}, u32[]{:S(2)}, u32[]{:S(2)}) collective-permute-start(s32[4,4,15]{2,1,0:T(4,128)S(1)} %get-tuple-element.108), channel_id=1, source_target_pairs={{0,64},{32,96},{64,0},{96,32},{128,192},{160,224},{192,128},{224,1... | collective-permute-start | bytes 2888 | tf_op jit(solution)/shard_map/ppermute | solution.py:31
  12.0 1.7 %shard_map.74 = (f32[6,2,32,128]{3,2,1,0:T(8,128)S(1)}, bf16[6,2,128,128]{3,2,1,0:T(8,128)(2,1)S(1)}, bf16[6,2,4,128,128]{4,3,2,1,0:T(8,128)(2,1)S(1)}, s32[4,4,15]{2,1,0:T(4,128)S(4)}, s32[8]{0:T(128)S(4)}) custom-call(f32[6,2,32,128]{3,2,1,0:T(8,128)} %refs_0_, bf16[6,2,128,128]{3,2,1,0:T(8,128)(2,1)} %refs_1_.2, bf16[15,2,4,128,128]{4,3,2,1,0:T(8,128)(2,1)} %refs_0_.2, ...), custom_call_target="tpu_custom_call" | custom-call | bytes 4000000 | tf_op jit(solution)/shard_map/pallas_call | solution.py:277
  14.1 10.4 %all_to_all.50.refs_0_.refs_1_ = bf16[16,32,128]{2,1,0:T(8,128)(2,1)S(1)} all-to-all(bf16[16,32,128]{2,1,0:T(8,128)(2,1)S(1)} %get-tuple-element.66), channel_id=1, replica_groups={{0,2,4,6,8,10,12,14},{1,3,5,7,9,11,13,15},{16,18,20,22,24,26,28,30},{17..., dimensions={0} | all-to-all | bytes 262144 | tf_op jit(solution)/shard_map/all_to_all | solution.py:37
  24.4 2.0 %collective-permute-start.1 = (bf16[16,32,128]{2,1,0:T(8,128)(2,1)S(1)}, bf16[16,32,128]{2,1,0:T(8,128)(2,1)S(1)}, u32[]{:S(2)}, u32[]{:S(2)}) collective-permute-start(bf16[16,32,128]{2,1,0:T(8,128)(2,1)S(1)} %all_to_all.50.refs_0_.refs_1_), channel_id=1, source_target_pairs={{0,1},{1,0},{2,3},{3,2},{4,5},{5,4},{6,7},{7,6},{8,9},{9,8},{10,11... | collective-permute-start | bytes 393224 | tf_op jit(solution)/shard_map/ppermute | solution.py:31
  26.6 1.2 shard_map.77.off
  28.4 11.7 %all_to_all.51.refs_0_.refs_3_ = bf16[32,32,128]{2,1,0:T(8,128)(2,1)S(1)} all-to-all(bf16[32,32,128]{2,1,0:T(8,128)(2,1)S(1)} %get-tuple-element.71), channel_id=1, replica_groups={{0,2,4,6,8,10,12,14,16,18,20,22,24,26,28,30},{1,3,5,7,9,11,13,15,17,19,..., dimensions={0} | all-to-all | bytes 524288 | tf_op jit(solution)/shard_map/all_to_all | solution.py:37
  40.1 1.9 %collective-permute-start.3 = (bf16[32,32,128]{2,1,0:T(8,128)(2,1)S(1)}, bf16[32,32,128]{2,1,0:T(8,128)(2,1)S(1)}, u32[]{:S(2)}, u32[]{:S(2)}) collective-permute-start(bf16[32,32,128]{2,1,0:T(8,128)(2,1)S(1)} %all_to_all.51.refs_0_.refs_3_), channel_id=1, source_target_pairs={{0,1},{1,0},{2,3},{3,2},{4,5},{5,4},{6,7},{7,6},{8,9},{9,8},{10,11... | collective-permute-start | bytes 786440 | tf_op jit(solution)/shard_map/ppermute | solution.py:31
  42.1 1.1 shard_map.79.table
  43.8 14.9 %all_to_all.52.own.refs_0_.refs_5_ = bf16[64,32,128]{2,1,0:T(8,128)(2,1)S(1)} all-to-all(bf16[64,32,128]{2,1,0:T(8,128)(2,1)S(1)} %get-tuple-element.75), channel_id=1, replica_groups={{0,2,4,6,8,10,12,14,16,18,20,22,24,26,28,30,32,34,36,38,40,42,44,46,48,..., dimensions={0} | all-to-all | bytes 1048576 | tf_op jit(solution)/shard_map/all_to_all | solution.py:37
  58.8 2.4 %collective-permute-start.4 = (bf16[16,32,128]{2,1,0:T(8,128)(2,1)S(1)}, bf16[16,32,128]{2,1,0:T(8,128)(2,1)S(1)}, u32[]{:S(2)}, u32[]{:S(2)}) collective-permute-start(bf16[16,32,128]{2,1,0:T(8,128)(2,1)S(1)} %shard_map.83), channel_id=1, source_target_pairs={{0,1},{1,0},{2,3},{3,2},{4,5},{5,4},{6,7},{7,6},{8,9},{9,8},{10,11... | collective-permute-start | bytes 393224 | tf_op jit(solution)/shard_map/ppermute | solution.py:31
  62.6 13.9 %all_to_all.53.own.refs_0_ = bf16[64,32,128]{2,1,0:T(8,128)(2,1)S(1)} all-to-all(bf16[64,32,128]{2,1,0:T(8,128)(2,1)S(1)} %get-tuple-element.77), channel_id=1, replica_groups={{0,2,4,6,8,10,12,14,16,18,20,22,24,26,28,30,32,34,36,38,40,42,44,46,48,..., dimensions={0} | all-to-all | bytes 1048576 | tf_op jit(solution)/shard_map/all_to_all | solution.py:37
  76.5 2.4 %collective-permute-start.5 = (bf16[16,32,128]{2,1,0:T(8,128)(2,1)S(1)}, bf16[16,32,128]{2,1,0:T(8,128)(2,1)S(1)}, u32[]{:S(2)}, u32[]{:S(2)}) collective-permute-start(bf16[16,32,128]{2,1,0:T(8,128)(2,1)S(1)} %shard_map.85), channel_id=1, source_target_pairs={{0,1},{1,0},{2,3},{3,2},{4,5},{5,4},{6,7},{7,6},{8,9},{9,8},{10,11... | collective-permute-start | bytes 393224 | tf_op jit(solution)/shard_map/ppermute | solution.py:31
  78.9 1.0 collective-permute-done.5.refs_0_.refs_1_
  79.9 2.0 %collective-permute-start.6 = (bf16[8,32,128]{2,1,0:T(8,128)(2,1)S(1)}, bf16[8,32,128]{2,1,0:T(8,128)(2,1)S(1)}, u32[]{:S(2)}, u32[]{:S(2)}) collective-permute-start(bf16[8,32,128]{2,1,0:T(8,128)(2,1)S(1)} %shard_map.86), channel_id=1, source_target_pairs={{0,64},{32,96},{64,0},{96,32},{128,192},{160,224},{192,128},{224,1... | collective-permute-start | bytes 196616 | tf_op jit(solution)/shard_map/ppermute | solution.py:31
  82.0 3.0 %shard_map.87 = (bf16[15,2,4,128,128]{4,3,2,1,0:T(8,128)(2,1)S(1)}, bf16[6,2,128,128]{3,2,1,0:T(8,128)(2,1)S(1)}, bf16[1,2,4,128,128]{4,3,2,1,0:T(8,128)(2,1)}) custom-call(bf16[15,2,4,128,128]{4,3,2,1,0:T(8,128)(2,1)} %refs_0_.2, bf16[6,2,128,128]{3,2,1,0:T(8,128)(2,1)} %refs_1_.3, bf16[15,2,4,128,128]{4,3,2,1,0:T(8,128)(2,1)} %refs_0_.3), custom_call_target="tpu_custom_call" | custom-call | bytes 4000000 | tf_op jit(solution)/shard_map/pallas_call | solution.py:277
  86.5 13.9 %all_to_all.54.own.refs_0_ = bf16[64,32,128]{2,1,0:T(8,128)(2,1)S(1)} all-to-all(bf16[64,32,128]{2,1,0:T(8,128)(2,1)S(1)} %get-tuple-element.81), channel_id=1, replica_groups={{0,2,4,6,8,10,12,14,16,18,20,22,24,26,28,30,32,34,36,38,40,42,44,46,48,..., dimensions={0} | all-to-all | bytes 1048576 | tf_op jit(solution)/shard_map/all_to_all | solution.py:37
  100.4 2.6 %collective-permute-start.7 = (bf16[16,32,128]{2,1,0:T(8,128)(2,1)S(1)}, bf16[16,32,128]{2,1,0:T(8,128)(2,1)S(1)}, u32[]{:S(2)}, u32[]{:S(2)}) collective-permute-start(bf16[16,32,128]{2,1,0:T(8,128)(2,1)S(1)} %shard_map.90), channel_id=1, source_target_pairs={{0,1},{1,0},{2,3},{3,2},{4,5},{5,4},{6,7},{7,6},{8,9},{9,8},{10,11... | collective-permute-start | bytes 393224 | tf_op jit(solution)/shard_map/ppermute | solution.py:31
  103.0 1.0 collective-permute-done.7.refs_0_.refs_1_
  104.5 1.8 %collective-permute-start.8 = (bf16[8,32,128]{2,1,0:T(8,128)(2,1)S(1)}, bf16[8,32,128]{2,1,0:T(8,128)(2,1)S(1)}, u32[]{:S(2)}, u32[]{:S(2)}) collective-permute-start(bf16[8,32,128]{2,1,0:T(8,128)(2,1)S(1)} %shard_map.91), channel_id=1, source_target_pairs={{0,64},{32,96},{64,0},{96,32},{128,192},{160,224},{192,128},{224,1... | collective-permute-start | bytes 196616 | tf_op jit(solution)/shard_map/ppermute | solution.py:31
  106.3 2.1 %shard_map.92.off = bf16[15,2,4,128,128]{4,3,2,1,0:T(8,128)(2,1)S(1)} custom-call(bf16[15,2,4,128,128]{4,3,2,1,0:T(8,128)(2,1)} %refs_0_.3), custom_call_target="tpu_custom_call" | custom-call | bytes 4000000 | tf_op jit(solution)/shard_map/pallas_call | solution.py:277
  108.4 1.9 %collective-permute-done.8.refs_2_ = bf16[8,32,128]{2,1,0:T(8,128)(2,1)S(1)} collective-permute-done((bf16[8,32,128]{2,1,0:T(8,128)(2,1)S(1)}, bf16[8,32,128]{2,1,0:T(8,128)(2,1)S(1)}, u32[]{:S(2)}, u32[]{:S(2)}) %collective-permute-start.8) | collective-permute-done | bytes 65568 | tf_op jit(solution)/shard_map/ppermute | solution.py:31
  110.8 13.8 %all_to_all.55.own.refs_0_.refs_2_ = bf16[64,32,128]{2,1,0:T(8,128)(2,1)S(1)} all-to-all(bf16[64,32,128]{2,1,0:T(8,128)(2,1)S(1)} %get-tuple-element.90), channel_id=1, replica_groups={{0,2,4,6,8,10,12,14,16,18,20,22,24,26,28,30,32,34,36,38,40,42,44,46,48,..., dimensions={0} | all-to-all | bytes 1048576 | tf_op jit(solution)/shard_map/all_to_all | solution.py:37
  124.7 2.6 %collective-permute-start.10 = (bf16[8,32,128]{2,1,0:T(8,128)(2,1)S(1)}, bf16[8,32,128]{2,1,0:T(8,128)(2,1)S(1)}, u32[]{:S(2)}, u32[]{:S(2)}) collective-permute-start(bf16[8,32,128]{2,1,0:T(8,128)(2,1)S(1)} %shard_map.95), channel_id=1, source_target_pairs={{0,1},{1,0},{2,3},{3,2},{4,5},{5,4},{6,7},{7,6},{8,9},{9,8},{10,11... | collective-permute-start | bytes 196616 | tf_op jit(solution)/shard_map/ppermute | solution.py:31
  129.0 11.0 %all_to_all.56.refs_0_.refs_4_ = bf16[32,32,128]{2,1,0:T(8,128)(2,1)S(1)} all-to-all(bf16[32,32,128]{2,1,0:T(8,128)(2,1)S(1)} %get-tuple-element.93), channel_id=1, replica_groups={{0,2,4,6,8,10,12,14,16,18,20,22,24,26,28,30},{1,3,5,7,9,11,13,15,17,19,..., dimensions={0} | all-to-all | bytes 524288 | tf_op jit(solution)/shard_map/all_to_all | solution.py:37
  140.0 1.7 %collective-permute-start.12 = (bf16[32,32,128]{2,1,0:T(8,128)(2,1)S(1)}, bf16[32,32,128]{2,1,0:T(8,128)(2,1)S(1)}, u32[]{:S(2)}, u32[]{:S(2)}) collective-permute-start(bf16[32,32,128]{2,1,0:T(8,128)(2,1)S(1)} %all_to_all.56.refs_0_.refs_4_), channel_id=1, source_target_pairs={{0,1},{1,0},{2,3},{3,2},{4,5},{5,4},{6,7},{7,6},{8,9},{9,8},{10,11... | collective-permute-start | bytes 786440 | tf_op jit(solution)/shard_map/ppermute | solution.py:31
  141.9 0.9 collective-permute-done.12.refs_1_.refs_5_
  143.3 8.0 %all_to_all.57.refs_0_ = bf16[16,32,128]{2,1,0:T(8,128)(2,1)S(1)} all-to-all(bf16[16,32,128]{2,1,0:T(8,128)(2,1)S(1)} %get-tuple-element.96), channel_id=1, replica_groups={{0,2,4,6,8,10,12,14},{1,3,5,7,9,11,13,15},{16,18,20,22,24,26,28,30},{17..., dimensions={0} | all-to-all | bytes 262144 | tf_op jit(solution)/shard_map/all_to_all | solution.py:37
  151.3 1.5 collective-permute-start.13
  154.2 8.0 %all_to_all.58.refs_2_ = bf16[16,32,128]{2,1,0:T(8,128)(2,1)S(1)} all-to-all(bf16[16,32,128]{2,1,0:T(8,128)(2,1)S(1)} %get-tuple-element.101), channel_id=1, replica_groups={{0,1,2,3,4,5,6,7},{8,9,10,11,12,13,14,15},{16,17,18,19,20,21,22,23},{24..., dimensions={0} | all-to-all | bytes 262144 | tf_op jit(solution)/shard_map/all_to_all | solution.py:37
  162.2 1.1 shard_map.102
  (44 shorter events, 10.7 us)
Async XLA Ops:
  1.7 12.0 %all-to-all-start = ((bf16[16,32,128]{2,1,0:T(8,128)(2,1)}), bf16[16,32,128]{2,1,0:T(8,128)(2,1)S(1)}, u32[]{:S(2)}, u32[]{:S(2)}) async-start(bf16[16,32,128]{2,1,0:T(8,128)(2,1)} %get-tuple-element.56), calls=%async_computation | async-start | bytes 262144 | tf_op jit(solution)/shard_map/all_to_all | solution.py:37
  8.9 4.7 %collective-permute-start = (s32[4,4,15]{2,1,0:T(4,128)S(1)}, s32[4,4,15]{2,1,0:T(4,128)S(1)}, u32[]{:S(2)}, u32[]{:S(2)}) collective-permute-start(s32[4,4,15]{2,1,0:T(4,128)S(1)} %get-tuple-element.108), channel_id=1, source_target_pairs={{0,64},{32,96},{64,0},{96,32},{128,192},{160,224},{192,128},{224,1... | collective-permute-start | bytes 2888 | tf_op jit(solution)/shard_map/ppermute | solution.py:31
  13.7 14.3 %copy-start = (s32[4,4,15]{2,1,0:T(4,128)}, s32[4,4,15]{2,1,0:T(4,128)S(1)}, u32[]{:S(2)}) copy-start(s32[4,4,15]{2,1,0:T(4,128)S(1)} %collective-permute-done) | copy-start | bytes 2884
  24.4 3.6 %collective-permute-start.1 = (bf16[16,32,128]{2,1,0:T(8,128)(2,1)S(1)}, bf16[16,32,128]{2,1,0:T(8,128)(2,1)S(1)}, u32[]{:S(2)}, u32[]{:S(2)}) collective-permute-start(bf16[16,32,128]{2,1,0:T(8,128)(2,1)S(1)} %all_to_all.50.refs_0_.refs_1_), channel_id=1, source_target_pairs={{0,1},{1,0},{2,3},{3,2},{4,5},{5,4},{6,7},{7,6},{8,9},{9,8},{10,11... | collective-permute-start | bytes 393224 | tf_op jit(solution)/shard_map/ppermute | solution.py:31
  26.5 1.5 collective-permute-start.2
  28.0 14.1 %copy-start.1 = (s32[2,4,4,15]{3,2,1,0:T(4,128)}, s32[2,4,4,15]{3,2,1,0:T(4,128)S(1)}, u32[]{:S(2)}) copy-start(s32[2,4,4,15]{3,2,1,0:T(4,128)S(1)} %collective-permute-done.2.refs_1_) | copy-start | bytes 5764
  40.1 3.2 %collective-permute-start.3 = (bf16[32,32,128]{2,1,0:T(8,128)(2,1)S(1)}, bf16[32,32,128]{2,1,0:T(8,128)(2,1)S(1)}, u32[]{:S(2)}, u32[]{:S(2)}) collective-permute-start(bf16[32,32,128]{2,1,0:T(8,128)(2,1)S(1)} %all_to_all.51.refs_0_.refs_3_), channel_id=1, source_target_pairs={{0,1},{1,0},{2,3},{3,2},{4,5},{5,4},{6,7},{7,6},{8,9},{9,8},{10,11... | collective-permute-start | bytes 786440 | tf_op jit(solution)/shard_map/ppermute | solution.py:31
  58.8 3.4 %collective-permute-start.4 = (bf16[16,32,128]{2,1,0:T(8,128)(2,1)S(1)}, bf16[16,32,128]{2,1,0:T(8,128)(2,1)S(1)}, u32[]{:S(2)}, u32[]{:S(2)}) collective-permute-start(bf16[16,32,128]{2,1,0:T(8,128)(2,1)S(1)} %shard_map.83), channel_id=1, source_target_pairs={{0,1},{1,0},{2,3},{3,2},{4,5},{5,4},{6,7},{7,6},{8,9},{9,8},{10,11... | collective-permute-start | bytes 393224 | tf_op jit(solution)/shard_map/ppermute | solution.py:31
  76.5 3.4 %collective-permute-start.5 = (bf16[16,32,128]{2,1,0:T(8,128)(2,1)S(1)}, bf16[16,32,128]{2,1,0:T(8,128)(2,1)S(1)}, u32[]{:S(2)}, u32[]{:S(2)}) collective-permute-start(bf16[16,32,128]{2,1,0:T(8,128)(2,1)S(1)} %shard_map.85), channel_id=1, source_target_pairs={{0,1},{1,0},{2,3},{3,2},{4,5},{5,4},{6,7},{7,6},{8,9},{9,8},{10,11... | collective-permute-start | bytes 393224 | tf_op jit(solution)/shard_map/ppermute | solution.py:31
  79.9 5.9 %collective-permute-start.6 = (bf16[8,32,128]{2,1,0:T(8,128)(2,1)S(1)}, bf16[8,32,128]{2,1,0:T(8,128)(2,1)S(1)}, u32[]{:S(2)}, u32[]{:S(2)}) collective-permute-start(bf16[8,32,128]{2,1,0:T(8,128)(2,1)S(1)} %shard_map.86), channel_id=1, source_target_pairs={{0,64},{32,96},{64,0},{96,32},{128,192},{160,224},{192,128},{224,1... | collective-permute-start | bytes 196616 | tf_op jit(solution)/shard_map/ppermute | solution.py:31
  100.4 3.6 %collective-permute-start.7 = (bf16[16,32,128]{2,1,0:T(8,128)(2,1)S(1)}, bf16[16,32,128]{2,1,0:T(8,128)(2,1)S(1)}, u32[]{:S(2)}, u32[]{:S(2)}) collective-permute-start(bf16[16,32,128]{2,1,0:T(8,128)(2,1)S(1)} %shard_map.90), channel_id=1, source_target_pairs={{0,1},{1,0},{2,3},{3,2},{4,5},{5,4},{6,7},{7,6},{8,9},{9,8},{10,11... | collective-permute-start | bytes 393224 | tf_op jit(solution)/shard_map/ppermute | solution.py:31
  104.0 6.3 %collective-permute-start.9 = (bf16[64,32,128]{2,1,0:T(8,128)(2,1)S(1)}, bf16[64,32,128]{2,1,0:T(8,128)(2,1)S(1)}, u32[]{:S(2)}, u32[]{:S(2)}) collective-permute-start(bf16[64,32,128]{2,1,0:T(8,128)(2,1)S(1)} %all_to_all.54.own.refs_0_), channel_id=1, source_target_pairs={{0,1},{1,0},{2,3},{3,2},{4,5},{5,4},{6,7},{7,6},{8,9},{9,8},{10,11... | collective-permute-start | bytes 1572872 | tf_op jit(solution)/shard_map/ppermute | solution.py:31
  104.5 5.9 %collective-permute-start.8 = (bf16[8,32,128]{2,1,0:T(8,128)(2,1)S(1)}, bf16[8,32,128]{2,1,0:T(8,128)(2,1)S(1)}, u32[]{:S(2)}, u32[]{:S(2)}) collective-permute-start(bf16[8,32,128]{2,1,0:T(8,128)(2,1)S(1)} %shard_map.91), channel_id=1, source_target_pairs={{0,64},{32,96},{64,0},{96,32},{128,192},{160,224},{192,128},{224,1... | collective-permute-start | bytes 196616 | tf_op jit(solution)/shard_map/ppermute | solution.py:31
  124.7 3.5 %collective-permute-start.10 = (bf16[8,32,128]{2,1,0:T(8,128)(2,1)S(1)}, bf16[8,32,128]{2,1,0:T(8,128)(2,1)S(1)}, u32[]{:S(2)}, u32[]{:S(2)}) collective-permute-start(bf16[8,32,128]{2,1,0:T(8,128)(2,1)S(1)} %shard_map.95), channel_id=1, source_target_pairs={{0,1},{1,0},{2,3},{3,2},{4,5},{5,4},{6,7},{7,6},{8,9},{9,8},{10,11... | collective-permute-start | bytes 196616 | tf_op jit(solution)/shard_map/ppermute | solution.py:31
  128.5 13.2 %collective-permute-start.11 = (bf16[64,32,128]{2,1,0:T(8,128)(2,1)S(1)}, bf16[64,32,128]{2,1,0:T(8,128)(2,1)S(1)}, u32[]{:S(2)}, u32[]{:S(2)}) collective-permute-start(bf16[64,32,128]{2,1,0:T(8,128)(2,1)S(1)} %all_to_all.55.own.refs_0_.refs_2_), channel_id=1, source_target_pairs={{0,1},{1,0},{2,3},{3,2},{4,5},{5,4},{6,7},{7,6},{8,9},{9,8},{10,11... | collective-permute-start | bytes 1572872 | tf_op jit(solution)/shard_map/ppermute | solution.py:31
  140.0 2.8 %collective-permute-start.12 = (bf16[32,32,128]{2,1,0:T(8,128)(2,1)S(1)}, bf16[32,32,128]{2,1,0:T(8,128)(2,1)S(1)}, u32[]{:S(2)}, u32[]{:S(2)}) collective-permute-start(bf16[32,32,128]{2,1,0:T(8,128)(2,1)S(1)} %all_to_all.56.refs_0_.refs_4_), channel_id=1, source_target_pairs={{0,1},{1,0},{2,3},{3,2},{4,5},{5,4},{6,7},{7,6},{8,9},{9,8},{10,11... | collective-permute-start | bytes 786440 | tf_op jit(solution)/shard_map/ppermute | solution.py:31
  151.3 2.5 %collective-permute-start.13 = (bf16[16,32,128]{2,1,0:T(8,128)(2,1)S(1)}, bf16[16,32,128]{2,1,0:T(8,128)(2,1)S(1)}, u32[]{:S(2)}, u32[]{:S(2)}) collective-permute-start(bf16[16,32,128]{2,1,0:T(8,128)(2,1)S(1)} %all_to_all.57.refs_0_), channel_id=1, source_target_pairs={{0,1},{1,0},{2,3},{3,2},{4,5},{5,4},{6,7},{7,6},{8,9},{9,8},{10,11... | collective-permute-start | bytes 393224 | tf_op jit(solution)/shard_map/ppermute | solution.py:31

commit v4 on v3

--- a/solution.py
+++ b/solution.py
@@ -101,27 +101,27 @@
     return jnp.where((local >> 1 & 1) == core, own[index], sent[slot])
 
 
-def send(ref, j, value):
-    value = value.astype(jnp.bfloat16)
+def send(ref, totals):
+    values = [total.astype(jnp.bfloat16) for total in totals]
     for way in range(ref.shape[0] // 2):
-        ref[2 * way + j] = value
-
-
-FIRST = (14, 13, 9, 12, 8, 5)
-SECOND = (11, 7, 4, 2)
+        for j in range(2):
+            ref[2 * way + j] = values[j]
+
+
+FIRST = (14, 13, 9, 12, 8, 5, 11, 7, 4, 2)
 BUFFERS = {"one": 1, "halves": 2, "core": 2, "far": 3}
 
 
 def coupled(total, j, plan, near, side, kept, me, table, off):
     for (kind, p, start), buffers in zip(plan, near):
         at = kept.index(p) if kept else p
-        matrices = off[at, j].reshape(512, 128)
         picked = [
-            read(kind, start, buffers, me, table[2 * side + j, n, p], j * 4 + n)
-            for n in range(4)
+            read(kind, start, buffers, me, table[2 * side + j, n, p], j * 4 + n) for n in range(4)
         ]
         total = total - jnp.dot(
-            jnp.concatenate(picked, 1), matrices, preferred_element_type=jnp.float32
+            jnp.concatenate(picked, 1),
+            off[at, j].reshape(512, 128),
+            preferred_element_type=jnp.float32,
         )
     return total
 
@@ -134,17 +134,16 @@
     refs = list(refs)
     near = [[refs.pop(0) for _ in range(BUFFERS[entry[0]])] for entry in plan]
     inverse = [refs.pop(0) for _ in range(inverses)]
+    totals = [
+        coupled(base[first, j] if first is not None else base[j], j, plan, near, side, kept, me, table, off)
+        for j in range(2)
+    ]
+    for matrix in inverse:
+        totals = [times(totals[j], matrix[level, j]) for j in range(2)]
     for j in range(2):
-        total = base[first, j] if first is not None else base[j]
-        total = coupled(total, j, plan, near, side, kept, me, table, off)
-        if not inverses:
-            refs[0][j] = total
-        for matrix in inverse:
-            total = times(total, matrix[level, j])
-        if inverses:
-            refs[0][j] = total
-        if ways:
-            send(refs[-1], j, total)
+        refs[0][j] = totals[j]
+    if ways:
+        send(refs[-1], totals)
 
 
 def update(me, table, off, base, first, plan, near, side, level=0, inverse=(), ways=0, kept=None):
@@ -171,22 +170,27 @@
     )(*arguments)
 
 
-def first_kernel(level, base, matrix, out, low, right, inverse, sems):
+def first_kernel(level, base, matrix, lower, upper, out, low, joined, right, inverse, sems):
+    rows = lower.shape[0]
     copies = [
         pltpu.make_async_copy(base.at[level], right, sems.at[0]),
         pltpu.make_async_copy(matrix.at[level], inverse, sems.at[1]),
+        pltpu.make_async_copy(lower, joined.at[pl.ds(0, rows)], sems.at[2]),
+        pltpu.make_async_copy(upper, joined.at[pl.ds(rows, rows)], sems.at[3]),
     ]
     for copy in copies:
         copy.start()
-    for copy in copies:
-        copy.wait()
+    copies[0].wait()
+    copies[1].wait()
+    totals = [times(right[j], inverse[j]) for j in range(2)]
     for j in range(2):
-        total = times(right[j], inverse[j])
-        out[j] = total
-        send(low, j, total)
-
-
-def first_update(right_sides, inverse, ways):
+        out[j] = totals[j]
+    send(low, totals)
+    copies[2].wait()
+    copies[3].wait()
+
+
+def first_update(right_sides, inverse, lower, upper, ways):
     levels = right_sides.shape[0]
     shape, matrix = right_sides.shape[1:], inverse.shape[1:]
     return pl.pallas_call(
@@ -194,16 +198,17 @@
         out_shape=[
             jax.ShapeDtypeStruct(shape, jnp.float32),
             jax.ShapeDtypeStruct((2 * ways,) + shape[1:], jnp.bfloat16),
+            jax.ShapeDtypeStruct((2 * lower.shape[0],) + lower.shape[1:], lower.dtype),
         ],
-        in_specs=[HBM, HBM],
-        out_specs=[VMEM, VMEM],
+        in_specs=[HBM] * 4,
+        out_specs=[VMEM] * 3,
         scratch_shapes=[
             pltpu.VMEM(shape, jnp.float32),
             pltpu.VMEM(matrix, jnp.bfloat16),
-            pltpu.SemaphoreType.DMA((2,)),
+            pltpu.SemaphoreType.DMA((4,)),
         ],
         compiler_params=PARAMS,
-    )(in_hbm(right_sides), in_hbm(inverse))
+    )(in_hbm(right_sides), in_hbm(inverse), in_hbm(lower), in_hbm(upper))
 
 
 def last_kernel(plan, level, me, table, off, base, *refs):
@@ -216,9 +221,9 @@
     ]
     for copy in copies:
         copy.start()
+    totals = [coupled(base[j], j, plan, near, 1, None, me, table, off) for j in range(2)]
     for j in range(2):
-        total = coupled(base[j], j, plan, near, 1, None, me, table, off)
-        result[j] = times(total, inverse[level, j])
+        result[j] = times(totals[j], inverse[level, j])
     copies.append(pltpu.make_async_copy(result, out.at[level], sems.at[level]))
     copies[-1].start()
     for copy in copies:
@@ -268,7 +273,7 @@
             size = part.shape[0]
             whole = rows is None and len(parts) == 1
             plan.append((len(arrays), size, rows, out, None if whole else at))
-            arrays.append(in_hbm(part))
+            arrays.append(part if part.ndim < 3 else in_hbm(part))
             copies += len(rows) if rows else 1
             at += len(rows) if rows else size
         shapes.append(space((at,) + parts[0].shape[1:], parts[0].dtype))
@@ -324,10 +329,8 @@
     square, plane, duo = (2, 4, 8), (2, 4, 8, 16), (2, 4, 8, 16, 32)
 
     tables = [x.transpose(1, 2, 0) for x in (lower_pattern, upper_pattern)]
-    mine = jnp.concatenate(tables)
+    f5, sent, mine = first_update(right_sides, lower_inv, *tables, 8)
     across = swapped(mine, "group", 2)
-
-    f5, sent = first_update(right_sides, lower_inv, 8)
     right, lower_inv, off_first, table, me = staged(
         (pltpu.VMEM, [after(right_sides, sent)], None),
         (pltpu.VMEM, [lower_inv], None),
@@ -343,15 +346,13 @@
     near4 = collected(sent, square)
     mates = swapped(after(jnp.stack([mine, across]), near4[0]), "sub", 1)
     (r3,) = low(after(right, near4[0]), 3, [("one", 13, NONE)], [near5])
-    (off_second,) = staged((pltpu.VMEM, [after(lower_off, near4[0])], SECOND))
-    near4 = (near4[0], after(near4[1], off_second, mates))
+    near4 = (near4[0], after(near4[1], mates))
     f3, sent = low(r3, None, [halves(9)], [near4], level=3, inverse=[lower_inv], ways=16)
     near3 = collected(sent, plane)
     (peers,) = staged((pltpu.SMEM, [after(across[None], near3[0]), mates], None))
     (r2,) = low(after(right, near3[0]), 2, [("one", 12, NONE), halves(8)], [near5, near4])
     near3 = (near3[0], after(near3[1], peers))
     f2, sent = low(r2, None, [halves(5)], [near3], level=2, inverse=[lower_inv], ways=32)
-    low = functools.partial(update, me, table, off_second, side=0, kept=SECOND)
     own2 = spread(sent, duo)
     near2 = (own2, swapped(pick(me, peers, [(MATE, 2), (MATE, 1)], 0, own2), "sub", 1))
     (r1,) = low(

time: 164 us -> 161 us (0.982)
  Pallas kernels: 17.8 us -> 15.6 us
    pallas_call x5 -> x4, Pallas kernels: 9.08 us -> 8.21 us  [staged(): pl.pallas_call(functools.partial(stage_kernel, tuple(plan), len(arrays)),...]
  transfers between devices with their start and end apart: 15 -> 15, of which waited for: 8 -> 10; matrix products, arithmetic and copies ran while one was open for 1% -> 0% of each run, Pallas kernels for 7% -> 6%
where the time goes in v4:
time: 161 us
  blocking collectives  105 us (65%)
  starting transfers between devices  30.9 us (19%)
  Pallas kernels  15.6 us (10%)
  waiting for transfers between devices  8.71 us (5%)
    all_to_all x9, blocking collectives, spread(): lax.all_to_all(copies, axes, 0, 0, tiled=True, axis_index_groups=groups)  105 us
    ppermute x14, starting transfers between devices, swapped(): lax.ppermute(block, axis, [(i, i ^ mask) for i in range(lax.axis_size(axi...  24.4 us
    pallas_call x4, Pallas kernels, staged(): pl.pallas_call(functools.partial(stage_kernel, tuple(plan), len(arrays)),...  8.21 us
    ppermute x14, waiting for transfers between devices, swapped(): lax.ppermute(block, axis, [(i, i ^ mask) for i in range(lax.axis_size(axi...  8.02 us
    all_to_all x1, starting transfers between devices, spread(): lax.all_to_all(copies, axes, 0, 0, tiled=True, axis_index_groups=groups)  6.53 us
    pallas_call x17, Pallas kernels, update(): pl.pallas_call(functools.partial(update_kernel, tuple(plan), side, kept,...  4.57 us
  transfers between devices with their start and end apart: 15, of which 10 were waited for; matrix products, arithmetic and copies ran while one was open for 0% of the time, Pallas kernels for 6%

profile of v4, /device:TPU:1, one launch (start us, length us, event | category | flops | bytes accessed | tf_op | source)
XLA Modules:
  0.0 160.8 jit_solution(4787826563086993551)
XLA Ops:
  0.0 1.7 %shard_map.73 = (f32[2,32,128]{2,1,0:T(8,128)S(1)}, bf16[16,32,128]{2,1,0:T(8,128)(2,1)}, s32[4,4,15]{2,1,0:T(4,128)S(1)}) custom-call(f32[6,2,32,128]{3,2,1,0:T(8,128)} %refs_0_, bf16[6,2,128,128]{3,2,1,0:T(8,128)(2,1)} %refs_1_.2, s32[2,4,15]{2,1,0:T(4,128)} %bitcast.15, s32[2,4,15]{2,1,0:T(4,128)} %bitcast.17), custom_call_target="tpu_custom_call" | custom-call | tf_op jit(solution)/shard_map/pallas_call | solution.py:196
  1.7 6.5 %all-to-all-start = ((bf16[16,32,128]{2,1,0:T(8,128)(2,1)}), bf16[16,32,128]{2,1,0:T(8,128)(2,1)S(1)}, u32[]{:S(2)}, u32[]{:S(2)}) async-start(bf16[16,32,128]{2,1,0:T(8,128)(2,1)} %get-tuple-element.56), calls=%async_computation | async-start | bytes 262144 | tf_op jit(solution)/shard_map/all_to_all | solution.py:37
  8.2 2.4 %collective-permute-start = (s32[4,4,15]{2,1,0:T(4,128)S(1)}, s32[4,4,15]{2,1,0:T(4,128)S(1)}, u32[]{:S(2)}, u32[]{:S(2)}) collective-permute-start(s32[4,4,15]{2,1,0:T(4,128)S(1)} %get-tuple-element.57), channel_id=1, source_target_pairs={{0,64},{32,96},{64,0},{96,32},{128,192},{160,224},{192,128},{224,1... | collective-permute-start | bytes 2888 | tf_op jit(solution)/shard_map/ppermute | solution.py:31
  10.8 2.0 %shard_map.74 = (f32[6,2,32,128]{3,2,1,0:T(8,128)S(1)}, bf16[6,2,128,128]{3,2,1,0:T(8,128)(2,1)S(1)}, bf16[10,2,4,128,128]{4,3,2,1,0:T(8,128)(2,1)S(1)}, s32[4,4,15]{2,1,0:T(4,128)S(4)}, s32[8]{0:T(128)S(4)}) custom-call(f32[6,2,32,128]{3,2,1,0:T(8,128)} %refs_0_, bf16[6,2,128,128]{3,2,1,0:T(8,128)(2,1)} %refs_1_.2, bf16[15,2,4,128,128]{4,3,2,1,0:T(8,128)(2,1)} %refs_0_.1, ...), custom_call_target="tpu_custom_call" | custom-call | bytes 4000000 | tf_op jit(solution)/shard_map/pallas_call | solution.py:282
  13.8 9.7 %all_to_all.50.refs_0_.refs_1_ = bf16[16,32,128]{2,1,0:T(8,128)(2,1)S(1)} all-to-all(bf16[16,32,128]{2,1,0:T(8,128)(2,1)S(1)} %get-tuple-element.67), channel_id=1, replica_groups={{0,2,4,6,8,10,12,14},{1,3,5,7,9,11,13,15},{16,18,20,22,24,26,28,30},{17..., dimensions={0} | all-to-all | bytes 262144 | tf_op jit(solution)/shard_map/all_to_all | solution.py:37
  23.5 2.0 %collective-permute-start.1 = (bf16[16,32,128]{2,1,0:T(8,128)(2,1)S(1)}, bf16[16,32,128]{2,1,0:T(8,128)(2,1)S(1)}, u32[]{:S(2)}, u32[]{:S(2)}) collective-permute-start(bf16[16,32,128]{2,1,0:T(8,128)(2,1)S(1)} %all_to_all.50.refs_0_.refs_1_), channel_id=1, source_target_pairs={{0,1},{1,0},{2,3},{3,2},{4,5},{5,4},{6,7},{7,6},{8,9},{9,8},{10,11... | collective-permute-start | bytes 393224 | tf_op jit(solution)/shard_map/ppermute | solution.py:31
  25.8 0.9 collective-permute-done.2.refs_1_
  27.0 12.0 %all_to_all.51.refs_0_.refs_3_ = bf16[32,32,128]{2,1,0:T(8,128)(2,1)S(1)} all-to-all(bf16[32,32,128]{2,1,0:T(8,128)(2,1)S(1)} %get-tuple-element.71), channel_id=1, replica_groups={{0,2,4,6,8,10,12,14,16,18,20,22,24,26,28,30},{1,3,5,7,9,11,13,15,17,19,..., dimensions={0} | all-to-all | bytes 524288 | tf_op jit(solution)/shard_map/all_to_all | solution.py:37
  39.0 1.7 %collective-permute-start.3 = (bf16[32,32,128]{2,1,0:T(8,128)(2,1)S(1)}, bf16[32,32,128]{2,1,0:T(8,128)(2,1)S(1)}, u32[]{:S(2)}, u32[]{:S(2)}) collective-permute-start(bf16[32,32,128]{2,1,0:T(8,128)(2,1)S(1)} %all_to_all.51.refs_0_.refs_3_), channel_id=1, source_target_pairs={{0,1},{1,0},{2,3},{3,2},{4,5},{5,4},{6,7},{7,6},{8,9},{9,8},{10,11... | collective-permute-start | bytes 786440 | tf_op jit(solution)/shard_map/ppermute | solution.py:31
  40.7 1.1 shard_map.78.table
  42.3 14.9 %all_to_all.52.own.refs_0_.refs_5_ = bf16[64,32,128]{2,1,0:T(8,128)(2,1)S(1)} all-to-all(bf16[64,32,128]{2,1,0:T(8,128)(2,1)S(1)} %get-tuple-element.75), channel_id=1, replica_groups={{0,2,4,6,8,10,12,14,16,18,20,22,24,26,28,30,32,34,36,38,40,42,44,46,48,..., dimensions={0} | all-to-all | bytes 1048576 | tf_op jit(solution)/shard_map/all_to_all | solution.py:37
  57.3 2.4 %collective-permute-start.4 = (bf16[16,32,128]{2,1,0:T(8,128)(2,1)S(1)}, bf16[16,32,128]{2,1,0:T(8,128)(2,1)S(1)}, u32[]{:S(2)}, u32[]{:S(2)}) collective-permute-start(bf16[16,32,128]{2,1,0:T(8,128)(2,1)S(1)} %shard_map.82), channel_id=1, source_target_pairs={{0,1},{1,0},{2,3},{3,2},{4,5},{5,4},{6,7},{7,6},{8,9},{9,8},{10,11... | collective-permute-start | bytes 393224 | tf_op jit(solution)/shard_map/ppermute | solution.py:31
  61.0 13.9 %all_to_all.53.own.refs_0_ = bf16[64,32,128]{2,1,0:T(8,128)(2,1)S(1)} all-to-all(bf16[64,32,128]{2,1,0:T(8,128)(2,1)S(1)} %get-tuple-element.77), channel_id=1, replica_groups={{0,2,4,6,8,10,12,14,16,18,20,22,24,26,28,30,32,34,36,38,40,42,44,46,48,..., dimensions={0} | all-to-all | bytes 1048576 | tf_op jit(solution)/shard_map/all_to_all | solution.py:37
  74.9 2.4 %collective-permute-start.5 = (bf16[16,32,128]{2,1,0:T(8,128)(2,1)S(1)}, bf16[16,32,128]{2,1,0:T(8,128)(2,1)S(1)}, u32[]{:S(2)}, u32[]{:S(2)}) collective-permute-start(bf16[16,32,128]{2,1,0:T(8,128)(2,1)S(1)} %shard_map.84), channel_id=1, source_target_pairs={{0,1},{1,0},{2,3},{3,2},{4,5},{5,4},{6,7},{7,6},{8,9},{9,8},{10,11... | collective-permute-start | bytes 393224 | tf_op jit(solution)/shard_map/ppermute | solution.py:31
  77.3 1.0 collective-permute-done.5.refs_0_.refs_1_
  78.3 2.2 %collective-permute-start.6 = (bf16[8,32,128]{2,1,0:T(8,128)(2,1)S(1)}, bf16[8,32,128]{2,1,0:T(8,128)(2,1)S(1)}, u32[]{:S(2)}, u32[]{:S(2)}) collective-permute-start(bf16[8,32,128]{2,1,0:T(8,128)(2,1)S(1)} %shard_map.85), channel_id=1, source_target_pairs={{0,64},{32,96},{64,0},{96,32},{128,192},{160,224},{192,128},{224,1... | collective-permute-start | bytes 196616 | tf_op jit(solution)/shard_map/ppermute | solution.py:31
  80.5 3.0 %shard_map.86 = (bf16[15,2,4,128,128]{4,3,2,1,0:T(8,128)(2,1)S(1)}, bf16[6,2,128,128]{3,2,1,0:T(8,128)(2,1)S(1)}, bf16[1,2,4,128,128]{4,3,2,1,0:T(8,128)(2,1)}) custom-call(bf16[15,2,4,128,128]{4,3,2,1,0:T(8,128)(2,1)} %refs_0_.1, bf16[6,2,128,128]{3,2,1,0:T(8,128)(2,1)} %refs_1_.3, bf16[15,2,4,128,128]{4,3,2,1,0:T(8,128)(2,1)} %refs_0_.2), custom_call_target="tpu_custom_call" | custom-call | bytes 4000000 | tf_op jit(solution)/shard_map/pallas_call | solution.py:282
  84.6 13.9 %all_to_all.54.own.refs_0_ = bf16[64,32,128]{2,1,0:T(8,128)(2,1)S(1)} all-to-all(bf16[64,32,128]{2,1,0:T(8,128)(2,1)S(1)} %get-tuple-element.81), channel_id=1, replica_groups={{0,2,4,6,8,10,12,14,16,18,20,22,24,26,28,30,32,34,36,38,40,42,44,46,48,..., dimensions={0} | all-to-all | bytes 1048576 | tf_op jit(solution)/shard_map/all_to_all | solution.py:37
  98.5 2.6 %collective-permute-start.7 = (bf16[16,32,128]{2,1,0:T(8,128)(2,1)S(1)}, bf16[16,32,128]{2,1,0:T(8,128)(2,1)S(1)}, u32[]{:S(2)}, u32[]{:S(2)}) collective-permute-start(bf16[16,32,128]{2,1,0:T(8,128)(2,1)S(1)} %shard_map.89), channel_id=1, source_target_pairs={{0,1},{1,0},{2,3},{3,2},{4,5},{5,4},{6,7},{7,6},{8,9},{9,8},{10,11... | collective-permute-start | bytes 393224 | tf_op jit(solution)/shard_map/ppermute | solution.py:31
  101.1 1.0 collective-permute-done.7.refs_0_.refs_1_
  102.6 1.9 %collective-permute-start.8 = (bf16[8,32,128]{2,1,0:T(8,128)(2,1)S(1)}, bf16[8,32,128]{2,1,0:T(8,128)(2,1)S(1)}, u32[]{:S(2)}, u32[]{:S(2)}) collective-permute-start(bf16[8,32,128]{2,1,0:T(8,128)(2,1)S(1)} %shard_map.90), channel_id=1, source_target_pairs={{0,64},{32,96},{64,0},{96,32},{128,192},{160,224},{192,128},{224,1... | collective-permute-start | bytes 196616 | tf_op jit(solution)/shard_map/ppermute | solution.py:31
  104.5 2.1 %shard_map.91.off = bf16[15,2,4,128,128]{4,3,2,1,0:T(8,128)(2,1)S(1)} custom-call(bf16[15,2,4,128,128]{4,3,2,1,0:T(8,128)(2,1)} %refs_0_.2), custom_call_target="tpu_custom_call" | custom-call | bytes 4000000 | tf_op jit(solution)/shard_map/pallas_call | solution.py:282
  106.7 1.8 %collective-permute-done.8.refs_2_ = bf16[8,32,128]{2,1,0:T(8,128)(2,1)S(1)} collective-permute-done((bf16[8,32,128]{2,1,0:T(8,128)(2,1)S(1)}, bf16[8,32,128]{2,1,0:T(8,128)(2,1)S(1)}, u32[]{:S(2)}, u32[]{:S(2)}) %collective-permute-start.8) | collective-permute-done | bytes 65568 | tf_op jit(solution)/shard_map/ppermute | solution.py:31
  108.8 13.8 %all_to_all.55.own.refs_0_.refs_2_ = bf16[64,32,128]{2,1,0:T(8,128)(2,1)S(1)} all-to-all(bf16[64,32,128]{2,1,0:T(8,128)(2,1)S(1)} %get-tuple-element.90), channel_id=1, replica_groups={{0,2,4,6,8,10,12,14,16,18,20,22,24,26,28,30,32,34,36,38,40,42,44,46,48,..., dimensions={0} | all-to-all | bytes 1048576 | tf_op jit(solution)/shard_map/all_to_all | solution.py:37
  122.6 2.6 %collective-permute-start.10 = (bf16[8,32,128]{2,1,0:T(8,128)(2,1)S(1)}, bf16[8,32,128]{2,1,0:T(8,128)(2,1)S(1)}, u32[]{:S(2)}, u32[]{:S(2)}) collective-permute-start(bf16[8,32,128]{2,1,0:T(8,128)(2,1)S(1)} %shard_map.94), channel_id=1, source_target_pairs={{0,1},{1,0},{2,3},{3,2},{4,5},{5,4},{6,7},{7,6},{8,9},{9,8},{10,11... | collective-permute-start | bytes 196616 | tf_op jit(solution)/shard_map/ppermute | solution.py:31
  126.8 11.0 %all_to_all.56.refs_0_.refs_4_ = bf16[32,32,128]{2,1,0:T(8,128)(2,1)S(1)} all-to-all(bf16[32,32,128]{2,1,0:T(8,128)(2,1)S(1)} %get-tuple-element.93), channel_id=1, replica_groups={{0,2,4,6,8,10,12,14,16,18,20,22,24,26,28,30},{1,3,5,7,9,11,13,15,17,19,..., dimensions={0} | all-to-all | bytes 524288 | tf_op jit(solution)/shard_map/all_to_all | solution.py:37
  137.9 1.7 %collective-permute-start.12 = (bf16[32,32,128]{2,1,0:T(8,128)(2,1)S(1)}, bf16[32,32,128]{2,1,0:T(8,128)(2,1)S(1)}, u32[]{:S(2)}, u32[]{:S(2)}) collective-permute-start(bf16[32,32,128]{2,1,0:T(8,128)(2,1)S(1)} %all_to_all.56.refs_0_.refs_4_), channel_id=1, source_target_pairs={{0,1},{1,0},{2,3},{3,2},{4,5},{5,4},{6,7},{7,6},{8,9},{9,8},{10,11... | collective-permute-start | bytes 786440 | tf_op jit(solution)/shard_map/ppermute | solution.py:31
  139.8 0.9 collective-permute-done.12.refs_1_.refs_5_
  141.0 8.0 %all_to_all.57.refs_0_ = bf16[16,32,128]{2,1,0:T(8,128)(2,1)S(1)} all-to-all(bf16[16,32,128]{2,1,0:T(8,128)(2,1)S(1)} %get-tuple-element.96), channel_id=1, replica_groups={{0,2,4,6,8,10,12,14},{1,3,5,7,9,11,13,15},{16,18,20,22,24,26,28,30},{17..., dimensions={0} | all-to-all | bytes 262144 | tf_op jit(solution)/shard_map/all_to_all | solution.py:37
  149.0 1.5 collective-permute-start.13
  151.8 8.0 %all_to_all.58.refs_2_ = bf16[16,32,128]{2,1,0:T(8,128)(2,1)S(1)} all-to-all(bf16[16,32,128]{2,1,0:T(8,128)(2,1)S(1)} %get-tuple-element.101), channel_id=1, replica_groups={{0,1,2,3,4,5,6,7},{8,9,10,11,12,13,14,15},{16,17,18,19,20,21,22,23},{24..., dimensions={0} | all-to-all | bytes 262144 | tf_op jit(solution)/shard_map/all_to_all | solution.py:37
  159.8 1.0 shard_map.101
  (42 shorter events, 8.9 us)
Async XLA Ops:
  1.7 11.8 %all-to-all-start = ((bf16[16,32,128]{2,1,0:T(8,128)(2,1)}), bf16[16,32,128]{2,1,0:T(8,128)(2,1)S(1)}, u32[]{:S(2)}, u32[]{:S(2)}) async-start(bf16[16,32,128]{2,1,0:T(8,128)(2,1)} %get-tuple-element.56), calls=%async_computation | async-start | bytes 262144 | tf_op jit(solution)/shard_map/all_to_all | solution.py:37
  8.2 4.6 %collective-permute-start = (s32[4,4,15]{2,1,0:T(4,128)S(1)}, s32[4,4,15]{2,1,0:T(4,128)S(1)}, u32[]{:S(2)}, u32[]{:S(2)}) collective-permute-start(s32[4,4,15]{2,1,0:T(4,128)S(1)} %get-tuple-element.57), channel_id=1, source_target_pairs={{0,64},{32,96},{64,0},{96,32},{128,192},{160,224},{192,128},{224,1... | collective-permute-start | bytes 2888 | tf_op jit(solution)/shard_map/ppermute | solution.py:31
  12.8 14.2 %copy-start = (s32[4,4,15]{2,1,0:T(4,128)}, s32[4,4,15]{2,1,0:T(4,128)S(1)}, u32[]{:S(2)}) copy-start(s32[4,4,15]{2,1,0:T(4,128)S(1)} %collective-permute-done) | copy-start | bytes 2884
  23.5 3.2 %collective-permute-start.1 = (bf16[16,32,128]{2,1,0:T(8,128)(2,1)S(1)}, bf16[16,32,128]{2,1,0:T(8,128)(2,1)S(1)}, u32[]{:S(2)}, u32[]{:S(2)}) collective-permute-start(bf16[16,32,128]{2,1,0:T(8,128)(2,1)S(1)} %all_to_all.50.refs_0_.refs_1_), channel_id=1, source_target_pairs={{0,1},{1,0},{2,3},{3,2},{4,5},{5,4},{6,7},{7,6},{8,9},{9,8},{10,11... | collective-permute-start | bytes 393224 | tf_op jit(solution)/shard_map/ppermute | solution.py:31
  25.5 1.2 collective-permute-start.2
  26.7 14.0 %copy-start.1 = (s32[2,4,4,15]{3,2,1,0:T(4,128)}, s32[2,4,4,15]{3,2,1,0:T(4,128)S(1)}, u32[]{:S(2)}) copy-start(s32[2,4,4,15]{3,2,1,0:T(4,128)S(1)} %collective-permute-done.2.refs_1_) | copy-start | bytes 5764
  39.0 3.0 %collective-permute-start.3 = (bf16[32,32,128]{2,1,0:T(8,128)(2,1)S(1)}, bf16[32,32,128]{2,1,0:T(8,128)(2,1)S(1)}, u32[]{:S(2)}, u32[]{:S(2)}) collective-permute-start(bf16[32,32,128]{2,1,0:T(8,128)(2,1)S(1)} %all_to_all.51.refs_0_.refs_3_), channel_id=1, source_target_pairs={{0,1},{1,0},{2,3},{3,2},{4,5},{5,4},{6,7},{7,6},{8,9},{9,8},{10,11... | collective-permute-start | bytes 786440 | tf_op jit(solution)/shard_map/ppermute | solution.py:31
  57.3 3.4 %collective-permute-start.4 = (bf16[16,32,128]{2,1,0:T(8,128)(2,1)S(1)}, bf16[16,32,128]{2,1,0:T(8,128)(2,1)S(1)}, u32[]{:S(2)}, u32[]{:S(2)}) collective-permute-start(bf16[16,32,128]{2,1,0:T(8,128)(2,1)S(1)} %shard_map.82), channel_id=1, source_target_pairs={{0,1},{1,0},{2,3},{3,2},{4,5},{5,4},{6,7},{7,6},{8,9},{9,8},{10,11... | collective-permute-start | bytes 393224 | tf_op jit(solution)/shard_map/ppermute | solution.py:31
  74.9 3.4 %collective-permute-start.5 = (bf16[16,32,128]{2,1,0:T(8,128)(2,1)S(1)}, bf16[16,32,128]{2,1,0:T(8,128)(2,1)S(1)}, u32[]{:S(2)}, u32[]{:S(2)}) collective-permute-start(bf16[16,32,128]{2,1,0:T(8,128)(2,1)S(1)} %shard_map.84), channel_id=1, source_target_pairs={{0,1},{1,0},{2,3},{3,2},{4,5},{5,4},{6,7},{7,6},{8,9},{9,8},{10,11... | collective-permute-start | bytes 393224 | tf_op jit(solution)/shard_map/ppermute | solution.py:31
  78.3 5.9 %collective-permute-start.6 = (bf16[8,32,128]{2,1,0:T(8,128)(2,1)S(1)}, bf16[8,32,128]{2,1,0:T(8,128)(2,1)S(1)}, u32[]{:S(2)}, u32[]{:S(2)}) collective-permute-start(bf16[8,32,128]{2,1,0:T(8,128)(2,1)S(1)} %shard_map.85), channel_id=1, source_target_pairs={{0,64},{32,96},{64,0},{96,32},{128,192},{160,224},{192,128},{224,1... | collective-permute-start | bytes 196616 | tf_op jit(solution)/shard_map/ppermute | solution.py:31
  98.5 3.6 %collective-permute-start.7 = (bf16[16,32,128]{2,1,0:T(8,128)(2,1)S(1)}, bf16[16,32,128]{2,1,0:T(8,128)(2,1)S(1)}, u32[]{:S(2)}, u32[]{:S(2)}) collective-permute-start(bf16[16,32,128]{2,1,0:T(8,128)(2,1)S(1)} %shard_map.89), channel_id=1, source_target_pairs={{0,1},{1,0},{2,3},{3,2},{4,5},{5,4},{6,7},{7,6},{8,9},{9,8},{10,11... | collective-permute-start | bytes 393224 | tf_op jit(solution)/shard_map/ppermute | solution.py:31
  102.1 6.3 %collective-permute-start.9 = (bf16[64,32,128]{2,1,0:T(8,128)(2,1)S(1)}, bf16[64,32,128]{2,1,0:T(8,128)(2,1)S(1)}, u32[]{:S(2)}, u32[]{:S(2)}) collective-permute-start(bf16[64,32,128]{2,1,0:T(8,128)(2,1)S(1)} %all_to_all.54.own.refs_0_), channel_id=1, source_target_pairs={{0,1},{1,0},{2,3},{3,2},{4,5},{5,4},{6,7},{7,6},{8,9},{9,8},{10,11... | collective-permute-start | bytes 1572872 | tf_op jit(solution)/shard_map/ppermute | solution.py:31
  102.6 5.9 %collective-permute-start.8 = (bf16[8,32,128]{2,1,0:T(8,128)(2,1)S(1)}, bf16[8,32,128]{2,1,0:T(8,128)(2,1)S(1)}, u32[]{:S(2)}, u32[]{:S(2)}) collective-permute-start(bf16[8,32,128]{2,1,0:T(8,128)(2,1)S(1)} %shard_map.90), channel_id=1, source_target_pairs={{0,64},{32,96},{64,0},{96,32},{128,192},{160,224},{192,128},{224,1... | collective-permute-start | bytes 196616 | tf_op jit(solution)/shard_map/ppermute | solution.py:31
  122.6 3.5 %collective-permute-start.10 = (bf16[8,32,128]{2,1,0:T(8,128)(2,1)S(1)}, bf16[8,32,128]{2,1,0:T(8,128)(2,1)S(1)}, u32[]{:S(2)}, u32[]{:S(2)}) collective-permute-start(bf16[8,32,128]{2,1,0:T(8,128)(2,1)S(1)} %shard_map.94), channel_id=1, source_target_pairs={{0,1},{1,0},{2,3},{3,2},{4,5},{5,4},{6,7},{7,6},{8,9},{9,8},{10,11... | collective-permute-start | bytes 196616 | tf_op jit(solution)/shard_map/ppermute | solution.py:31
  126.4 13.2 %collective-permute-start.11 = (bf16[64,32,128]{2,1,0:T(8,128)(2,1)S(1)}, bf16[64,32,128]{2,1,0:T(8,128)(2,1)S(1)}, u32[]{:S(2)}, u32[]{:S(2)}) collective-permute-start(bf16[64,32,128]{2,1,0:T(8,128)(2,1)S(1)} %all_to_all.55.own.refs_0_.refs_2_), channel_id=1, source_target_pairs={{0,1},{1,0},{2,3},{3,2},{4,5},{5,4},{6,7},{7,6},{8,9},{9,8},{10,11... | collective-permute-start | bytes 1572872 | tf_op jit(solution)/shard_map/ppermute | solution.py:31
  137.9 2.8 %collective-permute-start.12 = (bf16[32,32,128]{2,1,0:T(8,128)(2,1)S(1)}, bf16[32,32,128]{2,1,0:T(8,128)(2,1)S(1)}, u32[]{:S(2)}, u32[]{:S(2)}) collective-permute-start(bf16[32,32,128]{2,1,0:T(8,128)(2,1)S(1)} %all_to_all.56.refs_0_.refs_4_), channel_id=1, source_target_pairs={{0,1},{1,0},{2,3},{3,2},{4,5},{5,4},{6,7},{7,6},{8,9},{9,8},{10,11... | collective-permute-start | bytes 786440 | tf_op jit(solution)/shard_map/ppermute | solution.py:31
  149.0 2.5 %collective-permute-start.13 = (bf16[16,32,128]{2,1,0:T(8,128)(2,1)S(1)}, bf16[16,32,128]{2,1,0:T(8,128)(2,1)S(1)}, u32[]{:S(2)}, u32[]{:S(2)}) collective-permute-start(bf16[16,32,128]{2,1,0:T(8,128)(2,1)S(1)} %all_to_all.57.refs_0_), channel_id=1, source_target_pairs={{0,1},{1,0},{2,3},{3,2},{4,5},{5,4},{6,7},{7,6},{8,9},{9,8},{10,11... | collective-permute-start | bytes 393224 | tf_op jit(solution)/shard_map/ppermute | solution.py:31

commit v5 on v4

--- a/solution.py
+++ b/solution.py
@@ -170,6 +170,31 @@
     )(*arguments)
 
 
+def premultiply_kernel(entries, kept, count, off, *refs):
+    out = refs[count]
+    for at, (p, level) in enumerate(entries):
+        for j in range(2):
+            value = off[kept.index(p) if kept else p, j].reshape(512, 128)
+            for matrix in refs[:count]:
+                value = times(value, matrix[level, j]).astype(jnp.bfloat16)
+            out[at, j] = value.reshape(out.shape[2:])
+
+
+def premultiplied(off, kept, entries, matrices):
+    return pl.pallas_call(
+        functools.partial(premultiply_kernel, tuple(entries), kept, len(matrices)),
+        out_shape=pltpu.VMEM((len(entries),) + off.shape[1:], off.dtype),
+        in_specs=[VMEM] * (1 + len(matrices)),
+        out_specs=VMEM,
+        compiler_params=PARAMS,
+        cost_estimate=pl.CostEstimate(
+            flops=len(entries) * len(matrices) * 4 * 512 * 128 * 128,
+            bytes_accessed=len(entries) * 524288,
+            transcendentals=0,
+        ),
+    )(in_vmem(off), *[in_vmem(matrix) for matrix in matrices])
+
+
 def first_kernel(level, base, matrix, lower, upper, out, low, joined, right, inverse, sems):
     rows = lower.shape[0]
     copies = [
@@ -211,33 +236,32 @@
     )(in_hbm(right_sides), in_hbm(inverse), in_hbm(lower), in_hbm(upper))
 
 
-def last_kernel(plan, level, me, table, off, base, *refs):
+def last_kernel(plan, kept, me, table, off, base, *refs):
     refs = list(refs)
     near = [[refs.pop(0) for _ in range(BUFFERS[entry[0]])] for entry in plan]
-    inverse = refs.pop(0)
     out, result, sems = refs[-3:]
-    copies = [
-        pltpu.make_async_copy(ref, out.at[at], sems.at[at]) for at, ref in enumerate(refs[:-3])
-    ]
+    solved = refs[:-3]
+    copies = [pltpu.make_async_copy(ref, out.at[at], sems.at[at]) for at, ref in enumerate(solved)]
     for copy in copies:
         copy.start()
-    totals = [coupled(base[j], j, plan, near, 1, None, me, table, off) for j in range(2)]
+    totals = [coupled(base[j], j, plan, near, 1, kept, me, table, off) for j in range(2)]
     for j in range(2):
-        result[j] = times(totals[j], inverse[level, j])
+        result[j] = totals[j]
+    level = len(solved)
     copies.append(pltpu.make_async_copy(result, out.at[level], sems.at[level]))
     copies[-1].start()
     for copy in copies:
         copy.wait()
 
 
-def last_update(me, table, off, base, plan, near, inverse, solved):
+def last_update(me, table, off, base, plan, near, kept, solved):
     levels = len(solved) + 1
     arguments = [in_smem(me), in_smem(table), in_vmem(off), in_vmem(base)]
     for buffers in near:
         arguments += list(buffers)
-    arguments += [in_vmem(inverse)] + [in_vmem(value) for value in solved]
+    arguments += [in_vmem(value) for value in solved]
     return pl.pallas_call(
-        functools.partial(last_kernel, tuple(plan), levels - 1),
+        functools.partial(last_kernel, tuple(plan), kept),
         out_shape=jax.ShapeDtypeStruct((levels,) + base.shape, jnp.float32),
         in_specs=[SMEM, SMEM] + [VMEM] * (len(arguments) - 2),
         out_specs=HBM,
@@ -273,7 +297,7 @@
             size = part.shape[0]
             whole = rows is None and len(parts) == 1
             plan.append((len(arrays), size, rows, out, None if whole else at))
-            arrays.append(part if part.ndim < 3 else in_hbm(part))
+            arrays.append(in_hbm(part) if part.ndim == 3 or space is pltpu.VMEM else part)
             copies += len(rows) if rows else 1
             at += len(rows) if rows else size
         shapes.append(space((at,) + parts[0].shape[1:], parts[0].dtype))
@@ -345,28 +369,46 @@
     f4, sent = low(right, 4, [("one", 14, NONE)], [near5], level=4, inverse=[lower_inv], ways=8)
     near4 = collected(sent, square)
     mates = swapped(after(jnp.stack([mine, across]), near4[0]), "sub", 1)
-    (r3,) = low(after(right, near4[0]), 3, [("one", 13, NONE)], [near5])
-    near4 = (near4[0], after(near4[1], mates))
-    f3, sent = low(r3, None, [halves(9)], [near4], level=3, inverse=[lower_inv], ways=16)
+    (r3,) = low(
+        after(right, near4[0]), 3, [("one", 13, NONE)], [near5], level=3, inverse=[lower_inv]
+    )
+    off_low = premultiplied(after(off_first, near4[0]), FIRST, [(9, 3), (5, 2)], [lower_inv])
+    last_low = functools.partial(update, me, table, off_low, side=0, kept=(9, 5))
+    near4 = (near4[0], after(near4[1], mates, off_low))
+    f3, sent = last_low(r3, None, [halves(9)], [near4], ways=16)
     near3 = collected(sent, plane)
     (peers,) = staged((pltpu.SMEM, [after(across[None], near3[0]), mates], None))
-    (r2,) = low(after(right, near3[0]), 2, [("one", 12, NONE), halves(8)], [near5, near4])
+    (r2,) = low(
+        after(right, near3[0]),
+        2,
+        [("one", 12, NONE), halves(8)],
+        [near5, near4],
+        level=2,
+        inverse=[lower_inv],
+    )
     near3 = (near3[0], after(near3[1], peers))
-    f2, sent = low(r2, None, [halves(5)], [near3], level=2, inverse=[lower_inv], ways=32)
+    f2, sent = last_low(r2, None, [halves(5)], [near3], ways=32)
     own2 = spread(sent, duo)
     near2 = (own2, swapped(pick(me, peers, [(MATE, 2), (MATE, 1)], 0, own2), "sub", 1))
     (r1,) = low(
-        after(right, own2), 1, [("one", 11, NONE), halves(7), halves(4)], [near5, near4, near3]
-    )
-    f1, sent = low(r1, None, [("core", 2, 0)], [near2], level=1, inverse=[lower_inv], ways=32)
+        after(right, own2),
+        1,
+        [("one", 11, NONE), halves(7), halves(4)],
+        [near5, near4, near3],
+        level=1,
+        inverse=[lower_inv],
+    )
+    off_low = premultiplied(after(off_first, own2), FIRST, [(2, 1)], [lower_inv])
+    f1, sent = update(
+        me, table, off_low, r1, None, [("core", 2, 0)], [near2], 0, ways=32, kept=(2,)
+    )
     own1 = spread(sent, duo)
     near1 = (own1, swapped(pick(me, peers, [(MATE, 0), (MATE_ACROSS, 0)], 0, own1), "sub", 1))
     sent = pick(me, peers, [(ACROSS, 0)], 0, *near1)
     far = swapped(sent, "group", 2)
-    lower_off, upper_inv, upper_first = staged(
+    lower_off, upper_inv = staged(
         (pltpu.VMEM, [after(lower_off, sent)], None),
         (pltpu.VMEM, [upper_inv], None),
-        (pltpu.VMEM, [upper_off], (0,)),
     )
     low = functools.partial(update, me, table, lower_off, side=0)
     (r0,) = low(
@@ -374,16 +416,13 @@
         0,
         [("one", 10, NONE), halves(6), halves(3), ("core", 1, 8)],
         [near5, near4, near3, near2],
-    )
-    far, upper_first = lax.optimization_barrier((far, upper_first))
-    s0, sent = low(
-        r0,
-        None,
-        [("far", 0, 0)],
-        [near1 + (far,)],
         level=0,
         inverse=[lower_inv, upper_inv],
-        ways=32,
+    )
+    off_low = premultiplied(lower_off, None, [(0, 0)], [lower_inv, upper_inv])
+    far, r0, off_low = lax.optimization_barrier((far, r0, off_low))
+    s0, sent = update(
+        me, table, off_low, r0, None, [("far", 0, 0)], [near1 + (far,)], 0, ways=32, kept=(0,)
     )
 
     own0 = spread(sent, duo)
@@ -392,46 +431,58 @@
     far = swapped(sent, "group", 2)
     (upper_off,) = staged((pltpu.VMEM, [after(upper_off, sent)], None))
     other0 = swapped(after(own0, sent), "sub", 1)
-    far, upper_off, other0 = lax.optimization_barrier((far, upper_off, other0))
     up = functools.partial(update, me, table, upper_off, side=1)
-    s1, sent = up(
-        f1, None, [("far", 0, 0)], [near0 + (far,)], level=1, inverse=[upper_inv], ways=32
-    )
+    (r1,) = up(f1, None, [], [], level=1, inverse=[upper_inv])
+    entries = [(0, 1), (2, 2), (5, 3), (9, 4), (13, 5), (14, 5)]
+    off_up = premultiplied(upper_off, None, entries, [upper_inv])
+    kept = tuple(p for p, _ in entries)
+    last_up = functools.partial(update, me, table, off_up, side=1, kept=kept)
+    far, off_up, other0, r1 = lax.optimization_barrier((far, off_up, other0, r1))
+    s1, sent = last_up(r1, None, [("far", 0, 0)], [near0 + (far,)], ways=32)
     near0 = (own0, other0)
     own1 = spread(sent, duo)
     near1 = (own1, swapped(pick(me, peers, [(MATE, 2)], 1, own1), "sub", 1))
-    (r2,) = up(after(f2, own1), None, [halves(1)], [near0])
-    s2, sent = up(r2, None, [("core", 2, 0)], [near1], level=2, inverse=[upper_inv], ways=16)
-    near1 = (own1, swapped(after(own1, sent), "sub", 1))
+    (r2,) = up(after(f2, own1), None, [halves(1)], [near0], level=2, inverse=[upper_inv])
+    s2, sent = last_up(r2, None, [("core", 2, 0)], [near1], ways=16)
+    near1 = (own1, swapped(after(own1, r2), "sub", 1))
     near2 = collected(sent, plane)
     (r3,) = up(
-        after(f3, near2[0]), None, [halves(3, PLANE64), halves(4, PLANE64)], [near0, near1]
-    )
-    s3, sent = up(r3, None, [halves(5)], [near2], level=3, inverse=[upper_inv], ways=8)
+        after(f3, near2[0]),
+        None,
+        [halves(3, PLANE64), halves(4, PLANE64)],
+        [near0, near1],
+        level=3,
+        inverse=[upper_inv],
+    )
+    s3, sent = last_up(r3, None, [halves(5)], [near2], ways=8)
     near3 = collected(sent, square)
     (r4,) = up(
         after(f4, near3[0]),
         None,
         [halves(6, SIXTEEN64), halves(7, SIXTEEN64), halves(8, SIXTEEN32)],
         [near0, near1, near2],
+        level=4,
+        inverse=[upper_inv],
     )
     (r5,) = up(
         after(f5, near3[0]),
         None,
         [halves(10, EIGHT64), halves(11, EIGHT64), halves(12, EIGHT32)],
         [near0, near1, near2],
+        level=5,
+        inverse=[upper_inv],
     )
     near3 = (near3[0], after(near3[1], r5))
-    s4, sent = up(r4, None, [halves(9)], [near3], level=4, inverse=[upper_inv], ways=8)
+    s4, sent = last_up(r4, None, [halves(9)], [near3], ways=8)
     near4 = (spread(sent, (1, 2, 4)),)
     return last_update(
         me,
         table,
-        upper_off,
+        off_up,
         r5,
         [halves(13, EIGHT16), ("one", 14, NONE)],
         [near3, near4],
-        upper_inv,
+        kept,
         [s0, s1, s2, s3, s4],
     )
 

time: 161 us -> 160 us (level)
  waiting for transfers between devices: 8.71 us -> 6.91 us
    ppermute x14, waiting for transfers between devices: 8.02 us -> 6.21 us  [swapped(): lax.ppermute(block, axis, [(i, i ^ mask) for i in range(lax.axis_size(axi...]
    pallas_call x17 -> x18, Pallas kernels: 4.57 us -> 4.75 us  [update(): pl.pallas_call(functools.partial(update_kernel, tuple(plan), side, kept,...]
  transfers between devices with their start and end apart: 15 -> 15, of which waited for: 10 -> 10; matrix products, arithmetic and copies ran while one was open for 0% -> 0% of each run, Pallas kernels for 6% -> 7%
where the time goes in v5:
time: 160 us
  blocking collectives  105 us (66%)
  starting transfers between devices  30.7 us (19%)
  Pallas kernels  16.2 us (10%)
  waiting for transfers between devices  6.91 us (4%)
    all_to_all x9, blocking collectives, spread(): lax.all_to_all(copies, axes, 0, 0, tiled=True, axis_index_groups=groups)  105 us
    ppermute x14, starting transfers between devices, swapped(): lax.ppermute(block, axis, [(i, i ^ mask) for i in range(lax.axis_size(axi...  24.2 us
    pallas_call x4, Pallas kernels, staged(): pl.pallas_call(functools.partial(stage_kernel, tuple(plan), len(arrays)),...  7.3 us
    all_to_all x1, starting transfers between devices, spread(): lax.all_to_all(copies, axes, 0, 0, tiled=True, axis_index_groups=groups)  6.53 us
    ppermute x14, waiting for transfers between devices, swapped(): lax.ppermute(block, axis, [(i, i ^ mask) for i in range(lax.axis_size(axi...  6.21 us
    pallas_call x18, Pallas kernels, update(): pl.pallas_call(functools.partial(update_kernel, tuple(plan), side, kept,...  4.75 us
  transfers between devices with their start and end apart: 15, of which 10 were waited for; matrix products, arithmetic and copies ran while one was open for 0% of the time, Pallas kernels for 7%

profile of v5, /device:TPU:1, one launch (start us, length us, event | category | flops | bytes accessed | tf_op | source)
XLA Modules:
  0.0 159.5 jit_solution(14394931888565144414)
XLA Ops:
  0.0 1.7 %shard_map.73 = (f32[2,32,128]{2,1,0:T(8,128)S(1)}, bf16[16,32,128]{2,1,0:T(8,128)(2,1)}, s32[4,4,15]{2,1,0:T(4,128)S(1)}) custom-call(f32[6,2,32,128]{3,2,1,0:T(8,128)} %refs_0_, bf16[6,2,128,128]{3,2,1,0:T(8,128)(2,1)} %refs_1_.2, s32[2,4,15]{2,1,0:T(4,128)} %bitcast.15, s32[2,4,15]{2,1,0:T(4,128)} %bitcast.17), custom_call_target="tpu_custom_call" | custom-call | tf_op jit(solution)/shard_map/pallas_call | solution.py:221
  1.7 6.5 %all-to-all-start = ((bf16[16,32,128]{2,1,0:T(8,128)(2,1)}), bf16[16,32,128]{2,1,0:T(8,128)(2,1)S(1)}, u32[]{:S(2)}, u32[]{:S(2)}) async-start(bf16[16,32,128]{2,1,0:T(8,128)(2,1)} %get-tuple-element.62), calls=%async_computation | async-start | bytes 262144 | tf_op jit(solution)/shard_map/all_to_all | solution.py:37
  8.2 2.4 %collective-permute-start = (s32[4,4,15]{2,1,0:T(4,128)S(1)}, s32[4,4,15]{2,1,0:T(4,128)S(1)}, u32[]{:S(2)}, u32[]{:S(2)}) collective-permute-start(s32[4,4,15]{2,1,0:T(4,128)S(1)} %get-tuple-element.63), channel_id=1, source_target_pairs={{0,64},{32,96},{64,0},{96,32},{128,192},{160,224},{192,128},{224,1... | collective-permute-start | bytes 2888 | tf_op jit(solution)/shard_map/ppermute | solution.py:31
  10.8 2.0 %shard_map.74 = (f32[6,2,32,128]{3,2,1,0:T(8,128)S(1)}, bf16[6,2,128,128]{3,2,1,0:T(8,128)(2,1)S(1)}, bf16[10,2,4,128,128]{4,3,2,1,0:T(8,128)(2,1)S(1)}, s32[4,4,15]{2,1,0:T(4,128)S(4)}, s32[8]{0:T(128)S(4)}) custom-call(f32[6,2,32,128]{3,2,1,0:T(8,128)} %refs_0_, bf16[6,2,128,128]{3,2,1,0:T(8,128)(2,1)} %refs_1_.2, bf16[15,2,4,128,128]{4,3,2,1,0:T(8,128)(2,1)} %refs_0_.1, ...), custom_call_target="tpu_custom_call" | custom-call | bytes 4000000 | tf_op jit(solution)/shard_map/pallas_call | solution.py:306
  12.8 0.7 all-to-all-done.refs_0_
  13.8 9.7 %all_to_all.50.refs_0_.refs_1_ = bf16[16,32,128]{2,1,0:T(8,128)(2,1)S(1)} all-to-all(bf16[16,32,128]{2,1,0:T(8,128)(2,1)S(1)} %get-tuple-element.73), channel_id=1, replica_groups={{0,2,4,6,8,10,12,14},{1,3,5,7,9,11,13,15},{16,18,20,22,24,26,28,30},{17..., dimensions={0} | all-to-all | bytes 262144 | tf_op jit(solution)/shard_map/all_to_all | solution.py:37
  23.5 2.0 %collective-permute-start.1 = (bf16[16,32,128]{2,1,0:T(8,128)(2,1)S(1)}, bf16[16,32,128]{2,1,0:T(8,128)(2,1)S(1)}, u32[]{:S(2)}, u32[]{:S(2)}) collective-permute-start(bf16[16,32,128]{2,1,0:T(8,128)(2,1)S(1)} %all_to_all.50.refs_0_.refs_1_), channel_id=1, source_target_pairs={{0,1},{1,0},{2,3},{3,2},{4,5},{5,4},{6,7},{7,6},{8,9},{9,8},{10,11... | collective-permute-start | bytes 393224 | tf_op jit(solution)/shard_map/ppermute | solution.py:31
  26.9 12.0 %all_to_all.51.refs_0_.refs_3_ = bf16[32,32,128]{2,1,0:T(8,128)(2,1)S(1)} all-to-all(bf16[32,32,128]{2,1,0:T(8,128)(2,1)S(1)} %get-tuple-element.78), channel_id=1, replica_groups={{0,2,4,6,8,10,12,14,16,18,20,22,24,26,28,30},{1,3,5,7,9,11,13,15,17,19,..., dimensions={0} | all-to-all | bytes 524288 | tf_op jit(solution)/shard_map/all_to_all | solution.py:37
  38.8 1.7 %collective-permute-start.3 = (bf16[32,32,128]{2,1,0:T(8,128)(2,1)S(1)}, bf16[32,32,128]{2,1,0:T(8,128)(2,1)S(1)}, u32[]{:S(2)}, u32[]{:S(2)}) collective-permute-start(bf16[32,32,128]{2,1,0:T(8,128)(2,1)S(1)} %all_to_all.51.refs_0_.refs_3_), channel_id=1, source_target_pairs={{0,1},{1,0},{2,3},{3,2},{4,5},{5,4},{6,7},{7,6},{8,9},{9,8},{10,11... | collective-permute-start | bytes 786440 | tf_op jit(solution)/shard_map/ppermute | solution.py:31
  40.5 0.9 shard_map.79.table
  42.0 14.9 %all_to_all.52.own.refs_0_.refs_5_ = bf16[64,32,128]{2,1,0:T(8,128)(2,1)S(1)} all-to-all(bf16[64,32,128]{2,1,0:T(8,128)(2,1)S(1)} %get-tuple-element.82), channel_id=1, replica_groups={{0,2,4,6,8,10,12,14,16,18,20,22,24,26,28,30,32,34,36,38,40,42,44,46,48,..., dimensions={0} | all-to-all | bytes 1048576 | tf_op jit(solution)/shard_map/all_to_all | solution.py:37
  57.0 2.4 %collective-permute-start.4 = (bf16[16,32,128]{2,1,0:T(8,128)(2,1)S(1)}, bf16[16,32,128]{2,1,0:T(8,128)(2,1)S(1)}, u32[]{:S(2)}, u32[]{:S(2)}) collective-permute-start(bf16[16,32,128]{2,1,0:T(8,128)(2,1)S(1)} %shard_map.84), channel_id=1, source_target_pairs={{0,1},{1,0},{2,3},{3,2},{4,5},{5,4},{6,7},{7,6},{8,9},{9,8},{10,11... | collective-permute-start | bytes 393224 | tf_op jit(solution)/shard_map/ppermute | solution.py:31
  60.6 13.9 %all_to_all.53.own.refs_0_ = bf16[64,32,128]{2,1,0:T(8,128)(2,1)S(1)} all-to-all(bf16[64,32,128]{2,1,0:T(8,128)(2,1)S(1)} %get-tuple-element.85), channel_id=1, replica_groups={{0,2,4,6,8,10,12,14,16,18,20,22,24,26,28,30,32,34,36,38,40,42,44,46,48,..., dimensions={0} | all-to-all | bytes 1048576 | tf_op jit(solution)/shard_map/all_to_all | solution.py:37
  74.5 2.4 %collective-permute-start.5 = (bf16[16,32,128]{2,1,0:T(8,128)(2,1)S(1)}, bf16[16,32,128]{2,1,0:T(8,128)(2,1)S(1)}, u32[]{:S(2)}, u32[]{:S(2)}) collective-permute-start(bf16[16,32,128]{2,1,0:T(8,128)(2,1)S(1)} %shard_map.86), channel_id=1, source_target_pairs={{0,1},{1,0},{2,3},{3,2},{4,5},{5,4},{6,7},{7,6},{8,9},{9,8},{10,11... | collective-permute-start | bytes 393224 | tf_op jit(solution)/shard_map/ppermute | solution.py:31
  76.9 1.0 collective-permute-done.5.refs_0_.refs_1_
  77.9 2.2 %collective-permute-start.6 = (bf16[8,32,128]{2,1,0:T(8,128)(2,1)S(1)}, bf16[8,32,128]{2,1,0:T(8,128)(2,1)S(1)}, u32[]{:S(2)}, u32[]{:S(2)}) collective-permute-start(bf16[8,32,128]{2,1,0:T(8,128)(2,1)S(1)} %shard_map.87), channel_id=1, source_target_pairs={{0,64},{32,96},{64,0},{96,32},{128,192},{160,224},{192,128},{224,1... | collective-permute-start | bytes 196616 | tf_op jit(solution)/shard_map/ppermute | solution.py:31
  80.1 2.2 %shard_map.88 = (bf16[15,2,4,128,128]{4,3,2,1,0:T(8,128)(2,1)S(1)}, bf16[6,2,128,128]{3,2,1,0:T(8,128)(2,1)S(1)}) custom-call(bf16[15,2,4,128,128]{4,3,2,1,0:T(8,128)(2,1)} %refs_0_.1, bf16[6,2,128,128]{3,2,1,0:T(8,128)(2,1)} %refs_1_.3), custom_call_target="tpu_custom_call" | custom-call | bytes 4000000 | tf_op jit(solution)/shard_map/pallas_call | solution.py:306
  84.0 13.9 %all_to_all.54.own.refs_0_ = bf16[64,32,128]{2,1,0:T(8,128)(2,1)S(1)} all-to-all(bf16[64,32,128]{2,1,0:T(8,128)(2,1)S(1)} %get-tuple-element.92), channel_id=1, replica_groups={{0,2,4,6,8,10,12,14,16,18,20,22,24,26,28,30,32,34,36,38,40,42,44,46,48,..., dimensions={0} | all-to-all | bytes 1048576 | tf_op jit(solution)/shard_map/all_to_all | solution.py:37
  97.9 2.6 %collective-permute-start.7 = (bf16[16,32,128]{2,1,0:T(8,128)(2,1)S(1)}, bf16[16,32,128]{2,1,0:T(8,128)(2,1)S(1)}, u32[]{:S(2)}, u32[]{:S(2)}) collective-permute-start(bf16[16,32,128]{2,1,0:T(8,128)(2,1)S(1)} %shard_map.92), channel_id=1, source_target_pairs={{0,1},{1,0},{2,3},{3,2},{4,5},{5,4},{6,7},{7,6},{8,9},{9,8},{10,11... | collective-permute-start | bytes 393224 | tf_op jit(solution)/shard_map/ppermute | solution.py:31
  100.5 1.0 collective-permute-done.7.refs_0_.refs_1_
  102.0 2.0 %collective-permute-start.8 = (bf16[8,32,128]{2,1,0:T(8,128)(2,1)S(1)}, bf16[8,32,128]{2,1,0:T(8,128)(2,1)S(1)}, u32[]{:S(2)}, u32[]{:S(2)}) collective-permute-start(bf16[8,32,128]{2,1,0:T(8,128)(2,1)S(1)} %shard_map.93), channel_id=1, source_target_pairs={{0,64},{32,96},{64,0},{96,32},{128,192},{160,224},{192,128},{224,1... | collective-permute-start | bytes 196616 | tf_op jit(solution)/shard_map/ppermute | solution.py:31
  103.9 2.1 %shard_map.94.off = bf16[15,2,4,128,128]{4,3,2,1,0:T(8,128)(2,1)S(1)} custom-call(bf16[15,2,4,128,128]{4,3,2,1,0:T(8,128)(2,1)} %refs_0_.2), custom_call_target="tpu_custom_call" | custom-call | bytes 4000000 | tf_op jit(solution)/shard_map/pallas_call | solution.py:306
  106.8 1.1 collective-permute-done.8.refs_2_
  108.0 13.8 %all_to_all.55.own.refs_0_.refs_2_ = bf16[64,32,128]{2,1,0:T(8,128)(2,1)S(1)} all-to-all(bf16[64,32,128]{2,1,0:T(8,128)(2,1)S(1)} %get-tuple-element.102), channel_id=1, replica_groups={{0,2,4,6,8,10,12,14,16,18,20,22,24,26,28,30,32,34,36,38,40,42,44,46,48,..., dimensions={0} | all-to-all | bytes 1048576 | tf_op jit(solution)/shard_map/all_to_all | solution.py:37
  121.9 2.6 %collective-permute-start.10 = (bf16[8,32,128]{2,1,0:T(8,128)(2,1)S(1)}, bf16[8,32,128]{2,1,0:T(8,128)(2,1)S(1)}, u32[]{:S(2)}, u32[]{:S(2)}) collective-permute-start(bf16[8,32,128]{2,1,0:T(8,128)(2,1)S(1)} %shard_map.99), channel_id=1, source_target_pairs={{0,1},{1,0},{2,3},{3,2},{4,5},{5,4},{6,7},{7,6},{8,9},{9,8},{10,11... | collective-permute-start | bytes 196616 | tf_op jit(solution)/shard_map/ppermute | solution.py:31
  125.5 11.0 %all_to_all.56.refs_0_.refs_4_ = bf16[32,32,128]{2,1,0:T(8,128)(2,1)S(1)} all-to-all(bf16[32,32,128]{2,1,0:T(8,128)(2,1)S(1)} %get-tuple-element.105), channel_id=1, replica_groups={{0,2,4,6,8,10,12,14,16,18,20,22,24,26,28,30},{1,3,5,7,9,11,13,15,17,19,..., dimensions={0} | all-to-all | bytes 524288 | tf_op jit(solution)/shard_map/all_to_all | solution.py:37
  136.6 1.9 %collective-permute-start.12 = (bf16[32,32,128]{2,1,0:T(8,128)(2,1)S(1)}, bf16[32,32,128]{2,1,0:T(8,128)(2,1)S(1)}, u32[]{:S(2)}, u32[]{:S(2)}) collective-permute-start(bf16[32,32,128]{2,1,0:T(8,128)(2,1)S(1)} %all_to_all.56.refs_0_.refs_4_), channel_id=1, source_target_pairs={{0,1},{1,0},{2,3},{3,2},{4,5},{5,4},{6,7},{7,6},{8,9},{9,8},{10,11... | collective-permute-start | bytes 786440 | tf_op jit(solution)/shard_map/ppermute | solution.py:31
  138.8 0.8 collective-permute-done.12.refs_1_.refs_5_
  139.8 8.0 %all_to_all.57.refs_0_ = bf16[16,32,128]{2,1,0:T(8,128)(2,1)S(1)} all-to-all(bf16[16,32,128]{2,1,0:T(8,128)(2,1)S(1)} %get-tuple-element.108), channel_id=1, replica_groups={{0,2,4,6,8,10,12,14},{1,3,5,7,9,11,13,15},{16,18,20,22,24,26,28,30},{17..., dimensions={0} | all-to-all | bytes 262144 | tf_op jit(solution)/shard_map/all_to_all | solution.py:37
  147.8 1.5 collective-permute-start.13
  150.5 8.0 %all_to_all.58.refs_2_ = bf16[16,32,128]{2,1,0:T(8,128)(2,1)S(1)} all-to-all(bf16[16,32,128]{2,1,0:T(8,128)(2,1)S(1)} %get-tuple-element.113), channel_id=1, replica_groups={{0,1,2,3,4,5,6,7},{8,9,10,11,12,13,14,15},{16,17,18,19,20,21,22,23},{24..., dimensions={0} | all-to-all | bytes 262144 | tf_op jit(solution)/shard_map/all_to_all | solution.py:37
  158.5 0.9 shard_map.106
  (43 shorter events, 9.3 us)
Async XLA Ops:
  1.7 11.8 %all-to-all-start = ((bf16[16,32,128]{2,1,0:T(8,128)(2,1)}), bf16[16,32,128]{2,1,0:T(8,128)(2,1)S(1)}, u32[]{:S(2)}, u32[]{:S(2)}) async-start(bf16[16,32,128]{2,1,0:T(8,128)(2,1)} %get-tuple-element.62), calls=%async_computation | async-start | bytes 262144 | tf_op jit(solution)/shard_map/all_to_all | solution.py:37
  8.2 4.6 %collective-permute-start = (s32[4,4,15]{2,1,0:T(4,128)S(1)}, s32[4,4,15]{2,1,0:T(4,128)S(1)}, u32[]{:S(2)}, u32[]{:S(2)}) collective-permute-start(s32[4,4,15]{2,1,0:T(4,128)S(1)} %get-tuple-element.63), channel_id=1, source_target_pairs={{0,64},{32,96},{64,0},{96,32},{128,192},{160,224},{192,128},{224,1... | collective-permute-start | bytes 2888 | tf_op jit(solution)/shard_map/ppermute | solution.py:31
  23.5 3.2 %collective-permute-start.1 = (bf16[16,32,128]{2,1,0:T(8,128)(2,1)S(1)}, bf16[16,32,128]{2,1,0:T(8,128)(2,1)S(1)}, u32[]{:S(2)}, u32[]{:S(2)}) collective-permute-start(bf16[16,32,128]{2,1,0:T(8,128)(2,1)S(1)} %all_to_all.50.refs_0_.refs_1_), channel_id=1, source_target_pairs={{0,1},{1,0},{2,3},{3,2},{4,5},{5,4},{6,7},{7,6},{8,9},{9,8},{10,11... | collective-permute-start | bytes 393224 | tf_op jit(solution)/shard_map/ppermute | solution.py:31
  25.5 1.2 collective-permute-start.2
  38.8 3.0 %collective-permute-start.3 = (bf16[32,32,128]{2,1,0:T(8,128)(2,1)S(1)}, bf16[32,32,128]{2,1,0:T(8,128)(2,1)S(1)}, u32[]{:S(2)}, u32[]{:S(2)}) collective-permute-start(bf16[32,32,128]{2,1,0:T(8,128)(2,1)S(1)} %all_to_all.51.refs_0_.refs_3_), channel_id=1, source_target_pairs={{0,1},{1,0},{2,3},{3,2},{4,5},{5,4},{6,7},{7,6},{8,9},{9,8},{10,11... | collective-permute-start | bytes 786440 | tf_op jit(solution)/shard_map/ppermute | solution.py:31
  57.0 3.4 %collective-permute-start.4 = (bf16[16,32,128]{2,1,0:T(8,128)(2,1)S(1)}, bf16[16,32,128]{2,1,0:T(8,128)(2,1)S(1)}, u32[]{:S(2)}, u32[]{:S(2)}) collective-permute-start(bf16[16,32,128]{2,1,0:T(8,128)(2,1)S(1)} %shard_map.84), channel_id=1, source_target_pairs={{0,1},{1,0},{2,3},{3,2},{4,5},{5,4},{6,7},{7,6},{8,9},{9,8},{10,11... | collective-permute-start | bytes 393224 | tf_op jit(solution)/shard_map/ppermute | solution.py:31
  74.5 3.4 %collective-permute-start.5 = (bf16[16,32,128]{2,1,0:T(8,128)(2,1)S(1)}, bf16[16,32,128]{2,1,0:T(8,128)(2,1)S(1)}, u32[]{:S(2)}, u32[]{:S(2)}) collective-permute-start(bf16[16,32,128]{2,1,0:T(8,128)(2,1)S(1)} %shard_map.86), channel_id=1, source_target_pairs={{0,1},{1,0},{2,3},{3,2},{4,5},{5,4},{6,7},{7,6},{8,9},{9,8},{10,11... | collective-permute-start | bytes 393224 | tf_op jit(solution)/shard_map/ppermute | solution.py:31
  77.9 5.9 %collective-permute-start.6 = (bf16[8,32,128]{2,1,0:T(8,128)(2,1)S(1)}, bf16[8,32,128]{2,1,0:T(8,128)(2,1)S(1)}, u32[]{:S(2)}, u32[]{:S(2)}) collective-permute-start(bf16[8,32,128]{2,1,0:T(8,128)(2,1)S(1)} %shard_map.87), channel_id=1, source_target_pairs={{0,64},{32,96},{64,0},{96,32},{128,192},{160,224},{192,128},{224,1... | collective-permute-start | bytes 196616 | tf_op jit(solution)/shard_map/ppermute | solution.py:31
  97.9 3.6 %collective-permute-start.7 = (bf16[16,32,128]{2,1,0:T(8,128)(2,1)S(1)}, bf16[16,32,128]{2,1,0:T(8,128)(2,1)S(1)}, u32[]{:S(2)}, u32[]{:S(2)}) collective-permute-start(bf16[16,32,128]{2,1,0:T(8,128)(2,1)S(1)} %shard_map.92), channel_id=1, source_target_pairs={{0,1},{1,0},{2,3},{3,2},{4,5},{5,4},{6,7},{7,6},{8,9},{9,8},{10,11... | collective-permute-start | bytes 393224 | tf_op jit(solution)/shard_map/ppermute | solution.py:31
  101.5 6.3 %collective-permute-start.9 = (bf16[64,32,128]{2,1,0:T(8,128)(2,1)S(1)}, bf16[64,32,128]{2,1,0:T(8,128)(2,1)S(1)}, u32[]{:S(2)}, u32[]{:S(2)}) collective-permute-start(bf16[64,32,128]{2,1,0:T(8,128)(2,1)S(1)} %all_to_all.54.own.refs_0_), channel_id=1, source_target_pairs={{0,1},{1,0},{2,3},{3,2},{4,5},{5,4},{6,7},{7,6},{8,9},{9,8},{10,11... | collective-permute-start | bytes 1572872 | tf_op jit(solution)/shard_map/ppermute | solution.py:31
  102.0 5.9 %collective-permute-start.8 = (bf16[8,32,128]{2,1,0:T(8,128)(2,1)S(1)}, bf16[8,32,128]{2,1,0:T(8,128)(2,1)S(1)}, u32[]{:S(2)}, u32[]{:S(2)}) collective-permute-start(bf16[8,32,128]{2,1,0:T(8,128)(2,1)S(1)} %shard_map.93), channel_id=1, source_target_pairs={{0,64},{32,96},{64,0},{96,32},{128,192},{160,224},{192,128},{224,1... | collective-permute-start | bytes 196616 | tf_op jit(solution)/shard_map/ppermute | solution.py:31
  121.9 3.5 %collective-permute-start.10 = (bf16[8,32,128]{2,1,0:T(8,128)(2,1)S(1)}, bf16[8,32,128]{2,1,0:T(8,128)(2,1)S(1)}, u32[]{:S(2)}, u32[]{:S(2)}) collective-permute-start(bf16[8,32,128]{2,1,0:T(8,128)(2,1)S(1)} %shard_map.99), channel_id=1, source_target_pairs={{0,1},{1,0},{2,3},{3,2},{4,5},{5,4},{6,7},{7,6},{8,9},{9,8},{10,11... | collective-permute-start | bytes 196616 | tf_op jit(solution)/shard_map/ppermute | solution.py:31
  124.7 13.7 %collective-permute-start.11 = (bf16[64,32,128]{2,1,0:T(8,128)(2,1)S(1)}, bf16[64,32,128]{2,1,0:T(8,128)(2,1)S(1)}, u32[]{:S(2)}, u32[]{:S(2)}) collective-permute-start(bf16[64,32,128]{2,1,0:T(8,128)(2,1)S(1)} %all_to_all.55.own.refs_0_.refs_2_), channel_id=1, source_target_pairs={{0,1},{1,0},{2,3},{3,2},{4,5},{5,4},{6,7},{7,6},{8,9},{9,8},{10,11... | collective-permute-start | bytes 1572872 | tf_op jit(solution)/shard_map/ppermute | solution.py:31
  136.6 3.0 %collective-permute-start.12 = (bf16[32,32,128]{2,1,0:T(8,128)(2,1)S(1)}, bf16[32,32,128]{2,1,0:T(8,128)(2,1)S(1)}, u32[]{:S(2)}, u32[]{:S(2)}) collective-permute-start(bf16[32,32,128]{2,1,0:T(8,128)(2,1)S(1)} %all_to_all.56.refs_0_.refs_4_), channel_id=1, source_target_pairs={{0,1},{1,0},{2,3},{3,2},{4,5},{5,4},{6,7},{7,6},{8,9},{9,8},{10,11... | collective-permute-start | bytes 786440 | tf_op jit(solution)/shard_map/ppermute | solution.py:31
  147.8 2.5 %collective-permute-start.13 = (bf16[16,32,128]{2,1,0:T(8,128)(2,1)S(1)}, bf16[16,32,128]{2,1,0:T(8,128)(2,1)S(1)}, u32[]{:S(2)}, u32[]{:S(2)}) collective-permute-start(bf16[16,32,128]{2,1,0:T(8,128)(2,1)S(1)} %all_to_all.57.refs_0_), channel_id=1, source_target_pairs={{0,1},{1,0},{2,3},{3,2},{4,5},{5,4},{6,7},{7,6},{8,9},{9,8},{10,11... | collective-permute-start | bytes 393224 | tf_op jit(solution)/shard_map/ppermute | solution.py:31

commit v6 on v4

--- a/solution.py
+++ b/solution.py
@@ -79,26 +79,27 @@
     )
 
 
-def block(own, other, local, core):
-    index = (local >> 2 << 1) | (local & 1)
-    return jnp.where((local >> 1 & 1) == core, own[index], other[index])
+def half_of(value, me):
+    half = value.shape[0] // 2
+    return jnp.where(me[CORE] == 0, value[:half], value[half:])
 
 
 def read(kind, start, refs, me, wanted, slot):
+    local = wanted if start == NONE else wanted + me[start]
     if kind == "one":
-        return refs[0][wanted]
+        return refs[0][local]
     if kind == "halves":
-        local = wanted if start == NONE else wanted + me[start]
-        return block(refs[0], refs[1], local, me[CORE])
-    near = mixed(refs[0], refs[1], wanted & DUO_BLOCKS - 1, me[CORE], start + slot)
-    if kind == "core":
-        return near
-    return jnp.where(wanted >> DUO_BITS == me[DUO], near, refs[2][slot])
-
-
-def mixed(own, sent, local, core, slot):
-    index = (local >> 2 << 1) | (local & 1)
-    return jnp.where((local >> 1 & 1) == core, own[index], sent[slot])
+        index = (local >> 2 << 1) | (local & 1)
+        own = (local >> 1 & 1) == me[CORE]
+        return jnp.where(own, refs[0][index], refs[1][index])
+    if kind == "cols":
+        return refs[0][at_chip(local, me)]
+    near = refs[0][at_chip(local & DUO_BLOCKS - 1, me)]
+    return jnp.where(wanted >> DUO_BITS == me[DUO], near, refs[1][slot])
+
+
+def at_chip(local, me):
+    return local ^ (me[CORE] << 1)
 
 
 def send(ref, totals):
@@ -108,8 +109,8 @@
             ref[2 * way + j] = values[j]
 
 
-FIRST = (14, 13, 9, 12, 8, 5, 11, 7, 4, 2)
-BUFFERS = {"one": 1, "halves": 2, "core": 2, "far": 3}
+FIRST = (13, 9, 12, 8, 5, 11, 7, 4, 2)
+BUFFERS = {"one": 1, "halves": 2, "cols": 1, "far": 2}
 
 
 def coupled(total, j, plan, near, side, kept, me, table, off):
@@ -168,6 +169,72 @@
             flops=products * 2 * 32 * 128 * 128, bytes_accessed=products * 32768, transcendentals=0
         ),
     )(*arguments)
+
+
+def solve_kernel(plan, side, kept, first, level, inverses, ways, me, table, peers, *refs):
+    refs = list(refs)
+    off = (refs.pop(0), refs.pop(0))
+    base = [refs.pop(0) for _ in range(2 if first is not None else 1)]
+    near = [[refs.pop(0) for _ in range(BUFFERS[entry[0]])] for entry in plan]
+    inverse = [(refs.pop(0), refs.pop(0)) for _ in range(inverses)]
+    totals = []
+    for row in range(4):
+        whose, j = divmod(row, 2)
+        if first is None:
+            total = base[0][row]
+        else:
+            whole = base[whose][first, j] if len(base[whose].shape) == 4 else base[whose][j]
+            total = half_of(whole, me)
+        for (kind, p, start), buffers in zip(plan, near):
+            at = kept.index(p) if kept else p
+            picked = []
+            for n in range(4):
+                place = (2 * side + j, n, p)
+                wanted = table[place] if whose == 0 else peers[(MATE,) + place]
+                value = read(kind, start, buffers, me, wanted, 4 * row + n)
+                picked.append(half_of(value, me) if kind in ("one", "halves") else value)
+            total = total - jnp.dot(
+                jnp.concatenate(picked, 1),
+                off[whose][at, j].reshape(512, 128),
+                preferred_element_type=jnp.float32,
+            )
+        totals.append(total)
+    for matrices in inverse:
+        totals = [times(totals[row], matrices[row // 2][level, row % 2]) for row in range(4)]
+    for row in range(4):
+        refs[0][row] = totals[row]
+    if ways:
+        values = [total.astype(jnp.bfloat16) for total in totals]
+        for way in range(ways):
+            for row in range(4):
+                refs[1][4 * way + row] = values[row]
+
+
+def solve(me, table, peers, off, base, first, plan, near, side, level=0, inverse=(), ways=0, kept=None):
+    bases = list(base) if first is not None else [base]
+    rows = bases[0].shape[-2] // 2 if first is not None else base.shape[-2]
+    shape = (4, rows, bases[0].shape[-1])
+    shapes = [jax.ShapeDtypeStruct(shape, jnp.float32)]
+    if ways:
+        shapes.append(jax.ShapeDtypeStruct((4 * ways,) + shape[1:], jnp.bfloat16))
+    arguments = [in_vmem(array) for array in list(off) + bases]
+    for buffers in near:
+        arguments += list(buffers)
+    for matrices in inverse:
+        arguments += [in_vmem(matrix) for matrix in matrices]
+    products = 4 * (4 * len(plan) + len(inverse))
+    return pl.pallas_call(
+        functools.partial(
+            solve_kernel, tuple(plan), side, kept, first, level, len(inverse), ways
+        ),
+        out_shape=shapes,
+        in_specs=[SMEM] * 3 + [VMEM] * len(arguments),
+        out_specs=[VMEM] * len(shapes),
+        compiler_params=PARAMS,
+        cost_estimate=pl.CostEstimate(
+            flops=products * 2 * 16 * 128 * 128, bytes_accessed=products * 32768, transcendentals=0
+        ),
+    )(in_smem(me), in_smem(table), in_smem(peers), *arguments)
 
 
 def first_kernel(level, base, matrix, lower, upper, out, low, joined, right, inverse, sems):
@@ -211,42 +278,49 @@
     )(in_hbm(right_sides), in_hbm(inverse), in_hbm(lower), in_hbm(upper))
 
 
-def last_kernel(plan, level, me, table, off, base, *refs):
-    refs = list(refs)
-    near = [[refs.pop(0) for _ in range(BUFFERS[entry[0]])] for entry in plan]
-    inverse = refs.pop(0)
-    out, result, sems = refs[-3:]
-    copies = [
-        pltpu.make_async_copy(ref, out.at[at], sems.at[at]) for at, ref in enumerate(refs[:-3])
-    ]
+def pack_kernel(*refs):
+    for level, ref in enumerate(refs[:-1]):
+        refs[-1][level] = ref[2:]
+
+
+def pack(solved):
+    shape = solved[0].shape
+    return pl.pallas_call(
+        pack_kernel,
+        out_shape=jax.ShapeDtypeStruct((len(solved), shape[0] - 2) + shape[1:], jnp.float32),
+        in_specs=[VMEM] * len(solved),
+        out_specs=VMEM,
+        compiler_params=PARAMS,
+    )(*[in_vmem(value) for value in solved])
+
+
+def last_kernel(me, sent, *refs):
+    out, sems = refs[-2:]
+    half = sent.shape[-2]
+    mine = pl.ds(pl.multiple_of(me[CORE] * half, half), half)
+    other = pl.ds(pl.multiple_of((1 - me[CORE]) * half, half), half)
+    copies = []
+    for level, ref in enumerate(refs[:-2]):
+        for j in range(2):
+            for source, cols in ((ref.at[j], mine), (sent.at[level, j], other)):
+                target = out.at[level, j, cols]
+                copies.append(pltpu.make_async_copy(source, target, sems.at[len(copies)]))
     for copy in copies:
         copy.start()
-    totals = [coupled(base[j], j, plan, near, 1, None, me, table, off) for j in range(2)]
-    for j in range(2):
-        result[j] = times(totals[j], inverse[level, j])
-    copies.append(pltpu.make_async_copy(result, out.at[level], sems.at[level]))
-    copies[-1].start()
     for copy in copies:
         copy.wait()
 
 
-def last_update(me, table, off, base, plan, near, inverse, solved):
-    levels = len(solved) + 1
-    arguments = [in_smem(me), in_smem(table), in_vmem(off), in_vmem(base)]
-    for buffers in near:
-        arguments += list(buffers)
-    arguments += [in_vmem(inverse)] + [in_vmem(value) for value in solved]
-    return pl.pallas_call(
-        functools.partial(last_kernel, tuple(plan), levels - 1),
-        out_shape=jax.ShapeDtypeStruct((levels,) + base.shape, jnp.float32),
-        in_specs=[SMEM, SMEM] + [VMEM] * (len(arguments) - 2),
+def last_update(me, sent, solved):
+    levels, rows, half, width = sent.shape
+    return pl.pallas_call(
+        last_kernel,
+        out_shape=jax.ShapeDtypeStruct((levels, rows, 2 * half, width), jnp.float32),
+        in_specs=[SMEM] + [VMEM] * (1 + levels),
         out_specs=HBM,
-        scratch_shapes=[
-            pltpu.VMEM(base.shape, jnp.float32),
-            pltpu.SemaphoreType.DMA((levels,)),
-        ],
-        compiler_params=PARAMS,
-    )(*arguments)
+        scratch_shapes=[pltpu.SemaphoreType.DMA((4 * levels,))],
+        compiler_params=PARAMS,
+    )(in_smem(me), in_vmem(sent), *[in_vmem(value) for value in solved])
 
 
 def stage_kernel(plan, count, *refs):
@@ -273,7 +347,7 @@
             size = part.shape[0]
             whole = rows is None and len(parts) == 1
             plan.append((len(arrays), size, rows, out, None if whole else at))
-            arrays.append(part if part.ndim < 3 else in_hbm(part))
+            arrays.append(in_hbm(part) if part.ndim == 3 or space is pltpu.VMEM else part)
             copies += len(rows) if rows else 1
             at += len(rows) if rows else size
         shapes.append(space((at,) + parts[0].shape[1:], parts[0].dtype))
@@ -292,34 +366,28 @@
     )(*arrays)
 
 
-def pick_kernel(plan, side, me, table, own, *refs):
-    sent, out = refs if len(refs) == 2 else (None, refs[0])
-    for at, (peer, p) in enumerate(plan):
-        for j in range(2):
-            for n in range(4):
-                local = table[peer, 2 * side + j, n, p] & DUO_BLOCKS - 1
-                slot = 4 * j + n
-                if sent is None:
-                    out[8 * at + slot] = own[(local >> 2 << 1) | (local & 1)]
-                else:
-                    out[8 * at + slot] = mixed(own, sent, local, me[CORE], 8 + slot)
-
-
-def pick(me, table, plan, side, own, *sent):
-    return pl.pallas_call(
-        functools.partial(pick_kernel, tuple(plan), side),
-        out_shape=jax.ShapeDtypeStruct((8 * len(plan),) + own.shape[1:], jnp.bfloat16),
-        in_specs=[SMEM, SMEM, VMEM] + [VMEM] * len(sent),
+def pick_kernel(side, me, peers, near, out):
+    for row in range(4):
+        whose, j = divmod(row, 2)
+        peer = (ACROSS, MATE_ACROSS)[whose]
+        for n in range(4):
+            local = peers[peer, 2 * side + j, n, 0] & DUO_BLOCKS - 1
+            out[4 * row + n] = near[at_chip(local, me)]
+
+
+def pick(me, peers, side, near):
+    return pl.pallas_call(
+        functools.partial(pick_kernel, side),
+        out_shape=jax.ShapeDtypeStruct((16,) + near.shape[1:], jnp.bfloat16),
+        in_specs=[SMEM, SMEM, VMEM],
         out_specs=VMEM,
         compiler_params=PARAMS,
-        cost_estimate=pl.CostEstimate(
-            flops=0, bytes_accessed=131072 * len(plan), transcendentals=0
-        ),
-    )(in_smem(me), in_smem(table), own, *sent)
-
-
-def halves(p, start=NONE):
-    return ("halves", p, start)
+        cost_estimate=pl.CostEstimate(flops=0, bytes_accessed=131072, transcendentals=0),
+    )(in_smem(me), in_smem(peers), near)
+
+
+def cols(p, start=NONE):
+    return ("cols", p, start)
 
 
 def on_device(
@@ -331,109 +399,128 @@
     tables = [x.transpose(1, 2, 0) for x in (lower_pattern, upper_pattern)]
     f5, sent, mine = first_update(right_sides, lower_inv, *tables, 8)
     across = swapped(mine, "group", 2)
-    right, lower_inv, off_first, table, me = staged(
+    lower_all, inverse_all = after(lower_off, sent), lower_inv
+    right, lower_inv, off14, off_first, table, me = staged(
         (pltpu.VMEM, [after(right_sides, sent)], None),
         (pltpu.VMEM, [lower_inv], None),
+        (pltpu.VMEM, [lower_off], (14,)),
         (pltpu.VMEM, [lower_off], FIRST),
         (pltpu.SMEM, tables, None),
         (pltpu.SMEM, [positions(sub, group)], None),
     )
     near5, across, me = lax.optimization_barrier((spread(sent, (1, 2, 4)), across, me))
-    near5 = (near5,)
-    low = functools.partial(update, me, table, off_first, side=0, kept=FIRST)
-
-    f4, sent = low(right, 4, [("one", 14, NONE)], [near5], level=4, inverse=[lower_inv], ways=8)
-    near4 = collected(sent, square)
+    f4, sent = update(
+        me, table, off14, right, 4, [("one", 14, NONE)], [(near5,)], 0, 4, [lower_inv], 8, (14,)
+    )
+    theirs = [swapped(x, "sub", 1) for x in (right_sides, lower_all, inverse_all, upper_inv)]
+    near4, *theirs = lax.optimization_barrier((spread(sent, square), *theirs))
+    near4 = (near4, swapped(near4, "sub", 1))
     mates = swapped(after(jnp.stack([mine, across]), near4[0]), "sub", 1)
-    (r3,) = low(after(right, near4[0]), 3, [("one", 13, NONE)], [near5])
-    near4 = (near4[0], after(near4[1], mates))
-    f3, sent = low(r3, None, [halves(9)], [near4], level=3, inverse=[lower_inv], ways=16)
-    near3 = collected(sent, plane)
-    (peers,) = staged((pltpu.SMEM, [after(across[None], near3[0]), mates], None))
-    (r2,) = low(after(right, near3[0]), 2, [("one", 12, NONE), halves(8)], [near5, near4])
-    near3 = (near3[0], after(near3[1], peers))
-    f2, sent = low(r2, None, [halves(5)], [near3], level=2, inverse=[lower_inv], ways=32)
-    own2 = spread(sent, duo)
-    near2 = (own2, swapped(pick(me, peers, [(MATE, 2), (MATE, 1)], 0, own2), "sub", 1))
-    (r1,) = low(
-        after(right, own2), 1, [("one", 11, NONE), halves(7), halves(4)], [near5, near4, near3]
-    )
-    f1, sent = low(r1, None, [("core", 2, 0)], [near2], level=1, inverse=[lower_inv], ways=32)
-    own1 = spread(sent, duo)
-    near1 = (own1, swapped(pick(me, peers, [(MATE, 0), (MATE_ACROSS, 0)], 0, own1), "sub", 1))
-    sent = pick(me, peers, [(ACROSS, 0)], 0, *near1)
+    f4_mate = swapped(after(f4, near4[0]), "sub", 1)
+    f5_mate = swapped(after(f5, near4[0]), "sub", 1)
+    peers, right_mate, inv_mate, off_mate = staged(
+        (pltpu.SMEM, [across[None], mates], None),
+        (pltpu.VMEM, [theirs[0]], None),
+        (pltpu.VMEM, [theirs[2]], None),
+        (pltpu.VMEM, [theirs[1]], FIRST),
+    )
+    near4 = (near4[0], after(near4[1], right_mate, f4_mate, f5_mate))
+
+    low = functools.partial(
+        solve, me, table, peers, (off_first, off_mate), side=0, kept=FIRST, inverse=[(lower_inv, inv_mate)]
+    )
+    right = (right, right_mate)
+    f3, sent = low(
+        right, 3, [("one", 13, NONE), ("halves", 9, NONE)], [(near5,), near4], level=3, ways=16
+    )
+    near3 = (spread(sent, plane),)
+    f2, sent = low(
+        right,
+        2,
+        [("one", 12, NONE), ("halves", 8, NONE), cols(5)],
+        [(near5,), near4, near3],
+        level=2,
+        ways=32,
+    )
+    near2 = (spread(sent, duo),)
+    f1, sent = low(
+        right,
+        1,
+        [("one", 11, NONE), ("halves", 7, NONE), cols(4), cols(2)],
+        [(near5,), near4, near3, near2],
+        level=1,
+        ways=32,
+    )
+    near1 = spread(sent, duo)
+    sent = pick(me, peers, 0, near1)
     far = swapped(sent, "group", 2)
-    lower_off, upper_inv, upper_first = staged(
+    lower_off, low_mate, upper_inv, up_inv_mate = staged(
         (pltpu.VMEM, [after(lower_off, sent)], None),
+        (pltpu.VMEM, [theirs[1]], None),
         (pltpu.VMEM, [upper_inv], None),
-        (pltpu.VMEM, [upper_off], (0,)),
-    )
-    low = functools.partial(update, me, table, lower_off, side=0)
+        (pltpu.VMEM, [theirs[3]], None),
+    )
+    low = functools.partial(solve, me, table, peers, (lower_off, low_mate), side=0)
     (r0,) = low(
         right,
         0,
-        [("one", 10, NONE), halves(6), halves(3), ("core", 1, 8)],
-        [near5, near4, near3, near2],
-    )
-    far, upper_first = lax.optimization_barrier((far, upper_first))
+        [("one", 10, NONE), ("halves", 6, NONE), cols(3), cols(1)],
+        [(near5,), near4, near3, near2],
+    )
+    far, r0 = lax.optimization_barrier((far, r0))
     s0, sent = low(
         r0,
         None,
-        [("far", 0, 0)],
-        [near1 + (far,)],
+        [("far", 0, NONE)],
+        [(near1, far)],
         level=0,
-        inverse=[lower_inv, upper_inv],
+        inverse=[(lower_inv, inv_mate), (upper_inv, up_inv_mate)],
         ways=32,
     )
 
-    own0 = spread(sent, duo)
-    near0 = (own0, swapped(pick(me, peers, [(MATE, 0), (MATE_ACROSS, 0)], 1, own0), "sub", 1))
-    sent = pick(me, peers, [(ACROSS, 0)], 1, *near0)
+    up_mate = swapped(upper_off, "sub", 1)
+    near0 = spread(sent, duo)
+    sent = pick(me, peers, 1, near0)
     far = swapped(sent, "group", 2)
-    (upper_off,) = staged((pltpu.VMEM, [after(upper_off, sent)], None))
-    other0 = swapped(after(own0, sent), "sub", 1)
-    far, upper_off, other0 = lax.optimization_barrier((far, upper_off, other0))
-    up = functools.partial(update, me, table, upper_off, side=1)
-    s1, sent = up(
-        f1, None, [("far", 0, 0)], [near0 + (far,)], level=1, inverse=[upper_inv], ways=32
-    )
-    near0 = (own0, other0)
-    own1 = spread(sent, duo)
-    near1 = (own1, swapped(pick(me, peers, [(MATE, 2)], 1, own1), "sub", 1))
-    (r2,) = up(after(f2, own1), None, [halves(1)], [near0])
-    s2, sent = up(r2, None, [("core", 2, 0)], [near1], level=2, inverse=[upper_inv], ways=16)
-    near1 = (own1, swapped(after(own1, sent), "sub", 1))
-    near2 = collected(sent, plane)
-    (r3,) = up(
-        after(f3, near2[0]), None, [halves(3, PLANE64), halves(4, PLANE64)], [near0, near1]
-    )
-    s3, sent = up(r3, None, [halves(5)], [near2], level=3, inverse=[upper_inv], ways=8)
-    near3 = collected(sent, square)
-    (r4,) = up(
-        after(f4, near3[0]),
+    upper_off, up_mate = staged(
+        (pltpu.VMEM, [after(upper_off, sent)], None), (pltpu.VMEM, [after(up_mate, sent)], None)
+    )
+    far, upper_off = lax.optimization_barrier((far, upper_off))
+    up = functools.partial(
+        solve, me, table, peers, (upper_off, up_mate), side=1, inverse=[(upper_inv, up_inv_mate)]
+    )
+    s1, sent = up(f1, None, [("far", 0, NONE)], [(near0, far)], level=1, ways=32)
+    near0, near1 = (near0,), (spread(sent, duo),)
+    s2, sent = up(f2, None, [cols(1), cols(2)], [near0, near1], level=2, ways=16)
+    near2 = (spread(sent, plane),)
+    s3, sent = up(
+        f3,
         None,
-        [halves(6, SIXTEEN64), halves(7, SIXTEEN64), halves(8, SIXTEEN32)],
+        [cols(3, PLANE64), cols(4, PLANE64), cols(5)],
         [near0, near1, near2],
-    )
-    (r5,) = up(
-        after(f5, near3[0]),
-        None,
-        [halves(10, EIGHT64), halves(11, EIGHT64), halves(12, EIGHT32)],
-        [near0, near1, near2],
-    )
-    near3 = (near3[0], after(near3[1], r5))
-    s4, sent = up(r4, None, [halves(9)], [near3], level=4, inverse=[upper_inv], ways=8)
-    near4 = (spread(sent, (1, 2, 4)),)
-    return last_update(
-        me,
-        table,
-        upper_off,
-        r5,
-        [halves(13, EIGHT16), ("one", 14, NONE)],
-        [near3, near4],
-        upper_inv,
-        [s0, s1, s2, s3, s4],
-    )
+        level=3,
+        ways=8,
+    )
+    near3 = (spread(sent, square),)
+    s4, sent = up(
+        (f4, f4_mate),
+        0,
+        [cols(6, SIXTEEN64), cols(7, SIXTEEN64), cols(8, SIXTEEN32), cols(9)],
+        [near0, near1, near2, near3],
+        level=4,
+        ways=4,
+    )
+    near4 = (spread(sent, (2, 4)),)
+    (s5,) = up(
+        (f5, f5_mate),
+        0,
+        [cols(10, EIGHT64), cols(11, EIGHT64), cols(12, EIGHT32), cols(13, EIGHT16), cols(14)],
+        [near0, near1, near2, near3, near4],
+        level=5,
+    )
+    solved = [s0, s1, s2, s3, s4, s5]
+    sent = swapped(pack(solved), "sub", 1)
+    return last_update(me, sent, solved)
 
 
 def solution(mesh):

time: 161 us -> 153 us (0.950)
  blocking collectives: 105 us -> 92 us
  Pallas kernels: 15.6 us -> 18.7 us
  starting transfers between devices: 30.9 us -> 32.7 us
    all_to_all x9 -> x8, blocking collectives: 105 us -> 92 us  [spread(): lax.all_to_all(copies, axes, 0, 0, tiled=True, axis_index_groups=groups)]
    all_to_all x1 -> x2, waiting for transfers between devices: 0.69 us -> 5.43 us  [spread(): lax.all_to_all(copies, axes, 0, 0, tiled=True, axis_index_groups=groups)]
    ppermute x14 -> x13, waiting for transfers between devices: 8.02 us -> 3.66 us  [swapped(): lax.ppermute(block, axis, [(i, i ^ mask) for i in range(lax.axis_size(axi...]
    pallas_call x7 -> x14, Pallas kernels: 1.14 us -> 5.37 us  [the longest x10 4.42 us: solve(): pl.pallas_call(functools.partial(solve_kernel, tuple(plan), side, kept, f...]
    pallas_call x17 -> x1, Pallas kernels: 4.57 us -> 0.95 us  [update(): pl.pallas_call(functools.partial(update_kernel, tuple(plan), side, kept,...]
    pallas_call x4, Pallas kernels: 8.21 us -> 10.7 us  [staged(): pl.pallas_call(functools.partial(stage_kernel, tuple(plan), len(arrays)),...]
    all_to_all x1 -> x2, starting transfers between devices: 6.53 us -> 8.75 us  [spread(): lax.all_to_all(copies, axes, 0, 0, tiled=True, axis_index_groups=groups)]
    ppermute x14 -> x13, starting transfers between devices: 24.4 us -> 24 us  [swapped(): lax.ppermute(block, axis, [(i, i ^ mask) for i in range(lax.axis_size(axi...]
  transfers between devices with their start and end apart: 15 -> 15, of which waited for: 10 -> 5; matrix products, arithmetic and copies ran while one was open for 0% -> 0% of each run, Pallas kernels for 6% -> 9%
where the time goes in v6:
time: 153 us
  blocking collectives  92 us (60%)
  starting transfers between devices  32.7 us (21%)
  Pallas kernels  18.7 us (12%)
  waiting for transfers between devices  9.09 us (6%)
    all_to_all x8, blocking collectives, spread(): lax.all_to_all(copies, axes, 0, 0, tiled=True, axis_index_groups=groups)  92 us
    ppermute x13, starting transfers between devices, swapped(): lax.ppermute(block, axis, [(i, i ^ mask) for i in range(lax.axis_size(axi...  24 us
    pallas_call x4, Pallas kernels, staged(): pl.pallas_call(functools.partial(stage_kernel, tuple(plan), len(arrays)),...  10.7 us
    all_to_all x2, starting transfers between devices, spread(): lax.all_to_all(copies, axes, 0, 0, tiled=True, axis_index_groups=groups)  8.75 us
    all_to_all x2, waiting for transfers between devices, spread(): lax.all_to_all(copies, axes, 0, 0, tiled=True, axis_index_groups=groups)  5.43 us
    pallas_call x10, Pallas kernels, solve(): pl.pallas_call(functools.partial(solve_kernel, tuple(plan), side, kept, f...  4.42 us
    ppermute x13, waiting for transfers between devices, swapped(): lax.ppermute(block, axis, [(i, i ^ mask) for i in range(lax.axis_size(axi...  3.66 us
  transfers between devices with their start and end apart: 15, of which 5 were waited for; matrix products, arithmetic and copies ran while one was open for 0% of the time, Pallas kernels for 9%

profile of v6, /device:TPU:1, one launch (start us, length us, event | category | flops | bytes accessed | tf_op | source)
XLA Modules:
  0.0 152.8 jit_solution(15614172034442691121)
XLA Ops:
  0.0 1.7 %shard_map.73 = (f32[2,32,128]{2,1,0:T(8,128)S(1)}, bf16[16,32,128]{2,1,0:T(8,128)(2,1)}, s32[4,4,15]{2,1,0:T(4,128)S(1)}) custom-call(f32[6,2,32,128]{3,2,1,0:T(8,128)} %refs_0_, bf16[6,2,128,128]{3,2,1,0:T(8,128)(2,1)} %refs_1_.1, s32[2,4,15]{2,1,0:T(4,128)} %bitcast.15, s32[2,4,15]{2,1,0:T(4,128)} %bitcast.17), custom_call_target="tpu_custom_call" | custom-call | tf_op jit(solution)/shard_map/pallas_call | solution.py:263
  1.7 3.3 %collective-permute-start.2 = (bf16[15,2,4,128,128]{4,3,2,1,0:T(8,128)(2,1)}, bf16[15,2,4,128,128]{4,3,2,1,0:T(8,128)(2,1)}, u32[]{:S(2)}, u32[]{:S(2)}) collective-permute-start(bf16[15,2,4,128,128]{4,3,2,1,0:T(8,128)(2,1)} %refs_0_.1), channel_id=1, source_target_pairs={{0,1},{1,0},{2,3},{3,2},{4,5},{5,4},{6,7},{7,6},{8,9},{9,8},{10,11... | collective-permute-start | bytes 11796488 | tf_op jit(solution)/shard_map/ppermute | solution.py:31
  5.6 3.7 %all-to-all-start = ((bf16[16,32,128]{2,1,0:T(8,128)(2,1)}), bf16[16,32,128]{2,1,0:T(8,128)(2,1)S(1)}, u32[]{:S(2)}, u32[]{:S(2)}) async-start(bf16[16,32,128]{2,1,0:T(8,128)(2,1)} %get-tuple-element.63), calls=%async_computation | async-start | bytes 262144 | tf_op jit(solution)/shard_map/all_to_all | solution.py:37
  9.3 2.4 %collective-permute-start = (s32[4,4,15]{2,1,0:T(4,128)S(1)}, s32[4,4,15]{2,1,0:T(4,128)S(1)}, u32[]{:S(2)}, u32[]{:S(2)}) collective-permute-start(s32[4,4,15]{2,1,0:T(4,128)S(1)} %get-tuple-element.64), channel_id=1, source_target_pairs={{0,64},{32,96},{64,0},{96,32},{128,192},{160,224},{192,128},{224,1... | collective-permute-start | bytes 2888 | tf_op jit(solution)/shard_map/ppermute | solution.py:31
  11.8 1.0 collective-permute-done
  12.8 1.3 collective-permute-start.1
  14.2 2.0 %shard_map.74 = (f32[6,2,32,128]{3,2,1,0:T(8,128)S(1)}, bf16[6,2,128,128]{3,2,1,0:T(8,128)(2,1)S(1)}, bf16[1,2,4,128,128]{4,3,2,1,0:T(8,128)(2,1)S(1)}, bf16[9,2...) custom-call(f32[6,2,32,128]{3,2,1,0:T(8,128)} %refs_0_, bf16[6,2,128,128]{3,2,1,0:T(8,128)(2,1)} %refs_1_.1, ...), custom_call_target="tpu_custom_call" | custom-call | bytes 4000000 | tf_op jit(solution)/shard_map/pallas_call | solution.py:356
  16.2 0.9 shard_map.75
  17.2 5.1 %all-to-all-start.1 = ((bf16[16,32,128]{2,1,0:T(8,128)(2,1)}), bf16[16,32,128]{2,1,0:T(8,128)(2,1)S(1)}, u32[]{:S(2)}, u32[]{:S(2)}) async-start(bf16[16,32,128]{2,1,0:T(8,128)(2,1)} %get-tuple-element.74), calls=%async_computation.1 | async-start | bytes 262144 | tf_op jit(solution)/shard_map/all_to_all | solution.py:37
  22.2 5.4 %all-to-all-done.1.refs_5_ = bf16[16,32,128]{2,1,0:T(8,128)(2,1)S(1)} async-done(((bf16[16,32,128]{2,1,0:T(8,128)(2,1)}), bf16[16,32,128]{2,1,0:T(8,128)(2,1)S(1)}, u32[]{:S(2)}, u32[]{:S(2)}) %all-to-all-start.1) | async-done | bytes 131104 | tf_op jit(solution)/shard_map/all_to_all | solution.py:37
  27.7 1.5 collective-permute-start.6
  29.8 1.1 collective-permute-done.5.refs_1_
  30.9 1.9 %shard_map.76 = (s32[3,4,4,15]{3,2,1,0:T(4,128)S(4)}, f32[6,2,32,128]{3,2,1,0:T(8,128)S(1)}, bf16[6,2,128,128]{3,2,1,0:T(8,128)(2,1)S(1)}, bf16[9,2,4,128,128]{4,3,2,1,0:T(8,128)(2,1)S(1)}) custom-call(s32[1,4,4,15]{3,2,1,0:T(4,128)S(1)} %bitcast.13, s32[2,4,4,15]{3,2,1,0:T(4,128)S(1)} %collective-permute-done.5.refs_1_, ...), custom_call_target="tpu_custom_call" | custom-call | bytes 4000000 | tf_op jit(solution)/shard_map/pallas_call | solution.py:356
  33.2 12.0 %all_to_all.50.refs_7_ = bf16[64,16,128]{2,1,0:T(8,128)(2,1)S(1)} all-to-all(bf16[64,16,128]{2,1,0:T(8,128)(2,1)S(1)} %get-tuple-element.91), channel_id=1, replica_groups={{0,2,4,6,8,10,12,14,16,18,20,22,24,26,28,30},{1,3,5,7,9,11,13,15,17,19,..., dimensions={0} | all-to-all | bytes 524288 | tf_op jit(solution)/shard_map/all_to_all | solution.py:37
  45.7 14.5 %all_to_all.51.refs_8_ = bf16[128,16,128]{2,1,0:T(8,128)(2,1)S(1)} all-to-all(bf16[128,16,128]{2,1,0:T(8,128)(2,1)S(1)} %get-tuple-element.92), channel_id=1, replica_groups={{0,2,4,6,8,10,12,14,16,18,20,22,24,26,28,30,32,34,36,38,40,42,44,46,48,..., dimensions={0} | all-to-all | bytes 1048576 | tf_op jit(solution)/shard_map/all_to_all | solution.py:37
  60.1 0.5 shard_map.79
  60.7 14.1 %all_to_all.52.near.refs_3_ = bf16[128,16,128]{2,1,0:T(8,128)(2,1)S(1)} all-to-all(bf16[128,16,128]{2,1,0:T(8,128)(2,1)S(1)} %get-tuple-element.93), channel_id=1, replica_groups={{0,2,4,6,8,10,12,14,16,18,20,22,24,26,28,30,32,34,36,38,40,42,44,46,48,..., dimensions={0} | all-to-all | bytes 1048576 | tf_op jit(solution)/shard_map/all_to_all | solution.py:37
  74.8 2.7 %collective-permute-start.9 = (bf16[16,16,128]{2,1,0:T(8,128)(2,1)S(1)}, bf16[16,16,128]{2,1,0:T(8,128)(2,1)S(1)}, u32[]{:S(2)}, u32[]{:S(2)}) collective-permute-start(bf16[16,16,128]{2,1,0:T(8,128)(2,1)S(1)} %shard_map.80), channel_id=1, source_target_pairs={{0,64},{32,96},{64,0},{96,32},{128,192},{160,224},{192,128},{224,1... | collective-permute-start | bytes 196616 | tf_op jit(solution)/shard_map/ppermute | solution.py:31
  77.5 3.4 %shard_map.81 = (bf16[15,2,4,128,128]{4,3,2,1,0:T(8,128)(2,1)S(1)}, bf16[15,2,4,128,128]{4,3,2,1,0:T(8,128)(2,1)S(1)}, bf16[6,2,128,128]{3,2,1,0:T(8,128)(2,1)S(1)}, bf16[6,2,128,128]{3,2,1,0:T(8,128)(2,1)S(1)}) custom-call(bf16[15,2,4,128,128]{4,3,2,1,0:T(8,128)(2,1)} %refs_0_.1, bf16[15,2,4,128,128]{4,3,2,1,0:T(8,128)(2,1)} %collective-permute-done.2.refs_4_.refs_1_, ...), custom_call_target="tpu_custom_call" | custom-call | bytes 4000000 | tf_op jit(solution)/shard_map/pallas_call | solution.py:356
  81.8 13.1 %all_to_all.53.near.refs_3_.refs_4_ = bf16[128,16,128]{2,1,0:T(8,128)(2,1)S(1)} all-to-all(bf16[128,16,128]{2,1,0:T(8,128)(2,1)S(1)} %get-tuple-element.103), channel_id=1, replica_groups={{0,2,4,6,8,10,12,14,16,18,20,22,24,26,28,30,32,34,36,38,40,42,44,46,48,..., dimensions={0} | all-to-all | bytes 1048576 | tf_op jit(solution)/shard_map/all_to_all | solution.py:37
  95.0 0.9 collective-permute-start.10
  95.9 3.3 %shard_map.85 = (bf16[15,2,4,128,128]{4,3,2,1,0:T(8,128)(2,1)S(1)}, bf16[15,2,4,128,128]{4,3,2,1,0:T(8,128)(2,1)S(1)}) custom-call(bf16[15,2,4,128,128]{4,3,2,1,0:T(8,128)(2,1)} %refs_0_.2, bf16[15,2,4,128,128]{4,3,2,1,0:T(8,128)(2,1)} %collective-permute-done.11.refs_1_), custom_call_target="tpu_custom_call" | custom-call | bytes 4000000 | tf_op jit(solution)/shard_map/pallas_call | solution.py:356
  99.2 0.6 collective-permute-done.10.refs_4_
  100.1 13.0 %all_to_all.54.refs_4_.refs_5_ = bf16[128,16,128]{2,1,0:T(8,128)(2,1)S(1)} all-to-all(bf16[128,16,128]{2,1,0:T(8,128)(2,1)S(1)} %get-tuple-element.113), channel_id=1, replica_groups={{0,2,4,6,8,10,12,14,16,18,20,22,24,26,28,30,32,34,36,38,40,42,44,46,48,..., dimensions={0} | all-to-all | bytes 1048576 | tf_op jit(solution)/shard_map/all_to_all | solution.py:37
  113.4 10.6 %all_to_all.55.refs_5_.refs_6_ = bf16[64,16,128]{2,1,0:T(8,128)(2,1)S(1)} all-to-all(bf16[64,16,128]{2,1,0:T(8,128)(2,1)S(1)} %get-tuple-element.116), channel_id=1, replica_groups={{0,2,4,6,8,10,12,14,16,18,20,22,24,26,28,30},{1,3,5,7,9,11,13,15,17,19,..., dimensions={0} | all-to-all | bytes 524288 | tf_op jit(solution)/shard_map/all_to_all | solution.py:37
  124.5 7.8 %all_to_all.56.refs_7_ = bf16[32,16,128]{2,1,0:T(8,128)(2,1)S(1)} all-to-all(bf16[32,16,128]{2,1,0:T(8,128)(2,1)S(1)} %get-tuple-element.118), channel_id=1, replica_groups={{0,2,4,6,8,10,12,14},{1,3,5,7,9,11,13,15},{16,18,20,22,24,26,28,30},{17..., dimensions={0} | all-to-all | bytes 262144 | tf_op jit(solution)/shard_map/all_to_all | solution.py:37
  132.3 0.5 shard_map.89
  132.8 6.9 %all_to_all.57.refs_8_ = bf16[16,16,128]{2,1,0:T(8,128)(2,1)S(1)} all-to-all(bf16[16,16,128]{2,1,0:T(8,128)(2,1)S(1)} %get-tuple-element.120), channel_id=1, replica_groups={{0,2,4,6},{1,3,5,7},{8,10,12,14},{9,11,13,15},{16,18,20,22},{17,19,21,2..., dimensions={0} | all-to-all | bytes 131072 | tf_op jit(solution)/shard_map/all_to_all | solution.py:37
  139.8 0.6 shard_map.90.refs_5_
  140.4 10.6 %collective-permute-start.12 = (f32[6,2,16,128]{3,2,1,0:T(8,128)S(1)}, f32[6,2,16,128]{3,2,1,0:T(8,128)S(1)}, u32[]{:S(2)}, u32[]{:S(2)}) collective-permute-start(f32[6,2,16,128]{3,2,1,0:T(8,128)S(1)} %shard_map.91), channel_id=1, source_target_pairs={{0,1},{1,0},{2,3},{3,2},{4,5},{5,4},{6,7},{7,6},{8,9},{9,8},{10,11... | collective-permute-start | bytes 294920 | tf_op jit(solution)/shard_map/ppermute | solution.py:31
  151.0 0.9 collective-permute-done.12.sent
  151.9 0.9 shard_map.92
  (28 shorter events, 4.2 us)
Async XLA Ops:
  1.7 26.0 %collective-permute-start.2 = (bf16[15,2,4,128,128]{4,3,2,1,0:T(8,128)(2,1)}, bf16[15,2,4,128,128]{4,3,2,1,0:T(8,128)(2,1)}, u32[]{:S(2)}, u32[]{:S(2)}) collective-permute-start(bf16[15,2,4,128,128]{4,3,2,1,0:T(8,128)(2,1)} %refs_0_.1), channel_id=1, source_target_pairs={{0,1},{1,0},{2,3},{3,2},{4,5},{5,4},{6,7},{7,6},{8,9},{9,8},{10,11... | collective-permute-start | bytes 11796488 | tf_op jit(solution)/shard_map/ppermute | solution.py:31
  5.0 22.6 %collective-permute-start.3 = (bf16[6,2,128,128]{3,2,1,0:T(8,128)(2,1)}, bf16[6,2,128,128]{3,2,1,0:T(8,128)(2,1)}, u32[]{:S(2)}, u32[]{:S(2)}) collective-permute-start(bf16[6,2,128,128]{3,2,1,0:T(8,128)(2,1)} %refs_1_.1), channel_id=1, source_target_pairs={{0,1},{1,0},{2,3},{3,2},{4,5},{5,4},{6,7},{7,6},{8,9},{9,8},{10,11... | collective-permute-start | bytes 1179656 | tf_op jit(solution)/shard_map/ppermute | solution.py:31
  5.1 22.5 %collective-permute-start.4 = (bf16[6,2,128,128]{3,2,1,0:T(8,128)(2,1)}, bf16[6,2,128,128]{3,2,1,0:T(8,128)(2,1)}, u32[]{:S(2)}, u32[]{:S(2)}) collective-permute-start(bf16[6,2,128,128]{3,2,1,0:T(8,128)(2,1)} %refs_2_.3), channel_id=1, source_target_pairs={{0,1},{1,0},{2,3},{3,2},{4,5},{5,4},{6,7},{7,6},{8,9},{9,8},{10,11... | collective-permute-start | bytes 1179656 | tf_op jit(solution)/shard_map/ppermute | solution.py:31
  5.5 90.3 %collective-permute-start.11 = (bf16[15,2,4,128,128]{4,3,2,1,0:T(8,128)(2,1)}, bf16[15,2,4,128,128]{4,3,2,1,0:T(8,128)(2,1)}, u32[]{:S(2)}, u32[]{:S(2)}) collective-permute-start(bf16[15,2,4,128,128]{4,3,2,1,0:T(8,128)(2,1)} %refs_0_.2), channel_id=1, source_target_pairs={{0,1},{1,0},{2,3},{3,2},{4,5},{5,4},{6,7},{7,6},{8,9},{9,8},{10,11... | collective-permute-start | bytes 11796488 | tf_op jit(solution)/shard_map/ppermute | solution.py:31
  5.6 10.6 %all-to-all-start = ((bf16[16,32,128]{2,1,0:T(8,128)(2,1)}), bf16[16,32,128]{2,1,0:T(8,128)(2,1)S(1)}, u32[]{:S(2)}, u32[]{:S(2)}) async-start(bf16[16,32,128]{2,1,0:T(8,128)(2,1)} %get-tuple-element.63), calls=%async_computation | async-start | bytes 262144 | tf_op jit(solution)/shard_map/all_to_all | solution.py:37
  9.3 3.5 %collective-permute-start = (s32[4,4,15]{2,1,0:T(4,128)S(1)}, s32[4,4,15]{2,1,0:T(4,128)S(1)}, u32[]{:S(2)}, u32[]{:S(2)}) collective-permute-start(s32[4,4,15]{2,1,0:T(4,128)S(1)} %get-tuple-element.64), channel_id=1, source_target_pairs={{0,64},{32,96},{64,0},{96,32},{128,192},{160,224},{192,128},{224,1... | collective-permute-start | bytes 2888 | tf_op jit(solution)/shard_map/ppermute | solution.py:31
  12.8 9.4 %collective-permute-start.1 = (f32[6,2,32,128]{3,2,1,0:T(8,128)}, f32[6,2,32,128]{3,2,1,0:T(8,128)}, u32[]{:S(2)}, u32[]{:S(2)}) collective-permute-start(f32[6,2,32,128]{3,2,1,0:T(8,128)} %refs_0_), channel_id=1, source_target_pairs={{0,1},{1,0},{2,3},{3,2},{4,5},{5,4},{6,7},{7,6},{8,9},{9,8},{10,11... | collective-permute-start | bytes 589832 | tf_op jit(solution)/shard_map/ppermute | solution.py:31
  17.2 10.5 %all-to-all-start.1 = ((bf16[16,32,128]{2,1,0:T(8,128)(2,1)}), bf16[16,32,128]{2,1,0:T(8,128)(2,1)S(1)}, u32[]{:S(2)}, u32[]{:S(2)}) async-start(bf16[16,32,128]{2,1,0:T(8,128)(2,1)} %get-tuple-element.74), calls=%async_computation.1 | async-start | bytes 262144 | tf_op jit(solution)/shard_map/all_to_all | solution.py:37
  27.7 5.2 %collective-permute-start.6 = (bf16[16,32,128]{2,1,0:T(8,128)(2,1)S(1)}, bf16[16,32,128]{2,1,0:T(8,128)(2,1)S(1)}, u32[]{:S(2)}, u32[]{:S(2)}) collective-permute-start(bf16[16,32,128]{2,1,0:T(8,128)(2,1)S(1)} %all-to-all-done.1.refs_5_), channel_id=1, source_target_pairs={{0,1},{1,0},{2,3},{3,2},{4,5},{5,4},{6,7},{7,6},{8,9},{9,8},{10,11... | collective-permute-start | bytes 393224 | tf_op jit(solution)/shard_map/ppermute | solution.py:31
  29.2 3.6 %collective-permute-start.7 = (f32[2,32,128]{2,1,0:T(8,128)S(1)}, f32[2,32,128]{2,1,0:T(8,128)S(1)}, u32[]{:S(2)}, u32[]{:S(2)}) collective-permute-start(f32[2,32,128]{2,1,0:T(8,128)S(1)} %get-tuple-element.86.refs_2_), channel_id=1, source_target_pairs={{0,1},{1,0},{2,3},{3,2},{4,5},{5,4},{6,7},{7,6},{8,9},{9,8},{10,11... | collective-permute-start | bytes 98312 | tf_op jit(solution)/shard_map/ppermute | solution.py:31
  29.3 3.5 %collective-permute-start.8 = (f32[2,32,128]{2,1,0:T(8,128)S(1)}, f32[2,32,128]{2,1,0:T(8,128)S(1)}, u32[]{:S(2)}, u32[]{:S(2)}) collective-permute-start(f32[2,32,128]{2,1,0:T(8,128)S(1)} %get-tuple-element.88.refs_2_), channel_id=1, source_target_pairs={{0,1},{1,0},{2,3},{3,2},{4,5},{5,4},{6,7},{7,6},{8,9},{9,8},{10,11... | collective-permute-start | bytes 98312 | tf_op jit(solution)/shard_map/ppermute | solution.py:31
  29.7 1.2 collective-permute-start.5
  74.8 6.6 %collective-permute-start.9 = (bf16[16,16,128]{2,1,0:T(8,128)(2,1)S(1)}, bf16[16,16,128]{2,1,0:T(8,128)(2,1)S(1)}, u32[]{:S(2)}, u32[]{:S(2)}) collective-permute-start(bf16[16,16,128]{2,1,0:T(8,128)(2,1)S(1)} %shard_map.80), channel_id=1, source_target_pairs={{0,64},{32,96},{64,0},{96,32},{128,192},{160,224},{192,128},{224,1... | collective-permute-start | bytes 196616 | tf_op jit(solution)/shard_map/ppermute | solution.py:31
  95.0 4.8 %collective-permute-start.10 = (bf16[16,16,128]{2,1,0:T(8,128)(2,1)S(1)}, bf16[16,16,128]{2,1,0:T(8,128)(2,1)S(1)}, u32[]{:S(2)}, u32[]{:S(2)}) collective-permute-start(bf16[16,16,128]{2,1,0:T(8,128)(2,1)S(1)} %shard_map.84), channel_id=1, source_target_pairs={{0,64},{32,96},{64,0},{96,32},{128,192},{160,224},{192,128},{224,1... | collective-permute-start | bytes 196616 | tf_op jit(solution)/shard_map/ppermute | solution.py:31
  140.4 11.5 %collective-permute-start.12 = (f32[6,2,16,128]{3,2,1,0:T(8,128)S(1)}, f32[6,2,16,128]{3,2,1,0:T(8,128)S(1)}, u32[]{:S(2)}, u32[]{:S(2)}) collective-permute-start(f32[6,2,16,128]{3,2,1,0:T(8,128)S(1)} %shard_map.91), channel_id=1, source_target_pairs={{0,1},{1,0},{2,3},{3,2},{4,5},{5,4},{6,7},{7,6},{8,9},{9,8},{10,11... | collective-permute-start | bytes 294920 | tf_op jit(solution)/shard_map/ppermute | solution.py:31

commit v7 on v6

--- a/solution.py
+++ b/solution.py
@@ -59,7 +59,7 @@
 
 
 (CORE, DUO, PLANE64, SIXTEEN64, EIGHT64, SIXTEEN32, EIGHT32, EIGHT16, NONE) = range(9)
-ACROSS, MATE, MATE_ACROSS = range(3)
+ACROSS, MATE_ACROSS, MATE = range(3)
 
 
 def positions(sub, group):
@@ -110,6 +110,7 @@
 
 
 FIRST = (13, 9, 12, 8, 5, 11, 7, 4, 2)
+LAST = (10, 6, 3, 1, 0)
 BUFFERS = {"one": 1, "halves": 2, "cols": 1, "far": 2}
 
 
@@ -398,8 +399,9 @@
 
     tables = [x.transpose(1, 2, 0) for x in (lower_pattern, upper_pattern)]
     f5, sent, mine = first_update(right_sides, lower_inv, *tables, 8)
-    across = swapped(mine, "group", 2)
-    lower_all, inverse_all = after(lower_off, sent), lower_inv
+    mate = jnp.concatenate([swapped(x, "sub", 1) for x in tables])
+    across = swapped(jnp.stack([mine, mate]), "group", 2)
+    lower_all, inverse_all = lower_off, lower_inv
     right, lower_inv, off14, off_first, table, me = staged(
         (pltpu.VMEM, [after(right_sides, sent)], None),
         (pltpu.VMEM, [lower_inv], None),
@@ -412,14 +414,14 @@
     f4, sent = update(
         me, table, off14, right, 4, [("one", 14, NONE)], [(near5,)], 0, 4, [lower_inv], 8, (14,)
     )
-    theirs = [swapped(x, "sub", 1) for x in (right_sides, lower_all, inverse_all, upper_inv)]
-    near4, *theirs = lax.optimization_barrier((spread(sent, square), *theirs))
+    theirs = [right_sides, lower_all, inverse_all, upper_inv]
+    theirs = [swapped(after(x, across), "sub", 1) for x in theirs]
+    (peers,) = staged((pltpu.SMEM, [across, mate[None]], None))
+    near4, peers, *theirs = lax.optimization_barrier((spread(sent, square), peers, *theirs))
     near4 = (near4, swapped(near4, "sub", 1))
-    mates = swapped(after(jnp.stack([mine, across]), near4[0]), "sub", 1)
     f4_mate = swapped(after(f4, near4[0]), "sub", 1)
     f5_mate = swapped(after(f5, near4[0]), "sub", 1)
-    peers, right_mate, inv_mate, off_mate = staged(
-        (pltpu.SMEM, [across[None], mates], None),
+    right_mate, inv_mate, off_mate = staged(
         (pltpu.VMEM, [theirs[0]], None),
         (pltpu.VMEM, [theirs[2]], None),
         (pltpu.VMEM, [theirs[1]], FIRST),
@@ -455,12 +457,12 @@
     sent = pick(me, peers, 0, near1)
     far = swapped(sent, "group", 2)
     lower_off, low_mate, upper_inv, up_inv_mate = staged(
-        (pltpu.VMEM, [after(lower_off, sent)], None),
-        (pltpu.VMEM, [theirs[1]], None),
+        (pltpu.VMEM, [after(lower_off, sent)], LAST),
+        (pltpu.VMEM, [theirs[1]], LAST),
         (pltpu.VMEM, [upper_inv], None),
         (pltpu.VMEM, [theirs[3]], None),
     )
-    low = functools.partial(solve, me, table, peers, (lower_off, low_mate), side=0)
+    low = functools.partial(solve, me, table, peers, (lower_off, low_mate), side=0, kept=LAST)
     (r0,) = low(
         right,
         0,

time: 153 us -> 153 us (level)
    ppermute x13 -> x14, waiting for transfers between devices: 3.66 us -> 2.91 us  [swapped(): lax.ppermute(block, axis, [(i, i ^ mask) for i in range(lax.axis_size(axi...]
    pallas_call x4 -> x5, Pallas kernels: 10.7 us -> 10.2 us  [staged(): pl.pallas_call(functools.partial(stage_kernel, tuple(plan), len(arrays)),...]
    ppermute x13 -> x14, starting transfers between devices: 24 us -> 24.2 us  [swapped(): lax.ppermute(block, axis, [(i, i ^ mask) for i in range(lax.axis_size(axi...]
  transfers between devices with their start and end apart: 15 -> 16, of which waited for: 5 -> 4; matrix products, arithmetic and copies ran while one was open for 0% -> 0% of each run, Pallas kernels for 9% -> 10%
where the time goes in v7:
time: 153 us; the launch traced here: 152 us
  blocking collectives  93.3 us (61%)
  starting transfers between devices  32.5 us (21%)
  Pallas kernels  18.2 us (12%)
  waiting for transfers between devices  8.01 us (5%)
    all_to_all x8, blocking collectives, spread(): lax.all_to_all(copies, axes, 0, 0, tiled=True, axis_index_groups=groups)  93.3 us
    ppermute x14, starting transfers between devices, swapped(): lax.ppermute(block, axis, [(i, i ^ mask) for i in range(lax.axis_size(axi...  24.2 us
    pallas_call x5, Pallas kernels, staged(): pl.pallas_call(functools.partial(stage_kernel, tuple(plan), len(arrays)),...  10.2 us
    all_to_all x2, starting transfers between devices, spread(): lax.all_to_all(copies, axes, 0, 0, tiled=True, axis_index_groups=groups)  8.2 us
    all_to_all x2, waiting for transfers between devices, spread(): lax.all_to_all(copies, axes, 0, 0, tiled=True, axis_index_groups=groups)  5.1 us
    pallas_call x10, Pallas kernels, solve(): pl.pallas_call(functools.partial(solve_kernel, tuple(plan), side, kept, f...  4.43 us
  transfers between devices with their start and end apart: 16, of which 4 were waited for; matrix products, arithmetic and copies ran while one was open for 0% of the time, Pallas kernels for 10%

profile of v7, /device:TPU:1, one launch (start us, length us, event | category | flops | bytes accessed | tf_op | source)
XLA Modules:
  0.0 152.3 jit_solution(6830245124982569243)
XLA Ops:
  0.0 3.2 %collective-permute-start = (s32[2,4,15]{2,1,0:T(4,128)}, s32[2,4,15]{2,1,0:T(4,128)S(1)}, u32[]{:S(2)}, u32[]{:S(2)}) collective-permute-start(s32[2,4,15]{2,1,0:T(4,128)} %bitcast.14), channel_id=1, source_target_pairs={{0,1},{1,0},{2,3},{3,2},{4,5},{5,4},{6,7},{7,6},{8,9},{9,8},{10,11... | collective-permute-start | bytes 1448 | tf_op jit(solution)/shard_map/ppermute | solution.py:31
  3.2 1.7 %shard_map.73 = (f32[2,32,128]{2,1,0:T(8,128)S(1)}, bf16[16,32,128]{2,1,0:T(8,128)(2,1)}, s32[4,4,15]{2,1,0:T(4,128)S(1)}) custom-call(f32[6,2,32,128]{3,2,1,0:T(8,128)} %refs_0_, bf16[6,2,128,128]{3,2,1,0:T(8,128)(2,1)} %refs_1_.1, s32[2,4,15]{2,1,0:T(4,128)} %bitcast.15, s32[2,4,15]{2,1,0:T(4,128)} %bitcast.18), custom_call_target="tpu_custom_call" | custom-call | tf_op jit(solution)/shard_map/pallas_call | solution.py:264
  4.9 3.8 %all-to-all-start = ((bf16[16,32,128]{2,1,0:T(8,128)(2,1)}), bf16[16,32,128]{2,1,0:T(8,128)(2,1)S(1)}, u32[]{:S(2)}, u32[]{:S(2)}) async-start(bf16[16,32,128]{2,1,0:T(8,128)(2,1)} %get-tuple-element.65), calls=%async_computation | async-start | bytes 262144 | tf_op jit(solution)/shard_map/all_to_all | solution.py:37
  8.8 2.5 %collective-permute-start.2 = (s32[2,4,4,15]{3,2,1,0:T(4,128)S(1)}, s32[2,4,4,15]{3,2,1,0:T(4,128)S(1)}, u32[]{:S(2)}, u32[]{:S(2)}) collective-permute-start(s32[2,4,4,15]{3,2,1,0:T(4,128)S(1)} %pad_add_fusion), channel_id=1, source_target_pairs={{0,64},{32,96},{64,0},{96,32},{128,192},{160,224},{192,128},{224,1... | collective-permute-start | bytes 5768 | tf_op jit(solution)/shard_map/ppermute | solution.py:31
  11.4 2.0 %shard_map.74 = (f32[6,2,32,128]{3,2,1,0:T(8,128)S(1)}, bf16[6,2,128,128]{3,2,1,0:T(8,128)(2,1)S(1)}, bf16[1,2,4,128,128]{4,3,2,1,0:T(8,128)(2,1)S(1)}, bf16[9,2...) custom-call(f32[6,2,32,128]{3,2,1,0:T(8,128)} %refs_0_, bf16[6,2,128,128]{3,2,1,0:T(8,128)(2,1)} %refs_1_.1, ...), custom_call_target="tpu_custom_call" | custom-call | bytes 4000000 | tf_op jit(solution)/shard_map/pallas_call | solution.py:357
  13.5 0.6 all-to-all-done.refs_0_.refs_4_
  14.0 0.9 collective-permute-start.4
  14.9 0.5 collective-permute-start.6
  15.9 0.9 shard_map.75
  16.9 4.4 %all-to-all-start.1 = ((bf16[16,32,128]{2,1,0:T(8,128)(2,1)}), bf16[16,32,128]{2,1,0:T(8,128)(2,1)S(1)}, u32[]{:S(2)}, u32[]{:S(2)}) async-start(bf16[16,32,128]{2,1,0:T(8,128)(2,1)} %get-tuple-element.75), calls=%async_computation.1 | async-start | bytes 262144 | tf_op jit(solution)/shard_map/all_to_all | solution.py:37
  21.3 0.9 shard_map.76.peers
  22.2 4.5 %all-to-all-done.1.refs_5_ = bf16[16,32,128]{2,1,0:T(8,128)(2,1)S(1)} async-done(((bf16[16,32,128]{2,1,0:T(8,128)(2,1)}), bf16[16,32,128]{2,1,0:T(8,128)(2,1)S(1)}, u32[]{:S(2)}, u32[]{:S(2)}) %all-to-all-start.1) | async-done | bytes 131104 | tf_op jit(solution)/shard_map/all_to_all | solution.py:37
  26.7 1.9 %collective-permute-done.3.refs_0_ = f32[6,2,32,128]{3,2,1,0:T(8,128)} collective-permute-done((f32[6,2,32,128]{3,2,1,0:T(8,128)}, f32[6,2,32,128]{3,2,1,0:T(8,128)}, u32[]{:S(2)}, u32[]{:S(2)}) %collective-permute-start.3) | collective-permute-done | bytes 196640 | tf_op jit(solution)/shard_map/ppermute | solution.py:31
  29.7 1.9 %shard_map.77 = (f32[6,2,32,128]{3,2,1,0:T(8,128)S(1)}, bf16[6,2,128,128]{3,2,1,0:T(8,128)(2,1)S(1)}, bf16[9,2,4,128,128]{4,3,2,1,0:T(8,128)(2,1)S(1)}) custom-call(f32[6,2,32,128]{3,2,1,0:T(8,128)} %collective-permute-done.3.refs_0_, bf16[6,2,128,128]{3,2,1,0:T(8,128)(2,1)} %collective-permute-done.5.refs_1_, ...), custom_call_target="tpu_custom_call" | custom-call | bytes 4000000 | tf_op jit(solution)/shard_map/pallas_call | solution.py:357
  32.0 13.6 %all_to_all.50.refs_7_ = bf16[64,16,128]{2,1,0:T(8,128)(2,1)S(1)} all-to-all(bf16[64,16,128]{2,1,0:T(8,128)(2,1)S(1)} %get-tuple-element.95), channel_id=1, replica_groups={{0,2,4,6,8,10,12,14,16,18,20,22,24,26,28,30},{1,3,5,7,9,11,13,15,17,19,..., dimensions={0} | all-to-all | bytes 524288 | tf_op jit(solution)/shard_map/all_to_all | solution.py:37
  46.1 14.5 %all_to_all.51.refs_8_ = bf16[128,16,128]{2,1,0:T(8,128)(2,1)S(1)} all-to-all(bf16[128,16,128]{2,1,0:T(8,128)(2,1)S(1)} %get-tuple-element.96), channel_id=1, replica_groups={{0,2,4,6,8,10,12,14,16,18,20,22,24,26,28,30,32,34,36,38,40,42,44,46,48,..., dimensions={0} | all-to-all | bytes 1048576 | tf_op jit(solution)/shard_map/all_to_all | solution.py:37
  60.5 0.5 shard_map.80
  61.1 14.1 %all_to_all.52.near.refs_3_ = bf16[128,16,128]{2,1,0:T(8,128)(2,1)S(1)} all-to-all(bf16[128,16,128]{2,1,0:T(8,128)(2,1)S(1)} %get-tuple-element.97), channel_id=1, replica_groups={{0,2,4,6,8,10,12,14,16,18,20,22,24,26,28,30,32,34,36,38,40,42,44,46,48,..., dimensions={0} | all-to-all | bytes 1048576 | tf_op jit(solution)/shard_map/all_to_all | solution.py:37
  75.2 2.2 %collective-permute-start.10 = (bf16[16,16,128]{2,1,0:T(8,128)(2,1)S(1)}, bf16[16,16,128]{2,1,0:T(8,128)(2,1)S(1)}, u32[]{:S(2)}, u32[]{:S(2)}) collective-permute-start(bf16[16,16,128]{2,1,0:T(8,128)(2,1)S(1)} %shard_map.81), channel_id=1, source_target_pairs={{0,64},{32,96},{64,0},{96,32},{128,192},{160,224},{192,128},{224,1... | collective-permute-start | bytes 196616 | tf_op jit(solution)/shard_map/ppermute | solution.py:31
  77.4 2.0 %shard_map.82 = (bf16[5,2,4,128,128]{4,3,2,1,0:T(8,128)(2,1)S(1)}, bf16[5,2,4,128,128]{4,3,2,1,0:T(8,128)(2,1)S(1)}, bf16[6,2,128,128]{3,2,1,0:T(8,128)(2,1)S(1)}, bf16[6,2,128,128]{3,2,1,0:T(8,128)(2,1)S(1)}) custom-call(bf16[15,2,4,128,128]{4,3,2,1,0:T(8,128)(2,1)} %refs_0_.1, bf16[15,2,4,128,128]{4,3,2,1,0:T(8,128)(2,1)} %collective-permute-done.4.refs_2_.refs_1_, ...), custom_call_target="tpu_custom_call" | custom-call | bytes 4000000 | tf_op jit(solution)/shard_map/pallas_call | solution.py:357
  80.3 13.2 %all_to_all.53.near.refs_3_.refs_4_ = bf16[128,16,128]{2,1,0:T(8,128)(2,1)S(1)} all-to-all(bf16[128,16,128]{2,1,0:T(8,128)(2,1)S(1)} %get-tuple-element.107), channel_id=1, replica_groups={{0,2,4,6,8,10,12,14,16,18,20,22,24,26,28,30,32,34,36,38,40,42,44,46,48,..., dimensions={0} | all-to-all | bytes 1048576 | tf_op jit(solution)/shard_map/all_to_all | solution.py:37
  93.5 2.2 %collective-permute-start.11 = (bf16[16,16,128]{2,1,0:T(8,128)(2,1)S(1)}, bf16[16,16,128]{2,1,0:T(8,128)(2,1)S(1)}, u32[]{:S(2)}, u32[]{:S(2)}) collective-permute-start(bf16[16,16,128]{2,1,0:T(8,128)(2,1)S(1)} %shard_map.85), channel_id=1, source_target_pairs={{0,64},{32,96},{64,0},{96,32},{128,192},{160,224},{192,128},{224,1... | collective-permute-start | bytes 196616 | tf_op jit(solution)/shard_map/ppermute | solution.py:31
  95.7 3.3 %shard_map.86 = (bf16[15,2,4,128,128]{4,3,2,1,0:T(8,128)(2,1)S(1)}, bf16[15,2,4,128,128]{4,3,2,1,0:T(8,128)(2,1)S(1)}) custom-call(bf16[15,2,4,128,128]{4,3,2,1,0:T(8,128)(2,1)} %refs_0_.2, bf16[15,2,4,128,128]{4,3,2,1,0:T(8,128)(2,1)} %collective-permute-done.12.refs_1_), custom_call_target="tpu_custom_call" | custom-call | bytes 4000000 | tf_op jit(solution)/shard_map/pallas_call | solution.py:357
  99.4 12.7 %all_to_all.54.refs_4_.refs_5_ = bf16[128,16,128]{2,1,0:T(8,128)(2,1)S(1)} all-to-all(bf16[128,16,128]{2,1,0:T(8,128)(2,1)S(1)} %get-tuple-element.117), channel_id=1, replica_groups={{0,2,4,6,8,10,12,14,16,18,20,22,24,26,28,30,32,34,36,38,40,42,44,46,48,..., dimensions={0} | all-to-all | bytes 1048576 | tf_op jit(solution)/shard_map/all_to_all | solution.py:37
  112.4 10.6 %all_to_all.55.refs_5_.refs_6_ = bf16[64,16,128]{2,1,0:T(8,128)(2,1)S(1)} all-to-all(bf16[64,16,128]{2,1,0:T(8,128)(2,1)S(1)} %get-tuple-element.120), channel_id=1, replica_groups={{0,2,4,6,8,10,12,14,16,18,20,22,24,26,28,30},{1,3,5,7,9,11,13,15,17,19,..., dimensions={0} | all-to-all | bytes 524288 | tf_op jit(solution)/shard_map/all_to_all | solution.py:37
  123.5 7.8 %all_to_all.56.refs_7_ = bf16[32,16,128]{2,1,0:T(8,128)(2,1)S(1)} all-to-all(bf16[32,16,128]{2,1,0:T(8,128)(2,1)S(1)} %get-tuple-element.122), channel_id=1, replica_groups={{0,2,4,6,8,10,12,14},{1,3,5,7,9,11,13,15},{16,18,20,22,24,26,28,30},{17..., dimensions={0} | all-to-all | bytes 262144 | tf_op jit(solution)/shard_map/all_to_all | solution.py:37
  131.3 0.5 shard_map.90
  131.8 6.8 %all_to_all.57.refs_8_ = bf16[16,16,128]{2,1,0:T(8,128)(2,1)S(1)} all-to-all(bf16[16,16,128]{2,1,0:T(8,128)(2,1)S(1)} %get-tuple-element.124), channel_id=1, replica_groups={{0,2,4,6},{1,3,5,7},{8,10,12,14},{9,11,13,15},{16,18,20,22},{17,19,21,2..., dimensions={0} | all-to-all | bytes 131072 | tf_op jit(solution)/shard_map/all_to_all | solution.py:37
  138.7 0.6 shard_map.91.refs_5_
  139.3 11.2 %collective-permute-start.13 = (f32[6,2,16,128]{3,2,1,0:T(8,128)S(1)}, f32[6,2,16,128]{3,2,1,0:T(8,128)S(1)}, u32[]{:S(2)}, u32[]{:S(2)}) collective-permute-start(f32[6,2,16,128]{3,2,1,0:T(8,128)S(1)} %shard_map.92), channel_id=1, source_target_pairs={{0,1},{1,0},{2,3},{3,2},{4,5},{5,4},{6,7},{7,6},{8,9},{9,8},{10,11... | collective-permute-start | bytes 294920 | tf_op jit(solution)/shard_map/ppermute | solution.py:31
  150.5 0.9 collective-permute-done.13.sent
  151.4 0.9 shard_map.93
  (32 shorter events, 4.5 us)
Async XLA Ops:
  0.0 8.7 %collective-permute-start = (s32[2,4,15]{2,1,0:T(4,128)}, s32[2,4,15]{2,1,0:T(4,128)S(1)}, u32[]{:S(2)}, u32[]{:S(2)}) collective-permute-start(s32[2,4,15]{2,1,0:T(4,128)} %bitcast.14), channel_id=1, source_target_pairs={{0,1},{1,0},{2,3},{3,2},{4,5},{5,4},{6,7},{7,6},{8,9},{9,8},{10,11... | collective-permute-start | bytes 1448 | tf_op jit(solution)/shard_map/ppermute | solution.py:31
  3.2 5.5 %collective-permute-start.1 = (s32[2,4,15]{2,1,0:T(4,128)}, s32[2,4,15]{2,1,0:T(4,128)S(1)}, u32[]{:S(2)}, u32[]{:S(2)}) collective-permute-start(s32[2,4,15]{2,1,0:T(4,128)} %bitcast.17), channel_id=1, source_target_pairs={{0,1},{1,0},{2,3},{3,2},{4,5},{5,4},{6,7},{7,6},{8,9},{9,8},{10,11... | collective-permute-start | bytes 1448 | tf_op jit(solution)/shard_map/ppermute | solution.py:31
  4.9 9.1 %all-to-all-start = ((bf16[16,32,128]{2,1,0:T(8,128)(2,1)}), bf16[16,32,128]{2,1,0:T(8,128)(2,1)S(1)}, u32[]{:S(2)}, u32[]{:S(2)}) async-start(bf16[16,32,128]{2,1,0:T(8,128)(2,1)} %get-tuple-element.65), calls=%async_computation | async-start | bytes 262144 | tf_op jit(solution)/shard_map/all_to_all | solution.py:37
  8.8 4.7 %collective-permute-start.2 = (s32[2,4,4,15]{3,2,1,0:T(4,128)S(1)}, s32[2,4,4,15]{3,2,1,0:T(4,128)S(1)}, u32[]{:S(2)}, u32[]{:S(2)}) collective-permute-start(s32[2,4,4,15]{3,2,1,0:T(4,128)S(1)} %pad_add_fusion), channel_id=1, source_target_pairs={{0,64},{32,96},{64,0},{96,32},{128,192},{160,224},{192,128},{224,1... | collective-permute-start | bytes 5768 | tf_op jit(solution)/shard_map/ppermute | solution.py:31
  14.0 14.7 %collective-permute-start.4 = (bf16[15,2,4,128,128]{4,3,2,1,0:T(8,128)(2,1)}, bf16[15,2,4,128,128]{4,3,2,1,0:T(8,128)(2,1)}, u32[]{:S(2)}, u32[]{:S(2)}) collective-permute-start(bf16[15,2,4,128,128]{4,3,2,1,0:T(8,128)(2,1)} %refs_0_.1), channel_id=1, source_target_pairs={{0,1},{1,0},{2,3},{3,2},{4,5},{5,4},{6,7},{7,6},{8,9},{9,8},{10,11... | collective-permute-start | bytes 11796488 | tf_op jit(solution)/shard_map/ppermute | solution.py:31
  14.9 13.8 %collective-permute-start.5 = (bf16[6,2,128,128]{3,2,1,0:T(8,128)(2,1)}, bf16[6,2,128,128]{3,2,1,0:T(8,128)(2,1)}, u32[]{:S(2)}, u32[]{:S(2)}) collective-permute-start(bf16[6,2,128,128]{3,2,1,0:T(8,128)(2,1)} %refs_1_.1), channel_id=1, source_target_pairs={{0,1},{1,0},{2,3},{3,2},{4,5},{5,4},{6,7},{7,6},{8,9},{9,8},{10,11... | collective-permute-start | bytes 1179656 | tf_op jit(solution)/shard_map/ppermute | solution.py:31
  14.9 13.8 %collective-permute-start.6 = (bf16[6,2,128,128]{3,2,1,0:T(8,128)(2,1)}, bf16[6,2,128,128]{3,2,1,0:T(8,128)(2,1)}, u32[]{:S(2)}, u32[]{:S(2)}) collective-permute-start(bf16[6,2,128,128]{3,2,1,0:T(8,128)(2,1)} %refs_2_.3), channel_id=1, source_target_pairs={{0,1},{1,0},{2,3},{3,2},{4,5},{5,4},{6,7},{7,6},{8,9},{9,8},{10,11... | collective-permute-start | bytes 1179656 | tf_op jit(solution)/shard_map/ppermute | solution.py:31
  15.4 80.3 %collective-permute-start.12 = (bf16[15,2,4,128,128]{4,3,2,1,0:T(8,128)(2,1)}, bf16[15,2,4,128,128]{4,3,2,1,0:T(8,128)(2,1)}, u32[]{:S(2)}, u32[]{:S(2)}) collective-permute-start(bf16[15,2,4,128,128]{4,3,2,1,0:T(8,128)(2,1)} %refs_0_.2), channel_id=1, source_target_pairs={{0,1},{1,0},{2,3},{3,2},{4,5},{5,4},{6,7},{7,6},{8,9},{9,8},{10,11... | collective-permute-start | bytes 11796488 | tf_op jit(solution)/shard_map/ppermute | solution.py:31
  15.4 13.3 %collective-permute-start.3 = (f32[6,2,32,128]{3,2,1,0:T(8,128)}, f32[6,2,32,128]{3,2,1,0:T(8,128)}, u32[]{:S(2)}, u32[]{:S(2)}) collective-permute-start(f32[6,2,32,128]{3,2,1,0:T(8,128)} %refs_0_), channel_id=1, source_target_pairs={{0,1},{1,0},{2,3},{3,2},{4,5},{5,4},{6,7},{7,6},{8,9},{9,8},{10,11... | collective-permute-start | bytes 589832 | tf_op jit(solution)/shard_map/ppermute | solution.py:31
  16.9 9.9 %all-to-all-start.1 = ((bf16[16,32,128]{2,1,0:T(8,128)(2,1)}), bf16[16,32,128]{2,1,0:T(8,128)(2,1)S(1)}, u32[]{:S(2)}, u32[]{:S(2)}) async-start(bf16[16,32,128]{2,1,0:T(8,128)(2,1)} %get-tuple-element.75), calls=%async_computation.1 | async-start | bytes 262144 | tf_op jit(solution)/shard_map/all_to_all | solution.py:37
  28.7 2.9 %collective-permute-start.7 = (bf16[16,32,128]{2,1,0:T(8,128)(2,1)S(1)}, bf16[16,32,128]{2,1,0:T(8,128)(2,1)S(1)}, u32[]{:S(2)}, u32[]{:S(2)}) collective-permute-start(bf16[16,32,128]{2,1,0:T(8,128)(2,1)S(1)} %all-to-all-done.1.refs_5_), channel_id=1, source_target_pairs={{0,1},{1,0},{2,3},{3,2},{4,5},{5,4},{6,7},{7,6},{8,9},{9,8},{10,11... | collective-permute-start | bytes 393224 | tf_op jit(solution)/shard_map/ppermute | solution.py:31
  29.2 2.4 %collective-permute-start.8 = (f32[2,32,128]{2,1,0:T(8,128)S(1)}, f32[2,32,128]{2,1,0:T(8,128)S(1)}, u32[]{:S(2)}, u32[]{:S(2)}) collective-permute-start(f32[2,32,128]{2,1,0:T(8,128)S(1)} %get-tuple-element.90.refs_2_), channel_id=1, source_target_pairs={{0,1},{1,0},{2,3},{3,2},{4,5},{5,4},{6,7},{7,6},{8,9},{9,8},{10,11... | collective-permute-start | bytes 98312 | tf_op jit(solution)/shard_map/ppermute | solution.py:31
  29.3 2.3 %collective-permute-start.9 = (f32[2,32,128]{2,1,0:T(8,128)S(1)}, f32[2,32,128]{2,1,0:T(8,128)S(1)}, u32[]{:S(2)}, u32[]{:S(2)}) collective-permute-start(f32[2,32,128]{2,1,0:T(8,128)S(1)} %get-tuple-element.92.refs_2_), channel_id=1, source_target_pairs={{0,1},{1,0},{2,3},{3,2},{4,5},{5,4},{6,7},{7,6},{8,9},{9,8},{10,11... | collective-permute-start | bytes 98312 | tf_op jit(solution)/shard_map/ppermute | solution.py:31
  75.2 4.6 %collective-permute-start.10 = (bf16[16,16,128]{2,1,0:T(8,128)(2,1)S(1)}, bf16[16,16,128]{2,1,0:T(8,128)(2,1)S(1)}, u32[]{:S(2)}, u32[]{:S(2)}) collective-permute-start(bf16[16,16,128]{2,1,0:T(8,128)(2,1)S(1)} %shard_map.81), channel_id=1, source_target_pairs={{0,64},{32,96},{64,0},{96,32},{128,192},{160,224},{192,128},{224,1... | collective-permute-start | bytes 196616 | tf_op jit(solution)/shard_map/ppermute | solution.py:31
  93.5 5.6 %collective-permute-start.11 = (bf16[16,16,128]{2,1,0:T(8,128)(2,1)S(1)}, bf16[16,16,128]{2,1,0:T(8,128)(2,1)S(1)}, u32[]{:S(2)}, u32[]{:S(2)}) collective-permute-start(bf16[16,16,128]{2,1,0:T(8,128)(2,1)S(1)} %shard_map.85), channel_id=1, source_target_pairs={{0,64},{32,96},{64,0},{96,32},{128,192},{160,224},{192,128},{224,1... | collective-permute-start | bytes 196616 | tf_op jit(solution)/shard_map/ppermute | solution.py:31
  139.3 12.1 %collective-permute-start.13 = (f32[6,2,16,128]{3,2,1,0:T(8,128)S(1)}, f32[6,2,16,128]{3,2,1,0:T(8,128)S(1)}, u32[]{:S(2)}, u32[]{:S(2)}) collective-permute-start(f32[6,2,16,128]{3,2,1,0:T(8,128)S(1)} %shard_map.92), channel_id=1, source_target_pairs={{0,1},{1,0},{2,3},{3,2},{4,5},{5,4},{6,7},{7,6},{8,9},{9,8},{10,11... | collective-permute-start | bytes 294920 | tf_op jit(solution)/shard_map/ppermute | solution.py:31
